TPU v7x, 32 devices: a whole 2x2x4 slice. The times are simulated.
32 devices in a mesh: dp: 8 (over y, x, core), fsdp: 4 (over z).
Axes of the slice: x: 2, y: 2, z: 4, core: 2. Of those that a mesh axis runs over, the one named last changes fastest.
Arguments:
- tokens: bfloat16 [8192, 800], P(('dp', 'fsdp')), may hold values from -6 to 6
- cotangent: bfloat16 [8192, 800], P(('dp', 'fsdp')), may hold values from -6 to 6
- lengths: int32 [32, 8], P(('dp', 'fsdp')), may hold values from 1 to 192, 256 in all within a row
- dilation: int32 [2], replicated, may hold values from 1 to 8, as said below
- proj_in: float32 [2, 800, 400], P(None, 'fsdp'), may hold values from -0.21875 to 0.21875
- conv_weight: float32 [400, 3200], P('fsdp'), may hold values from -0.15625 to 0.15625
- proj_out: float32 [2, 400, 800], P(None, 'fsdp'), may hold values from -0.3125 to 0.3125
- vec_wide: float32 [2, 3, 800], P(None, None, 'fsdp'), may hold values from -1.2 to 1.6
- vec_narrow: float32 [2, 6, 400], P(None, None, 'fsdp'), may hold values from -1.2 to 1.6
- mom_in: float32 [2, 800, 400], P(None, 'fsdp'), may hold values from -160 to 160
- mom_conv: float32 [400, 3200], P('fsdp'), may hold values from -160 to 160
- mom_out: float32 [2, 400, 800], P(None, 'fsdp'), may hold values from -160 to 160
- mom_wide: float32 [2, 3, 800], P(None, None, 'fsdp'), may hold values from -160 to 160
- mom_narrow: float32 [2, 6, 400], P(None, None, 'fsdp'), may hold values from -160 to 160
Outputs:
- out_tokens: bfloat16 [8192, 800], P(('dp', 'fsdp'))
- grad_tokens: float32 [8192, 800], P(('dp', 'fsdp'))
- new_mom_in: float32 [2, 800, 400], P(None, 'fsdp')
- new_mom_conv: float32 [400, 3200], P('fsdp')
- new_mom_out: float32 [2, 400, 800], P(None, 'fsdp')
- new_mom_wide: float32 [2, 3, 800], P(None, None, 'fsdp')
- new_mom_narrow: float32 [2, 6, 400], P(None, None, 'fsdp')
- new_proj_in: float32 [2, 800, 400], P(None, 'fsdp')
- new_conv: float32 [400, 3200], P('fsdp')
- new_proj_out: float32 [2, 400, 800], P(None, 'fsdp')
- new_vec_wide: float32 [2, 3, 800], P(None, None, 'fsdp')
- new_vec_narrow: float32 [2, 6, 400], P(None, None, 'fsdp')
- low_proj_in: bfloat16 [2, 800, 400], P(None, 'fsdp')
- low_conv: bfloat16 [400, 3200], P('fsdp')
- low_proj_out: bfloat16 [2, 400, 800], P(None, 'fsdp')
Inputs may be any that keep to these rules, and one draw needn't show every extreme that they name: `lengths`: row r holds the sentences of the r-th device in order and sums to 256; each row has one sentence of exactly 192 characters. `dilation`: one of the two rates is exactly 8.
All inputs are finite; a program needn't handle non-finite values.
Results may differ from a plain program's by a relative error of at most 0.017.
Values may be sent and summed in bfloat16 or wider, within the bound.
A program may use at most 192 MiB of HBM per device.

v0:
```python
import math

import jax
import jax.numpy as jnp
from jax import lax
from jax.sharding import PartitionSpec as P

D = 800
H = 400
K_ENC = 5
K_DEC = 3
MAX_DILATION = 8
NS_STEPS = 5


EPSILON = 1e-05
NORM_FLOOR = 1e-07
COEF_A = 3.4445
COEF_B = -4.775
COEF_C = 2.0315
MOMENT_DECAY = 0.5
MATRIX_RATE = 0.5
VECTOR_RATE = 0.1
PRECISE = lax.Precision.HIGHEST


def layer_norm(values, gain_row, offset):
    center = values - jnp.mean(values, axis=-1, keepdims=True)
    spread = jnp.mean(center * center, axis=-1, keepdims=True)
    return center * lax.rsqrt(spread + EPSILON) * gain_row + offset


def norm_gelu(values, gain_row, offset):
    return jax.nn.gelu(layer_norm(values, gain_row, offset), approximate=True)


def segment_ids(lengths_row, count_rows):
    seq_ends = jnp.cumsum(lengths_row)
    places = jnp.arange(count_rows, dtype=jnp.int32)
    return jnp.sum((places[:, None] >= seq_ends[None, :]).astype(jnp.int32), axis=1)


def shifted(values, segment, offset, receptive_rows):
    count_rows = values.shape[0]
    padded = jnp.pad(values, ((receptive_rows, receptive_rows), (0, 0)))
    padded_seg = jnp.pad(segment, (receptive_rows, receptive_rows), constant_values=-1)
    first_index = offset + receptive_rows
    moved = lax.dynamic_slice_in_dim(padded, first_index, count_rows, 0)
    moved_seg = lax.dynamic_slice_in_dim(padded_seg, first_index, count_rows, 0)
    return jnp.where((moved_seg == segment)[:, None], moved, jnp.zeros((), values.dtype))


def orthogonalize(matrix):
    flipped = matrix.shape[0] > matrix.shape[1]
    current = matrix.T if flipped else matrix
    current = current / (jnp.sqrt(jnp.sum(current * current)) + NORM_FLOOR)
    for unused in range(NS_STEPS):
        gram_matrix = jnp.dot(current, current.T, precision=PRECISE)
        polynomial = COEF_B * gram_matrix + COEF_C * jnp.dot(
            gram_matrix, gram_matrix, precision=PRECISE
        )
        current = COEF_A * current + jnp.dot(polynomial, current, precision=PRECISE)
    return current.T if flipped else current


def step_scale(row_count, col_count, fan_count):
    return math.sqrt(max(row_count, col_count) / fan_count)


def block_forward(inputs, weights, segment, offsets, receptive_rows):
    w_in, w_conv, w_out, vec_wide, vec_narrow = weights
    wide_vec = vec_wide.astype(jnp.float32)
    narrow_vec = vec_narrow.astype(jnp.float32)
    first_act = norm_gelu(inputs, wide_vec[0], wide_vec[1]).astype(jnp.bfloat16)
    hidden = jnp.dot(first_act, w_in, preferred_element_type=jnp.float32) + narrow_vec[0]
    second_act = norm_gelu(hidden, narrow_vec[1], narrow_vec[2]).astype(jnp.bfloat16)
    tap_products = jnp.dot(second_act, w_conv, preferred_element_type=jnp.float32)
    inner_width = w_in.shape[1]
    conv_sum = shifted(tap_products[:, :inner_width], segment, offsets[0], receptive_rows)
    for j in range(1, len(offsets)):
        conv_sum = conv_sum + shifted(
            tap_products[:, j * inner_width : (j + 1) * inner_width],
            segment,
            offsets[j],
            receptive_rows,
        )
    conv_sum = conv_sum + narrow_vec[3]
    third_act = norm_gelu(conv_sum, narrow_vec[4], narrow_vec[5]).astype(jnp.bfloat16)
    result = inputs + jnp.dot(third_act, w_out, preferred_element_type=jnp.float32) + wide_vec[2]
    return (result, (inputs, first_act, hidden, second_act, conv_sum, third_act))


def block_backward(upstream, weights, stored, segment, offsets, receptive_rows):
    w_in, w_conv, w_out, vec_wide, vec_narrow = weights
    wide_vec = vec_wide.astype(jnp.float32)
    narrow_vec = vec_narrow.astype(jnp.float32)
    inputs, first_act, hidden, second_act, conv_sum, third_act = stored
    grad_bias_out = jnp.sum(upstream, axis=0)
    upstream_low = upstream.astype(jnp.bfloat16)
    grad_out = jnp.einsum("ti,to->io", third_act, upstream_low, preferred_element_type=jnp.float32)
    back_third = jnp.dot(upstream_low, w_out.T, preferred_element_type=jnp.float32)
    unused, pull_third = jax.vjp(norm_gelu, conv_sum, narrow_vec[4], narrow_vec[5])
    back_conv, grad_gain3, grad_shift3 = pull_third(back_third)
    grad_bias_conv = jnp.sum(back_conv, axis=0)
    conv_low = back_conv.astype(jnp.bfloat16)
    stacked = jnp.concatenate(
        [shifted(conv_low, segment, -offsets[j], receptive_rows) for j in range(len(offsets))],
        axis=1,
    )
    grad_conv = jnp.einsum("ti,tk->ik", second_act, stacked, preferred_element_type=jnp.float32)
    back_second = jnp.dot(stacked, w_conv.T, preferred_element_type=jnp.float32)
    unused, pull_second = jax.vjp(norm_gelu, hidden, narrow_vec[1], narrow_vec[2])
    back_hidden, grad_gain2, grad_shift2 = pull_second(back_second)
    grad_bias_in = jnp.sum(back_hidden, axis=0)
    hidden_low = back_hidden.astype(jnp.bfloat16)
    grad_in = jnp.einsum("td,th->dh", first_act, hidden_low, preferred_element_type=jnp.float32)
    back_first = jnp.dot(hidden_low, w_in.T, preferred_element_type=jnp.float32)
    unused, pull_first = jax.vjp(norm_gelu, inputs, wide_vec[0], wide_vec[1])
    back_inputs, grad_gain1, grad_shift1 = pull_first(back_first)
    grad_wide = jnp.stack([grad_gain1, grad_shift1, grad_bias_out])
    grad_narrow = jnp.stack(
        [grad_bias_in, grad_gain2, grad_shift2, grad_bias_conv, grad_gain3, grad_shift3]
    )
    return (upstream + back_inputs, (grad_in, grad_conv, grad_out, grad_wide, grad_narrow))


def by_owner(arrays, shard_dims, owners):
    flat_rows = []
    for array_full, shard_dim in zip(arrays, shard_dims):
        full_shape = array_full.shape
        split_shape = (
            full_shape[:shard_dim]
            + (owners, full_shape[shard_dim] // owners)
            + full_shape[shard_dim + 1 :]
        )
        leading_owner = jnp.moveaxis(array_full.reshape(split_shape), shard_dim, 0)
        flat_rows.append(leading_owner.reshape(owners, -1))
    return jnp.concatenate(flat_rows, axis=1)


def unflatten(flat_values, shard_shapes):
    results = []
    begin_at = 0
    for shard_shape in shard_shapes:
        length = math.prod(shard_shape)
        results.append(flat_values[begin_at : begin_at + length].reshape(shard_shape))
        begin_at += length
    return results


def assemble(owner_table, shard_shapes, shard_dims, owners):
    results = []
    begin_at = 0
    for shard_shape, shard_dim in zip(shard_shapes, shard_dims):
        length = math.prod(shard_shape)
        part_block = owner_table[:, begin_at : begin_at + length].reshape(
            (owners,) + tuple(shard_shape)
        )
        owner_inside = jnp.moveaxis(part_block, 0, shard_dim)
        merged_shape = (
            tuple(owner_inside.shape[:shard_dim])
            + (owners * shard_shape[shard_dim],)
            + tuple(owner_inside.shape[shard_dim + 2 :])
        )
        results.append(owner_inside.reshape(merged_shape))
        begin_at += length
    return results


def shards(
    tokens,
    cotangent,
    lengths,
    dilation,
    proj_in,
    conv_weight,
    proj_out,
    vec_wide,
    vec_narrow,
    mom_in,
    mom_conv,
    mom_out,
    mom_wide,
    mom_narrow,
):
    owners = lax.axis_size("fsdp")
    groups = lax.axis_size("dp")
    count_rows = tokens.shape[0]
    segment = segment_ids(lengths[0], count_rows)
    receptive_rows = 2 * MAX_DILATION
    split_col = K_ENC * H
    enc_offsets = [(j - K_ENC // 2) * dilation[0] for j in range(K_ENC)]
    dec_offsets = [-j * dilation[1] for j in range(K_DEC)]
    low_in = proj_in.astype(jnp.bfloat16)
    low_conv_part = conv_weight.astype(jnp.bfloat16)
    low_out = proj_out.astype(jnp.bfloat16)
    low_wide = vec_wide.astype(jnp.bfloat16)
    low_narrow = vec_narrow.astype(jnp.bfloat16)

    def conv_columns(b):
        if b == 0:
            return low_conv_part[:, :split_col]
        return low_conv_part[:, split_col:]

    def fetch_forward(b):
        conv_part = conv_columns(b)
        return (
            lax.all_gather(low_in[b], "fsdp", axis=0, tiled=True),
            lax.all_gather(conv_part, "fsdp", axis=0, tiled=True),
            lax.all_gather(low_out[b], "fsdp", axis=0, tiled=True),
            lax.all_gather(low_wide[b], "fsdp", axis=1, tiled=True),
            lax.all_gather(low_narrow[b], "fsdp", axis=1, tiled=True),
        )

    def fetch_again(b):
        conv_part = conv_columns(b)
        return (
            lax.all_gather(low_in[b], "fsdp", axis=0, tiled=True),
            lax.all_gather(conv_part, "fsdp", axis=0, tiled=True),
            lax.all_gather(low_out[b], "fsdp", axis=0, tiled=True),
            lax.all_gather(low_wide[b], "fsdp", axis=1, tiled=True),
            lax.all_gather(low_narrow[b], "fsdp", axis=1, tiled=True),
        )

    inputs = tokens.astype(jnp.float32)
    enc_weights = fetch_forward(0)
    enc_result, enc_stored = block_forward(
        inputs, enc_weights, segment, enc_offsets, receptive_rows
    )
    dec_weights = fetch_forward(1)
    dec_result, dec_stored = block_forward(
        enc_result, dec_weights, segment, dec_offsets, receptive_rows
    )
    dec_back = fetch_again(1)
    upstream, dec_grads = block_backward(
        cotangent.astype(jnp.float32), dec_back, dec_stored, segment, dec_offsets, receptive_rows
    )
    enc_back = fetch_again(0)
    grad_tokens, enc_grads = block_backward(
        upstream, enc_back, enc_stored, segment, enc_offsets, receptive_rows
    )
    full_grads = (
        jnp.stack([enc_grads[0], dec_grads[0]]),
        jnp.concatenate([enc_grads[1], dec_grads[1]], axis=1),
        jnp.stack([enc_grads[2], dec_grads[2]]),
        jnp.stack([enc_grads[3], dec_grads[3]]),
        jnp.stack([enc_grads[4], dec_grads[4]]),
    )
    owner_table = by_owner(full_grads, (1, 0, 1, 2, 2), owners)
    shard_len = owner_table.shape[1]
    padding = -shard_len % groups
    owner_table = jnp.pad(owner_table, ((0, 0), (0, padding)))
    padded_len = shard_len + padding
    old_shards = (mom_in, mom_conv, mom_out, mom_wide, mom_narrow)
    old_moment = jnp.pad(jnp.concatenate([m.reshape(-1) for m in old_shards]), (0, padding))
    own_sum = lax.psum_scatter(
        owner_table.reshape(-1).astype(jnp.bfloat16), "fsdp", scatter_dimension=0, tiled=True
    ).astype(jnp.float32)
    total_sum = lax.psum(own_sum, "dp")
    new_moment = MOMENT_DECAY * old_moment + total_sum
    shard_shapes = [m.shape for m in old_shards]
    new_mom_in, new_mom_conv, new_mom_out, new_mom_wide, new_mom_narrow = unflatten(
        new_moment, shard_shapes
    )
    total_tokens = count_rows * groups * owners
    vector_step = VECTOR_RATE / math.sqrt(total_tokens)
    new_vec_wide = vec_wide - vector_step * new_mom_wide
    new_vec_narrow = vec_narrow - vector_step * new_mom_narrow
    scales = [
        step_scale(D, H, D),
        step_scale(D, H, D),
        step_scale(H, K_ENC * H, K_ENC * H),
        step_scale(H, K_DEC * H, K_DEC * H),
        step_scale(H, D, H),
        step_scale(H, D, H),
    ]
    owner_self = lax.axis_index("fsdp")
    whole_table = (
        lax.all_gather(new_moment.astype(jnp.bfloat16), "fsdp", axis=0, tiled=True)
        .astype(new_moment.dtype)
        .reshape(owners, padded_len)
    )
    whole_in, whole_conv, whole_out = assemble(whole_table, shard_shapes[:3], (1, 0, 1), owners)
    matrices = [
        whole_in[0],
        whole_in[1],
        whole_conv[:, :split_col],
        whole_conv[:, split_col:],
        whole_out[0],
        whole_out[1],
    ]
    updates = []
    for k in range(6):
        ortho_part = lax.cond(owner_self == k % owners, orthogonalize, jnp.zeros_like, matrices[k])
        updates.append(ortho_part * scales[k])
    step_in, step_conv, step_out = (
        lax.psum_scatter(
            jnp.stack([updates[0], updates[1]]).astype(jnp.bfloat16),
            "fsdp",
            scatter_dimension=1,
            tiled=True,
        ).astype(jnp.float32),
        lax.psum_scatter(
            jnp.concatenate([updates[2], updates[3]], axis=1).astype(jnp.bfloat16),
            "fsdp",
            scatter_dimension=0,
            tiled=True,
        ).astype(jnp.float32),
        lax.psum_scatter(
            jnp.stack([updates[4], updates[5]]).astype(jnp.bfloat16),
            "fsdp",
            scatter_dimension=1,
            tiled=True,
        ).astype(jnp.float32),
    )
    new_proj_in = proj_in - MATRIX_RATE * step_in
    new_conv = conv_weight - MATRIX_RATE * step_conv
    new_proj_out = proj_out - MATRIX_RATE * step_out
    return (
        dec_result.astype(jnp.bfloat16),
        grad_tokens,
        new_mom_in,
        new_mom_conv,
        new_mom_out,
        new_mom_wide,
        new_mom_narrow,
        new_proj_in,
        new_conv,
        new_proj_out,
        new_vec_wide,
        new_vec_narrow,
        new_proj_in.astype(jnp.bfloat16),
        new_conv.astype(jnp.bfloat16),
        new_proj_out.astype(jnp.bfloat16),
    )


def solution(mesh):
    placed = (
        P(("dp", "fsdp"), None),
        P(("dp", "fsdp"), None),
        P(("dp", "fsdp"), None),
        P(),
        P(None, "fsdp", None),
        P("fsdp", None),
        P(None, "fsdp", None),
        P(None, None, "fsdp"),
        P(None, None, "fsdp"),
        P(None, "fsdp", None),
        P("fsdp", None),
        P(None, "fsdp", None),
        P(None, None, "fsdp"),
        P(None, None, "fsdp"),
    )
    return jax.shard_map(
        shards,
        mesh=mesh,
        in_specs=placed,
        out_specs=(
            P(("dp", "fsdp"), None),
            P(("dp", "fsdp"), None),
            P(None, "fsdp", None),
            P("fsdp", None),
            P(None, "fsdp", None),
            P(None, None, "fsdp"),
            P(None, None, "fsdp"),
            P(None, "fsdp", None),
            P("fsdp", None),
            P(None, "fsdp", None),
            P(None, None, "fsdp"),
            P(None, None, "fsdp"),
            P(None, "fsdp", None),
            P("fsdp", None),
            P(None, "fsdp", None),
        ),
        check_vma=False,
    )
```

profile of v0, /device:TPU:1, one launch (start us, length us, event | category | flops | bytes accessed | tf_op | source)
XLA Modules:
  0.0 1153.2 jit_solution(15029752469641934540)
XLA Ops:
  10.6 13.0 %all-gather.2 = bf16[1,6,400]{1,0,2:T(2,128)(2,1)S(1)} all-gather(bf16[1,6,100]{1,0,2:T(2,128)(2,1)S(1)} %get-tuple-element.222), channel_id=4, replica_groups=mesh['dp'=8,'fsdp'=4] {'fsdp'}, dimensions={2}, use_global_device_ids=true | all-gather | bytes 6000 | tf_op jit(solution)/shard_map/all_gather | solution.py:212
  23.9 8.7 slice_reduce_fusion.13
  32.5 17.2 %all-gather = bf16[1,3,800]{1,0,2:T(2,128)(2,1)S(1)} all-gather(bf16[1,3,200]{1,0,2:T(2,128)(2,1)S(1)} %get-tuple-element.220), channel_id=2, replica_groups=mesh['dp'=8,'fsdp'=4] {'fsdp'}, dimensions={2}, use_global_device_ids=true | all-gather | bytes 6000 | tf_op jit(solution)/shard_map/all_gather | solution.py:211
  50.2 8.0 slice_reduce_fusion.5
  59.0 16.7 %all-gather.9 = bf16[4,100,1200]{2,1,0:T(8,128)(2,1)S(1)} all-gather(bf16[1,100,1200]{2,1,0:T(8,128)(2,1)S(1)} %slice_bitcast_fusion.1), channel_id=1, replica_groups=mesh['dp'=8,'fsdp'=4] {'fsdp'}, dimensions={0}, use_global_device_ids=true | all-gather | bytes 1200000 | tf_op jit(solution)/shard_map/all_gather | solution.py:209
  75.6 15.0 %all-gather.1 = bf16[1,800,400]{2,1,0:T(8,128)(2,1)S(1)} all-gather(bf16[1,200,400]{2,1,0:T(8,128)(2,1)S(1)} %get-tuple-element.214), channel_id=3, replica_groups=mesh['dp'=8,'fsdp'=4] {'fsdp'}, dimensions={1}, use_global_device_ids=true | all-gather | bytes 800000 | tf_op jit(solution)/shard_map/all_gather | solution.py:208
  97.9 10.7 all-gather.6
  108.8 12.1 %all-gather.4 = bf16[1,3,800]{1,0,2:T(2,128)(2,1)S(1)} all-gather(bf16[1,3,200]{1,0,2:T(2,128)(2,1)S(1)} %get-tuple-element.219), channel_id=6, replica_groups=mesh['dp'=8,'fsdp'=4] {'fsdp'}, dimensions={2}, use_global_device_ids=true | all-gather | bytes 6000 | tf_op jit(solution)/shard_map/all_gather | solution.py:211
  125.5 8.7 slice_reduce_fusion.7
  134.2 14.7 %all-gather.5 = bf16[1,800,400]{2,1,0:T(8,128)(2,1)} all-gather(bf16[1,200,400]{2,1,0:T(8,128)(2,1)S(1)} %copy-done.31), channel_id=7, replica_groups=mesh['dp'=8,'fsdp'=4] {'fsdp'}, dimensions={1}, use_global_device_ids=true | all-gather | bytes 800000 | tf_op jit(solution)/shard_map/all_gather | solution.py:208
  149.4 22.9 %all-gather.7 = bf16[1,400,800]{2,0,1:T(2,128)(2,1)} all-gather(bf16[1,100,800]{2,0,1:T(2,128)(2,1)S(1)} %get-tuple-element.215), channel_id=9, replica_groups=mesh['dp'=8,'fsdp'=4] {'fsdp'}, dimensions={1}, use_global_device_ids=true | all-gather | bytes 800000 | tf_op jit(solution)/shard_map/all_gather | solution.py:210
  172.4 27.5 %all-gather.3 = bf16[1,400,800]{2,0,1:T(2,128)(2,1)} all-gather(bf16[1,100,800]{2,0,1:T(2,128)(2,1)S(1)} %get-tuple-element.216), channel_id=5, replica_groups=mesh['dp'=8,'fsdp'=4] {'fsdp'}, dimensions={1}, use_global_device_ids=true | all-gather | bytes 800000 | tf_op jit(solution)/shard_map/all_gather | solution.py:210
  199.9 7.9 slice_reduce_fusion.2
  246.6 4.6 reshape.585
  251.3 2.9 reshape.488
  256.7 3.2 pad_maximum_fusion
  267.6 5.2 reshape.583
  272.8 2.8 reshape.487
  284.5 11.0 convert_element_type.165
  297.4 203.3 %all-reduce.25.cloned.1.call-done = bf16[2569600]{0:T(1024)(128)(2,1)} async-done(((bf16[2569600]{0:T(1024)(128)(2,1)}), bf16[2569600]{0:T(1024)(128)(2,1)}) %all-reduce.25.cloned.1.call-update) | async-done | bytes 5139216
  500.7 3.5 dynamic-slice_convert_fusion
  511.7 20.4 %concatenate.39 = f32[642400]{0:T(1024)} concatenate(f32[160000]{0:T(1024)} %reshape.482, f32[320000]{0:T(1024)S(1)} %reshape.483, f32[160000]{0:T(1024)} %reshape.484, f32[1200]{0:T(1024)S(1)} %reshape.485, f32[1200]{0:T(1024)S(1)} %reshape.486), dimensions={0} | concatenate | bytes 5139200 | tf_op jit(solution)/shard_map/concatenate | solution.py:255
  532.1 2.9 fusion.63
  535.0 32.7 %all-reduce.21.cloned.1.call-done = f32[642400]{0:T(1024)} async-done(((f32[642400]{0:T(1024)}), f32[642400]{0:T(1024)}) %all-reduce.21.cloned.1.call-update) | async-done | bytes 2569616 | tf_op jit(solution)/shard_map/psum | solution.py:259
  567.7 3.8 fusion.196
  571.5 3.0 broadcast.405
  574.6 20.7 %dynamic-update-slice = bf16[2569600]{0:T(1024)(128)(2,1)} dynamic-update-slice(bf16[2569600]{0:T(1024)(128)(2,1)} %broadcast.405, bf16[642400]{0:T(1024)(128)(2,1)} %get-tuple-element.174, u32[]{:T(128)} %bitcast.48) | dynamic-update-slice | bytes 2569604
  600.8 180.1 %all-reduce.23.cloned.1.call-done = bf16[2569600]{0:T(1024)(128)(2,1)} async-done(((bf16[2569600]{0:T(1024)(128)(2,1)}), bf16[2569600]{0:T(1024)(128)(2,1)}) %all-reduce.23.cloned.1.call-update) | async-done | bytes 5139216
  780.9 13.0 %reshape.501 = f32[4,642400]{1,0:T(4,128)} reshape(bf16[2569600]{0:T(1024)(128)(2,1)} %all-reduce.23.cloned.1.call-done) | data formatting | bytes 15417600 | tf_op jit(solution)/shard_map/reshape | solution.py:281
  793.9 5.7 slice.302
  799.6 3.7 fusion.207
  803.3 7.3 reshape_reshape.10
  810.6 4.2 reshape.499
  816.8 45.4 %conditional.10 = (f32[400,800]{1,0:T(8,128)}) conditional(s32[]{:T(128)} %convert_element_type.167, () %tuple.52, f32[2,4,100,800]{3,2,1,0:T(8,128)S(1)} %copy.143), branch_computations={%region_60.61_spmd, %region_61.63_spmd} | conditional | flops 19206561792 | bytes 43520064 | solution.py:294
  822.6 4.6 fusion.229
  828.8 2.8 convolution_add_fusion.11
  831.6 2.8 fusion.230
  835.9 3.1 convolution_add_fusion.10
  843.3 2.8 convolution_add_fusion.9
  846.2 2.8 fusion.232
  850.9 2.8 convolution_add_fusion.8
  858.1 4.0 convolution_add_fusion.7
  864.6 12.1 %conditional.11 = (f32[400,800]{1,0:T(8,128)S(1)}) conditional(s32[]{:T(128)} %convert_element_type.169, () %tuple.53, f32[2,4,100,800]{3,2,1,0:T(8,128)S(1)} %copy.143), branch_computations={%region_63.64_spmd, %region_64.66_spmd} | conditional | flops 19206561792 | bytes 38400036 | solution.py:294
  880.2 5.7 reshape.498
  885.8 3.2 copy.140
  889.0 2.8 conditional.7
  892.7 49.3 %conditional.6 = (bf16[1,800,400]{1,2,0:T(8,128)(2,1)S(1)}) conditional(s32[]{:T(128)} %convert_element_type.167, () %tuple.48, f32[2,4,200,400]{2,1,3,0:T(4,128)} %copy.140), branch_computations={%region_46.47_spmd, %region_47.49_spmd} | conditional | flops 19213279232 | bytes 62080064 | solution.py:294
  892.7 2.9 multiply_reduce_fusion
  896.3 3.3 broadcast_multiply_fusion
  899.5 3.5 mul.217
  908.5 2.8 fusion.240
  911.3 2.9 fusion.19
  915.7 3.1 multiply_add_fusion.2
  923.2 2.8 fusion.242
  926.0 2.9 fusion.17
  930.6 2.9 fusion.16
  933.5 3.1 fusion.11
  938.2 3.4 fusion.1
  946.0 13.2 %conditional.9 = (bf16[400,1200]{1,0:T(8,128)(2,1)S(1)}) conditional(s32[]{:T(128)} %convert_element_type.172, () %tuple.51, f32[400,3200]{1,0:T(8,128)} %reshape_reshape.10), branch_computations={%region_56.57_spmd, %region_57.59_spmd} | conditional | flops 26890078208 | bytes 44865060 | solution.py:294
  960.1 11.5 conditional.8
  975.1 98.9 %fusion = bf16[112,3200]{1,0:T(8,128)(2,1)S(1)} fusion(bf16[400,3200]{1,0:T(8,128)(2,1)S(1)} %pad_maximum_fusion.1), kind=kCustom, calls=%all-reduce-scatter | all-reduce-scatter fusion | flops 1433601 | bytes 3277312
  1074.1 5.6 collective-permute-start
  1089.5 5.9 concatenate.43
  1098.2 43.6 %all-reduce.27.cloned.1.call-done = (bf16[2,800,400]{2,1,0:T(8,128)(2,1)}, bf16[2,400,800]{2,0,1:T(2,128)(2,1)}) async-done(((bf16[2,800,400]{2,1,0:T(8,128)(2,1)}, bf16[2,400,800]{2,0,1:T(2,128)(2,1)}), (bf16[2,800,400]{2,1,0:T(8,128)(2,1)}, bf16[2,400,800]{2,0,1:T(2,128)(2,1)})) %all-reduce.27.cloned.1.call-update) | async-done | bytes 2560016
  (305 shorter events, 148.8 us)
Async XLA Ops:
  7.2 2.5 copy-start.2
  7.2 200.6 %all-gather.12.cloned.1.call-start = ((), (), s32[]{:S(2)}) async-start(), calls=%async_computation.2 | async-start | bytes 2129920 | tf_op jit(solution)/shard_map/all_gather | solution.py:209
  8.7 1.4 copy-start.35
  8.7 1.6 copy-start.37
  9.5 491.2 %all-reduce.25.cloned.1.call-start = ((), (), s32[]{:S(2)}) async-start(), calls=%async_computation.3 | async-start | bytes 10280960
  32.5 25.7 %copy-start.17 = (f32[2,200,400]{2,1,0:T(8,128)S(1)}, f32[2,200,400]{2,1,0:T(8,128)}, u32[]{:S(2)}) copy-start(f32[2,200,400]{2,1,0:T(8,128)} %param.30) | copy-start | bytes 1920004
  90.7 0.9 copy-start.28
  90.7 0.9 copy-start.42
  90.7 6.7 copy-start.47
  90.7 6.9 copy-start.11
  91.6 118.5 %copy-start.4 = (f32[256,400]{0,1:T(8,128)}, f32[256,400]{0,1:T(8,128)S(1)}, u32[]{:S(2)}) copy-start(f32[256,400]{0,1:T(8,128)S(1)} %get-tuple-element.241) | copy-start | bytes 1228804
  124.1 10.0 copy-start.31
  211.3 0.7 copy-start.43
  211.3 0.7 copy-start.44
  211.3 0.7 copy-start.45
  211.3 0.7 copy-start.46
  212.0 1.4 copy-start.25
  213.4 1.1 copy-start.30
  214.1 11.2 copy-start.15
  214.5 1.2 copy-start.26
  217.0 2.3 copy-start.13
  217.0 1.5 copy-start.24
  225.3 1.0 copy-start.12
  228.9 1.0 copy-start.5
  230.9 1.2 copy-start.29
  278.1 2.4 copy-start.9
  295.5 0.7 copy-start.41
  295.6 272.1 %all-reduce.21.cloned.1.call-start = ((), (), s32[]{:S(2)}) async-start(), calls=%async_computation | async-start | bytes 5144576 | tf_op jit(solution)/shard_map/psum | solution.py:259
  504.2 1.5 copy-start.39
  504.2 1.6 copy-start.40
  504.2 1.7 copy-start.27
  504.3 3.3 copy-start.32
  504.3 276.7 %all-reduce.23.cloned.1.call-start = ((), (), s32[]{:S(2)}) async-start(), calls=%async_computation.1 | async-start | bytes 10280960
  511.7 20.4 %copy-start.14 = (f32[256,400]{0,1:T(8,128)S(1)}, f32[256,400]{0,1:T(8,128)}, u32[]{:S(2)}) copy-start(f32[256,400]{0,1:T(8,128)} %copy-done.13) | copy-start | bytes 1228804
  511.7 20.4 %copy-start.16 = (f32[256,800]{0,1:T(8,128)S(1)}, f32[256,800]{0,1:T(8,128)}, u32[]{:S(2)}) copy-start(f32[256,800]{0,1:T(8,128)} %copy-done.15) | copy-start | bytes 2457604
  571.5 28.2 %copy-start.1 = (f32[642400]{0:T(1024)}, f32[642400]{0:T(1024)S(1)}, u32[]{:S(2)}) copy-start(f32[642400]{0:T(1024)S(1)} %get-tuple-element.175) | copy-start | bytes 7708804
  595.3 546.5 %all-reduce.27.cloned.1.call-start = ((), (), s32[]{:S(2)}) async-start(), calls=%async_computation.4 | async-start | bytes 6144000
  827.2 1.5 copy-start
  876.6 1.1 copy-start.20
  891.8 0.9 copy-start.21
  936.6 1.5 copy-start.7
  942.0 0.9 copy-start.22
  959.1 1.0 copy-start.10
  971.6 1.2 copy-start.3
  975.1 104.6 %copy-start.33 = (f32[2,6,100]{2,1,0:T(8,128)S(1)}, f32[2,6,100]{2,1,0:T(8,128)}, u32[]{:S(2)}) copy-start(f32[2,6,100]{2,1,0:T(8,128)} %reshape.495) | copy-start | bytes 14404
  975.1 104.6 %copy-start.36 = (f32[2,6,100]{2,0,1:T(2,128)S(1)}, f32[2,6,100]{2,0,1:T(2,128)}, u32[]{:S(2)}) copy-start(f32[2,6,100]{2,0,1:T(2,128)} %param.34) | copy-start | bytes 14404
  1074.1 8.2 copy-start.34
  1074.1 8.9 copy-start.38
  1074.1 15.4 %collective-permute-start = (bf16[36,3200]{1,0:T(8,128)(2,1)S(1)}, bf16[36,3200]{1,0:T(8,128)(2,1)S(1)}, u32[]{:S(2)}, u32[]{:S(2)}) collective-permute-start(bf16[36,3200]{1,0:T(8,128)(2,1)S(1)} %slice.304), channel_id=1, source_target_pairs={{0,1},{1,2},{2,3},{4,5},{5,6},{6,7},{8,9},{9,10},{10,11},{12,13},{... | collective-permute-start | bytes 691208
  1084.9 2.9 copy-start.23
  1087.8 7.7 copy-start.8
  1095.4 46.3 %copy-start.18 = (f32[2,200,400]{2,1,0:T(8,128)S(1)}, f32[2,200,400]{2,1,0:T(8,128)}, u32[]{:S(2)}) copy-start(f32[2,200,400]{2,1,0:T(8,128)} %param.30) | copy-start | bytes 1920004
  1098.2 45.8 %copy-start.19 = (f32[2,100,800]{2,0,1:T(2,128)S(1)}, f32[2,100,800]{2,0,1:T(2,128)}, u32[]{:S(2)}) copy-start(f32[2,100,800]{2,0,1:T(2,128)} %param.32) | copy-start | bytes 1920004
Sparse Core Ops, SparseCore 0:
  10.2 48.4 all-gather.11
  295.7 205.0 all-reduce.24
  504.4 63.2 all-reduce.20
  595.4 185.5 all-reduce.22
  975.2 166.4 all-reduce.26
where the time goes:
time: 1170 us; the launch traced here: 1150 us
  waiting for transfers between devices  460 us (39%)
  blocking collectives  249 us (21%)
  local copies, waits for them, and re-layouts  223 us (19%)
  matrix products  98.6 us (8%)
  other arithmetic  51.9 us (4%)
  loops' own time  41.4 us (4%)
  between operations  23.5 us (2%)
    unnamed x9, waiting for transfers between devices  427 us
    unnamed x1, blocking collectives  98.9 us
    unnamed x126, local copies, waits for them, and re-layouts  65 us
    all_gather x2, blocking collectives, fetch_forward(): lax.all_gather(low_out[b], 'fsdp', axis=0, tiled=True)  50.4 us
    another operation x6, loops' own time, shards(): lax.cond(owner_self == k % owners, orthogonalize, jnp.zeros_like, matrice...  41.4 us
    psum x1, waiting for transfers between devices, shards(): total_sum = lax.psum(own_sum, 'dp')  32.7 us
    dot_general x10, matrix products, orthogonalize(): current = COEF_A * current + jnp.dot(polynomial, current, precision=PRECISE)  30.6 us
    dot_general x10, matrix products, orthogonalize(): gram_matrix = jnp.dot(current, current.T, precision=PRECISE)  30.2 us
  transfers between devices with their start and end apart: 6, of which 4 were waited for; matrix products, arithmetic and copies ran while one was open for 17% of the time, Pallas kernels for 0%

commit v1 on v0

v1 whole, which is shorter than its diff:
```python
import functools
import math

import jax
import jax.numpy as jnp
from jax import lax
from jax.experimental import pallas as pl
from jax.experimental.pallas import tpu as pltpu
from jax.sharding import PartitionSpec as P

D = 800
H = 400
K_ENC = 5
K_DEC = 3
NS_STEPS = 5
EPSILON = 1e-05
NORM_FLOOR = 1e-07
COEF_A = 3.4445
COEF_B = -4.775
COEF_C = 2.0315
MOMENT_DECAY = 0.5
MATRIX_RATE = 0.5
VECTOR_RATE = 0.1

F32 = jnp.float32
BF16 = jnp.bfloat16
MESH = pl.DeviceIdType.MESH

OWNERS = 4
PIECES = 8
SHARD = 100
ROWS = 112
PIECE = 896
COLS = PIECES * PIECE
WO_AT = (0, 896)
CONV_AT = 1792
WI_AT = ((4992, 5504), (6016, 6528))
VEC_AT = 7040
SPLIT = K_ENC * H
TOK = 256
GROUPED = OWNERS * ROWS

GELU_K = math.sqrt(2.0 / math.pi)
GELU_C = 0.044715


def vmem(shape, dtype):
    return pltpu.VMEM(shape, dtype)


def dot(a, b):
    return lax.dot_general(a, b, (((1,), (0,)), ((), ())), preferred_element_type=F32)


def dot_nt(a, b):
    return lax.dot_general(a, b, (((1,), (1,)), ((), ())), preferred_element_type=F32)


def dot_tn(a, b):
    return lax.dot_general(a, b, (((0,), (0,)), ((), ())), preferred_element_type=F32)


def one_hot(mask):
    return jnp.where(mask, 1.0, 0.0).astype(BF16)


def pack(slab, conv, w_in, w_out, wide, narrow):
    slab[...] = jnp.zeros((ROWS, COLS), BF16)
    slab[:SHARD, CONV_AT : CONV_AT + 3200] = conv[...].astype(BF16)
    for b in range(2):
        slab[:SHARD, WO_AT[b] : WO_AT[b] + D] = w_out[b].astype(BF16)
        for h in range(2):
            at = WI_AT[b][h]
            slab[:SHARD, at : at + H] = w_in[b, h * SHARD : (h + 1) * SHARD, :].astype(BF16)
    for b in range(2):
        for k in range(6):
            m = 6 * b + k
            slab[m : m + 1, VEC_AT : VEC_AT + SHARD] = narrow[b, k : k + 1, :].astype(BF16)
        for k in range(3):
            for h in range(2):
                m = 16 + 16 * h + 3 * b + k
                part = wide[b, k : k + 1, h * SHARD : (h + 1) * SHARD]
                slab[m : m + 1, VEC_AT : VEC_AT + SHARD] = part.astype(BF16)


def place():
    at = lax.axis_index("dp")
    piece = at % PIECES
    return at - piece, piece, lax.axis_index("fsdp")


def flip(value, bit):
    return value + bit - 2 * bit * ((value // bit) % 2)


def other_owner(own, step):
    if step == 3:
        return 3 - own
    return flip(own, step)


def columns(piece):
    return pl.ds(pl.multiple_of(piece * PIECE, PIECE), PIECE)


def remote(src, dst, send, recv, device):
    return pltpu.make_async_remote_copy(
        src_ref=src,
        dst_ref=dst,
        send_sem=send,
        recv_sem=recv,
        device_id=device,
        device_id_type=MESH,
    )


def greet(devices):
    barrier = pltpu.get_barrier_semaphore()
    for device in devices:
        pl.semaphore_signal(barrier, inc=1, device_id=device, device_id_type=MESH)
    return barrier


class Gather:
    SEMS = 10

    def __init__(self, view, send, recv, at):
        base, piece, own = place()
        self.view, self.send, self.recv, self.at = view, send, recv, at
        self.piece = piece
        self.near = {bit: (base + flip(piece, bit), own) for bit in (1, 2, 4)}
        self.started = []

    def copy(self, bit, q, part, k):
        ref = self.view(q, part)
        sems = (self.send.at[self.at + k], self.recv.at[self.at + k])
        return remote(ref, ref, sems[0], sems[1], self.near[bit])

    def start(self, bit, q, part, k):
        copy = self.copy(bit, q, part, k)
        copy.start()
        self.started.append(copy)

    def first(self):
        p = self.piece
        self.start(4, p, 0, 0)
        self.start(2, p, 1, 1)

    def second(self):
        p = self.piece
        for k in (0, 1):
            self.started[k].wait_recv()
        self.start(2, p, 0, 2)
        self.start(2, flip(p, 4), 0, 3)
        self.start(4, p, 1, 4)
        self.start(4, flip(p, 2), 1, 5)
        self.start(1, p, None, 6)

    def third(self):
        p = self.piece
        for k in (2, 3, 4, 5):
            self.started[k].wait_recv()
        self.start(1, flip(p, 2), None, 7)
        self.start(1, flip(p, 4), None, 8)
        self.start(1, flip(flip(p, 2), 4), None, 9)

    def last(self):
        for k in (6, 7, 8, 9):
            self.started[k].wait_recv()

    def finish(self):
        for copy in self.started:
            copy.wait_send()


def part_rows(part):
    if part is None:
        return pl.ds(0, ROWS)
    return pl.ds(0, 64) if part == 0 else pl.ds(64, 48)


def gather_kernel(conv, w_in, w_out, wide, narrow, full, z_send, z_recv, send, recv):
    base, piece, own = place()
    me = base + piece
    near = [(base + flip(piece, bit), own) for bit in (1, 2, 4)]
    column = [(me, other_owner(own, step)) for step in (1, 2, 3)]
    barrier = greet(near + column)
    pack(full.at[own], conv, w_in, w_out, wide, narrow)
    pl.semaphore_wait(barrier, 6)
    mine = full.at[own, :, columns(piece)]
    crossing = []
    for step in (1, 2, 3):
        copy = remote(mine, mine, z_send.at[step - 1], z_recv.at[step - 1], column[step - 1])
        copy.start()
        crossing.append(copy)
    gathers = []
    for step in (1, 2, 3):
        there = other_owner(own, step)

        def view(q, part, there=there):
            return full.at[there, part_rows(part), columns(q)]

        gathers.append(Gather(view, send, recv, (step - 1) * Gather.SEMS))
    for step in (1, 2, 3):
        crossing[step - 1].wait_recv()
        gathers[step - 1].first()
    for one in gathers:
        one.second()
    for one in gathers:
        one.third()
    for one in gathers:
        one.last()
    for one in gathers:
        one.finish()
    for copy in crossing:
        copy.wait_send()


def gather_weights(conv, w_in, w_out, wide, narrow):
    in_vmem = pl.BlockSpec(memory_space=pltpu.VMEM)
    count = 3 * Gather.SEMS
    return pl.pallas_call(
        gather_kernel,
        out_shape=jax.ShapeDtypeStruct((OWNERS, ROWS, COLS), BF16),
        in_specs=[in_vmem] * 5,
        out_specs=in_vmem,
        scratch_shapes=[
            pltpu.SemaphoreType.DMA((3,)),
            pltpu.SemaphoreType.DMA((3,)),
            pltpu.SemaphoreType.DMA((count,)),
            pltpu.SemaphoreType.DMA((count,)),
        ],
        compiler_params=pltpu.CompilerParams(
            collective_id=0, has_side_effects=True, vmem_limit_bytes=40 << 20
        ),
        name="gather_weights",
    )(conv, w_in, w_out, wide, narrow)


def norm_forward(src, width, chunk, gain, shift, act, unit, slope, spread):
    def body(k, carry):
        rows = pl.ds(pl.multiple_of(k * chunk, chunk), chunk)
        x = src[rows, :width].astype(F32)
        center = x - jnp.mean(x, axis=1, keepdims=True)
        scale = lax.rsqrt(jnp.mean(center * center, axis=1, keepdims=True) + EPSILON)
        xhat = center * scale
        a = xhat * gain + shift
        square = a * a
        half = 0.5 + 0.5 * jnp.tanh(a * (GELU_K + (GELU_K * GELU_C) * square))
        act[rows, :width] = (a * half).astype(BF16)
        unit[rows, :width] = xhat
        inner = GELU_K + (3.0 * GELU_K * GELU_C) * square
        slope[rows, :width] = half + (2.0 * a * inner) * (half * (1.0 - half))
        spread[rows, :] = jnp.broadcast_to(scale, (chunk, 128))
        return carry

    lax.fori_loop(0, TOK // chunk, body, 0)


def fold_rows(values):
    total = values[0:8]
    for k in range(1, values.shape[0] // 8):
        total = total + values[8 * k : 8 * k + 8]
    return total


def norm_backward(grad, width, chunk, gain, unit, slope, spread, finish):
    def body(k, sums):
        rows = pl.ds(pl.multiple_of(k * chunk, chunk), chunk)
        da = grad[rows, :width] * slope[rows, :width]
        xhat = unit[rows, :width]
        product = da * xhat
        dxhat = da * gain
        mean_one = jnp.mean(dxhat, axis=1, keepdims=True)
        mean_two = jnp.mean(dxhat * xhat, axis=1, keepdims=True)
        dx = spread[rows, 0:1] * (dxhat - mean_one - xhat * mean_two)
        finish(rows, dx)
        return (sums[0] + fold_rows(product), sums[1] + fold_rows(da), sums[2] + fold_rows(dx))

    zero = jnp.zeros((8, width), F32)
    sums = lax.fori_loop(0, TOK // chunk, body, (zero, zero, zero))
    return tuple(jnp.sum(s, axis=0, keepdims=True) for s in sums)


def iota(shape, dim):
    return lax.broadcasted_iota(jnp.int32, shape, dim)


def compute_kernel(
    dilation, lengths, tokens, cotangent, full, mom_conv, mom_in, mom_out, mom_wide, mom_narrow,
    out, grad_tokens, grads,
    far, perm_h, vec_w, vec_n, w_in, x_one, wide_grad, tall,
    act_d, act_h, act_g, hid, conv_in, spare, e_all,
    unit_d, slope_d, spread_d, unit_h, slope_h, spread_h,
):
    own = lax.axis_index("fsdp")
    row, col = iota((TOK, TOK), 0), iota((TOK, TOK), 1)
    seg_row, seg_col = jnp.zeros((TOK, TOK), jnp.int32), jnp.zeros((TOK, TOK), jnp.int32)
    end = jnp.int32(0)
    for k in range(8):
        end = end + lengths[0, k]
        seg_row = seg_row + jnp.where(row >= end, 1, 0)
        seg_col = seg_col + jnp.where(col >= end, 1, 0)
    far[...] = jnp.where(seg_row == seg_col, col - row, 4 * TOK)

    def mover(offset):
        return one_hot(far[...] == offset)

    row, col = iota((H, GROUPED), 0), iota((H, GROUPED), 1)
    group = jnp.where(col >= ROWS, 1, 0) + jnp.where(col >= 2 * ROWS, 1, 0) + jnp.where(col >= 3 * ROWS, 1, 0)
    used = col - ROWS * group < SHARD
    perm_h[...] = one_hot((row == col - (ROWS - SHARD) * group) & used)

    row_n, col_n = iota((128, H), 0), iota((128, H), 1)
    row_w, col_w = iota((128, D), 0), iota((128, D), 1)
    total_n, total_w = jnp.zeros((16, H), F32), jnp.zeros((16, D), F32)
    put_n, put_w = [], []
    for i in range(OWNERS):
        lanes = slice(VEC_AT, VEC_AT + 128)
        put_n.append(one_hot((col_n == row_n + SHARD * i) & (row_n < SHARD)))
        total_n = total_n + dot(full[i, 0:16, lanes], put_n[i])
        for h in range(2):
            put_w.append(one_hot((col_w == row_w + SHARD * (2 * i + h)) & (row_w < SHARD)))
            total_w = total_w + dot(full[i, 16 + 16 * h : 32 + 16 * h, lanes], put_w[2 * i + h])
    vec_n[...] = total_n
    vec_w[...] = total_w

    def narrow(b, k):
        return vec_n[6 * b + k : 6 * b + k + 1, :]

    def wide(b, k):
        return vec_w[3 * b + k : 3 * b + k + 1, :]

    def weight_out(b):
        return full[:, :, WO_AT[b] : WO_AT[b] + D].reshape(GROUPED, D)

    for b in range(2):
        for i in range(OWNERS):
            for h in range(2):
                at = SHARD * (2 * i + h)
                lanes = slice(WI_AT[b][h], WI_AT[b][h] + H)
                w_in[b, at : at + SHARD, :] = full[i, 0:SHARD, lanes].astype(F32)

    def taps(b):
        if b == 0:
            return [(H * j, (j - K_ENC // 2) * dilation[0]) for j in range(K_ENC)]
        return [(SPLIT + H * j, -j * dilation[1]) for j in range(K_DEC)]

    def window(at):
        return at - at % 128

    x_one[...] = tokens[...].astype(F32)
    for b in range(2):
        src = tokens if b == 0 else x_one
        norm_forward(src, D, 16, wide(b, 0), wide(b, 1), act_d.at[b], unit_d.at[b], slope_d.at[b], spread_d.at[b])
        hid[:, :] = dot(act_d[b], w_in[b].astype(BF16)) + narrow(b, 0)
        norm_forward(hid, H, 32, narrow(b, 1), narrow(b, 2), act_h.at[0], unit_h.at[b, 0], slope_h.at[b, 0], spread_h.at[b, 0])
        act_g[b, 0] = dot(act_h[0], perm_h[...]).astype(BF16)
        for j, (at, offset) in enumerate(taps(b)):
            moved = dot(mover(offset), act_g[b, 0]).astype(BF16)
            low = CONV_AT + window(at)
            product = dot(moved, full[:, :, low : low + 512].reshape(GROUPED, 512))
            if at % 128:
                product = pltpu.roll(product, 512 - at % 128, 1)
            if j == 0:
                conv_in[...] = product
            else:
                conv_in[...] += product
        conv_in[:, :H] += narrow(b, 3)
        norm_forward(conv_in, H, 32, narrow(b, 4), narrow(b, 5), act_h.at[1], unit_h.at[b, 1], slope_h.at[b, 1], spread_h.at[b, 1])
        act_g[b, 1] = dot(act_h[1], perm_h[...]).astype(BF16)
        result = (x_one[...] + dot(act_g[b, 1], weight_out(b))) + wide(b, 2)
        if b == 0:
            x_one[...] = result
        else:
            out[...] = result.astype(BF16)

    grads[:, :, VEC_AT : VEC_AT + 128] = jnp.zeros((OWNERS, ROWS, 128), BF16)
    upstream = cotangent
    rows_w, rows_n = [None] * 6, [None] * 12
    for b in (1, 0):
        if b == 1:
            e3 = cotangent[...]
            rows_w[3 * b + 2] = jnp.sum(cotangent[...].astype(F32), axis=0, keepdims=True)
        else:
            e3 = wide_grad[...].astype(BF16)
        grads[:, :, WO_AT[b] : WO_AT[b] + D] = dot_tn(act_g[b, 1], e3).astype(BF16).reshape(OWNERS, ROWS, D)
        grads[:, :, WO_AT[b] + D : WO_AT[b] + PIECE] = jnp.zeros((OWNERS, ROWS, PIECE - D), BF16)
        back = dot_nt(e3, weight_out(b)).astype(BF16)
        spare[...] = dot_nt(back, perm_h[...])

        def keep_low(rows, dx):
            act_h[0, rows, :] = dx.astype(BF16)

        sums = norm_backward(spare, H, 32, narrow(b, 4), unit_h.at[b, 1], slope_h.at[b, 1], spread_h.at[b, 1], keep_low)
        rows_n[6 * b + 4], rows_n[6 * b + 5], rows_n[6 * b + 3] = sums
        low_at, high_at = (1920, 3200) if b == 1 else (0, 2048)
        span = high_at - low_at
        e_all[:, :span] = jnp.zeros((TOK, span), BF16)
        for at, offset in taps(b):
            moved = dot(mover(-offset), act_h[0])
            moved = jnp.concatenate([moved, jnp.zeros((TOK, 512 - H), F32)], axis=1)
            if at % 128:
                moved = pltpu.roll(moved, at % 128, 1)
            low = window(at) - low_at
            e_all[:, low : low + 512] += moved.astype(BF16)
        piece = dot_tn(act_g[b, 0], e_all[:, :span]).astype(BF16).reshape(OWNERS, ROWS, span)
        low, high = CONV_AT + low_at, CONV_AT + high_at
        if b == 1:
            grads[:, :, low:high] = piece
        else:
            grads[:, :, low : high - 128] = piece[:, :, : span - 128]
            grads[:, :, high - 128 : high] += piece[:, :, span - 128 :]
        back = dot_nt(e_all[:, :span], full[:, :, low:high].reshape(GROUPED, span)).astype(BF16)
        spare[...] = dot_nt(back, perm_h[...])
        sums = norm_backward(spare, H, 32, narrow(b, 1), unit_h.at[b, 0], slope_h.at[b, 0], spread_h.at[b, 0], keep_low)
        rows_n[6 * b + 1], rows_n[6 * b + 2], rows_n[6 * b + 0] = sums
        tall[:, :] = dot_tn(act_d[b], act_h[0])
        for i in range(OWNERS):
            for h in range(2):
                at = SHARD * (2 * i + h)
                low = WI_AT[b][h]
                grads[i, 0:SHARD, low : low + H] = tall[at : at + SHARD, :].astype(BF16)
                grads[i, SHARD:ROWS, low : low + H] = jnp.zeros((ROWS - SHARD, H), BF16)
                grads[i, :, low + H : low + 512] = jnp.zeros((ROWS, 512 - H), BF16)
        wide_back = dot_nt(act_h[0], w_in[b].astype(BF16))
        x_one[...] = wide_back

        def add_up(rows, dx, b=b):
            if b == 1:
                wide_grad[rows, :] = cotangent[rows, :].astype(F32) + dx
            else:
                grad_tokens[rows, :] = wide_grad[rows, :] + dx

        sums = norm_backward(x_one, D, 16, wide(b, 0), unit_d.at[b], slope_d.at[b], spread_d.at[b], add_up)
        rows_w[3 * b + 0], rows_w[3 * b + 1] = sums[0], sums[1]
        if b == 1:
            rows_w[2] = jnp.sum(wide_grad[...], axis=0, keepdims=True)
    for m in range(12):
        vec_n[m : m + 1, :] = rows_n[m]
    for m in range(6):
        vec_w[m : m + 1, :] = rows_w[m]
    low_n, low_w = vec_n[...].astype(BF16), vec_w[...].astype(BF16)
    lanes = slice(VEC_AT, VEC_AT + 128)
    for i in range(OWNERS):
        grads[i, 0:16, lanes] = dot_nt(low_n, put_n[i]).astype(BF16)
        for h in range(2):
            grads[i, 16 + 16 * h : 32 + 16 * h, lanes] = dot_nt(low_w, put_w[2 * i + h]).astype(BF16)

    @pl.when(lax.axis_index("dp") == 0)
    def _():
        slab = grads.at[own]

        def add(rows, lanes, value):
            slab[rows, lanes] = (slab[rows, lanes].astype(F32) + MOMENT_DECAY * value).astype(BF16)

        full_rows = slice(0, SHARD)
        add(full_rows, slice(CONV_AT, CONV_AT + 3200), mom_conv[...])
        for b in range(2):
            add(full_rows, slice(WO_AT[b], WO_AT[b] + D), mom_out[b])
            for h in range(2):
                at = WI_AT[b][h]
                add(full_rows, slice(at, at + H), mom_in[b, h * SHARD : (h + 1) * SHARD, :])
            for k in range(6):
                m = 6 * b + k
                add(slice(m, m + 1), slice(VEC_AT, VEC_AT + SHARD), mom_narrow[b, k : k + 1, :])
            for k in range(3):
                for h in range(2):
                    m = 16 + 16 * h + 3 * b + k
                    part = mom_wide[b, k : k + 1, h * SHARD : (h + 1) * SHARD]
                    add(slice(m, m + 1), slice(VEC_AT, VEC_AT + SHARD), part)


def compute(dilation, lengths, tokens, cotangent, full, moments):
    in_vmem = pl.BlockSpec(memory_space=pltpu.VMEM)
    in_smem = pl.BlockSpec(memory_space=pltpu.SMEM)
    return pl.pallas_call(
        compute_kernel,
        out_shape=(
            jax.ShapeDtypeStruct((TOK, D), BF16),
            jax.ShapeDtypeStruct((TOK, D), F32),
            jax.ShapeDtypeStruct((OWNERS, ROWS, COLS), BF16),
        ),
        in_specs=[in_smem] * 2 + [in_vmem] * 8,
        out_specs=(in_vmem,) * 3,
        scratch_shapes=[
            vmem((TOK, TOK), jnp.int32),
            vmem((H, GROUPED), BF16),
            vmem((16, D), F32),
            vmem((16, H), F32),
            vmem((2, D, H), F32),
            vmem((TOK, D), F32),
            vmem((TOK, D), F32),
            vmem((D, H), F32),
            vmem((2, TOK, D), BF16),
            vmem((2, TOK, H), BF16),
            vmem((2, 2, TOK, GROUPED), BF16),
            vmem((TOK, H), F32),
            vmem((TOK, 512), F32),
            vmem((TOK, H), F32),
            vmem((TOK, 2048), BF16),
            vmem((2, TOK, D), F32),
            vmem((2, TOK, D), F32),
            vmem((2, TOK, 128), F32),
            vmem((2, 2, TOK, H), F32),
            vmem((2, 2, TOK, H), F32),
            vmem((2, 2, TOK, 128), F32),
        ],
        compiler_params=pltpu.CompilerParams(vmem_limit_bytes=58 << 20),
        name="blocks",
    )(dilation, lengths, tokens, cotangent, full, *moments)


MATRICES = (
    dict(kind="out", pieces=(0,), piece=0, own=2, lanes=(0, D), scale=math.sqrt(D / H)),
    dict(kind="out", pieces=(1,), piece=1, own=1, lanes=(0, D), scale=math.sqrt(D / H)),
    dict(kind="conv", pieces=(2, 3, 4), piece=3, own=1, lanes=(0, 2000), scale=1.0),
    dict(kind="conv", pieces=(4, 5), piece=4, own=2, lanes=(208, 1408), scale=1.0),
    dict(kind="in", pieces=(5, 6), piece=6, own=2, lanes=(512, 1536), scale=1.0),
    dict(kind="in", pieces=(6, 7), piece=7, own=1, lanes=(640, 1664), scale=1.0),
)
WINDOW = 3 * PIECE
ROUTES = tuple((k, s, q) for k, m in enumerate(MATRICES) for s, q in enumerate(m["pieces"]))


def is_at(piece, own, matrix):
    return (piece == matrix["piece"]) & (own == matrix["own"])


def not_at(piece, own, matrix):
    return (piece != matrix["piece"]) | (own != matrix["own"])


def window_lanes(s):
    return pl.ds(s * PIECE, PIECE)


def greet_owners(barrier, base, piece, own):
    for k, s, q in ROUTES:
        matrix = MATRICES[k]
        there = (base + matrix["piece"], matrix["own"])

        @pl.when((piece == q) & not_at(piece, own, matrix))
        def _(there=there):
            pl.semaphore_signal(barrier, inc=1, device_id=there, device_id_type=MESH)

    for k, s, q in ROUTES:
        matrix = MATRICES[k]

        @pl.when(is_at(piece, own, matrix))
        def _(matrix=matrix, q=q):
            for i in range(OWNERS):
                if q != matrix["piece"] or i != matrix["own"]:
                    pl.semaphore_signal(barrier, inc=1, device_id=(base + q, i), device_id_type=MESH)


def owner_greetings(piece, own):
    count = jnp.int32(0)
    for k, s, q in ROUTES:
        matrix = MATRICES[k]
        holds = (piece == q) & not_at(piece, own, matrix)
        count = count + jnp.where(holds, 1, 0)
        count = count + jnp.where(is_at(piece, own, matrix), OWNERS - (1 if q == matrix["piece"] else 0), 0)
    return count


def reduce_kernel(
    extra, grads, moment, matrix_window,
    from_core, sums, from_x, from_y, last_x, last_y, from_z, from_far,
    core_send, core_recv, plane_send, plane_recv, z_send, z_recv, far_send, far_recv,
    gather_send, gather_recv, own_send, own_recv,
):
    base, piece, own = place()
    me = base + piece
    core, near_x, near_y = [(base + flip(piece, bit), own) for bit in (1, 2, 4)]
    column = [(me, other_owner(own, step)) for step in (1, 2, 3)]
    far = [(flip(me, bit), own) for bit in extra]
    barrier = greet([core, near_x, near_y] + column + far)
    greet_owners(barrier, base, piece, own)
    pl.semaphore_wait(barrier, 6 + len(extra) + owner_greetings(piece, own))

    parity = piece % 2
    at = piece // 2
    at_x, at_y, at_xy = flip(at, 1), flip(at, 2), 3 - at
    order = (at_xy, at_x, at_y, at)
    started = []

    def send(src, dst, sems, k, device):
        copy = remote(src, dst, sems[0].at[k], sems[1].at[k], device)
        copy.start()
        started.append(copy)
        return copy

    crossing = []
    for k, m in enumerate(order):
        theirs = grads.at[:, :, columns(2 * m + 1 - parity)]
        crossing.append(send(theirs, from_core.at[k], (core_send, core_recv), k, core))

    def merge(k, m):
        crossing[k].wait_recv()
        mine = grads[:, :, columns(2 * m + parity)].astype(F32)
        sums[k] = (mine + from_core[k].astype(F32)).astype(BF16)

    plane = (plane_send, plane_recv)
    low, high = pl.ds(0, 2), pl.ds(2, 2)
    merge(0, at_xy)
    one_x = send(sums.at[0, low], from_x.at[0], plane, 0, near_x)
    one_y = send(sums.at[0, high], from_y.at[0], plane, 1, near_y)
    merge(1, at_x)
    two_x = send(sums.at[1, low], from_x.at[1], plane, 2, near_x)
    merge(2, at_y)
    two_y = send(sums.at[2, high], from_y.at[1], plane, 3, near_y)
    merge(3, at)
    one_x.wait_recv()
    sums[2, 0:2] = (sums[2, 0:2].astype(F32) + from_x[0].astype(F32)).astype(BF16)
    three_y = send(sums.at[2, low], last_y, plane, 4, near_y)
    one_y.wait_recv()
    sums[1, 2:4] = (sums[1, 2:4].astype(F32) + from_y[0].astype(F32)).astype(BF16)
    three_x = send(sums.at[1, high], last_x, plane, 5, near_x)
    two_x.wait_recv()
    two_y.wait_recv()
    three_y.wait_recv()
    three_x.wait_recv()
    low_sum = sums[3, 0:2].astype(F32) + from_x[1].astype(F32) + last_y[...].astype(F32)
    high_sum = sums[3, 2:4].astype(F32) + from_y[1].astype(F32) + last_x[...].astype(F32)
    sums[3, 0:2] = low_sum.astype(BF16)
    sums[3, 2:4] = high_sum.astype(BF16)
    for k, device in enumerate(far):
        copy = remote(sums.at[3], from_far.at[k], far_send.at[k], far_recv.at[k], device)
        copy.start()
        copy.wait()
        sums[3] = (sums[3].astype(F32) + from_far[k].astype(F32)).astype(BF16)
    crossing = []
    for step in (1, 2, 3):
        there = other_owner(own, step)
        crossing.append(
            send(sums.at[3, there], from_z.at[step - 1], (z_send, z_recv), step - 1, column[step - 1])
        )
    total = sums[3, own].astype(F32)
    for step in (1, 2, 3):
        crossing[step - 1].wait_recv()
        total = total + from_z[step - 1].astype(F32)
    moment[:, columns(piece)] = total.astype(BF16)

    def view(q, part):
        return moment.at[part_rows(part), columns(q)]

    gather = Gather(view, gather_send, gather_recv, 0)
    gather.first()

    def to_owner(k, s, q):
        matrix = MATRICES[k]
        there = (base + matrix["piece"], matrix["own"])
        src = moment.at[:, columns(piece)]
        dst = matrix_window.at[own, :, window_lanes(s)]
        return remote(src, dst, own_send.at[k], own_recv.at[OWNERS * s + own], there)

    for k, s, q in ROUTES:
        matrix = MATRICES[k]

        @pl.when((piece == q) & not_at(piece, own, matrix))
        def _(k=k, s=s, q=q):
            to_owner(k, s, q).start()

        @pl.when((piece == q) & is_at(piece, own, matrix))
        def _(s=s):
            matrix_window[own, :, window_lanes(s)] = moment[:, columns(piece)]

    gather.second()
    gather.third()
    gather.last()
    for k, s, q in ROUTES:
        matrix = MATRICES[k]

        @pl.when((piece == q) & not_at(piece, own, matrix))
        def _(k=k, s=s, q=q):
            to_owner(k, s, q).wait_send()

        @pl.when(is_at(piece, own, matrix))
        def _(matrix=matrix, s=s, q=q):
            for i in range(OWNERS):
                if q != matrix["piece"] or i != matrix["own"]:
                    dst = matrix_window.at[i, :, window_lanes(s)]
                    src = moment.at[:, columns(piece)]
                    sems = (own_send.at[0], own_recv.at[OWNERS * s + i])
                    remote(src, dst, sems[0], sems[1], (base + q, i)).wait_recv()

    gather.finish()
    for copy in started:
        copy.wait_send()


def reduce_grads(grads, extra):
    in_vmem = pl.BlockSpec(memory_space=pltpu.VMEM)

    def dma(n):
        return pltpu.SemaphoreType.DMA((max(n, 1),))

    part = (OWNERS, ROWS, PIECE)
    half = (2, ROWS, PIECE)
    return pl.pallas_call(
        functools.partial(reduce_kernel, extra),
        out_shape=(
            jax.ShapeDtypeStruct((ROWS, COLS), BF16),
            jax.ShapeDtypeStruct((OWNERS, ROWS, WINDOW), BF16),
        ),
        in_specs=[in_vmem],
        out_specs=(in_vmem,) * 2,
        scratch_shapes=[
            vmem((4,) + part, BF16),
            vmem((4,) + part, BF16),
            vmem((2,) + half, BF16),
            vmem((2,) + half, BF16),
            vmem(half, BF16),
            vmem(half, BF16),
            vmem((3, ROWS, PIECE), BF16),
            vmem((max(len(extra), 1),) + part, BF16),
            dma(4), dma(4), dma(6), dma(6), dma(3), dma(3), dma(len(extra)), dma(len(extra)),
            dma(Gather.SEMS), dma(Gather.SEMS), dma(6), dma(12),
        ],
        compiler_params=pltpu.CompilerParams(
            collective_id=1, has_side_effects=True, vmem_limit_bytes=48 << 20
        ),
        name="reduce_grads",
    )(grads)


def split(a):
    high = a.astype(BF16)
    return high, (a - high.astype(F32)).astype(BF16)


def dot_fine(a, b):
    a_high, a_low = split(a)
    b_high, b_low = split(b)
    return dot(a_high, b_high) + (dot(a_high, b_low) + dot(a_low, b_high))


def dot_low(a, b):
    return dot(a.astype(BF16), b.astype(BF16))


def polynomial_of(gram, size):
    eye = iota((size, size), 0) == iota((size, size), 1)
    unit = jnp.where(eye, 1.0, 0.0)
    power = jnp.sum(jnp.sum(jnp.where(eye, gram, 0.0), axis=1, keepdims=True), axis=0, keepdims=True)
    inverse = 1.0 / (jnp.sqrt(power) + NORM_FLOOR)
    current = gram * inverse * inverse
    result = None
    for step in range(NS_STEPS):
        square = dot_fine if step > 2 else dot_low
        poly = COEF_A * unit + COEF_B * current + COEF_C * square(current, current)
        result = poly if result is None else dot_low(poly, result)
        if step < NS_STEPS - 1:
            first = dot_fine if step < 2 else dot_low
            second = dot_fine if step < 1 else dot_low
            current = second(first(poly, current), poly)
    return result, inverse


def ortho_kernel(window, update):
    piece, own = lax.axis_index("dp") % PIECES, lax.axis_index("fsdp")
    for matrix in MATRICES:

        @pl.when(is_at(piece, own, matrix))
        def _(matrix=matrix):
            low, high = matrix["lanes"]
            factor = MATRIX_RATE * matrix["scale"]
            if matrix["kind"] == "in":
                halves = [
                    window[:, :, low + 512 * h : low + 512 * (h + 1)].reshape(GROUPED, 512) for h in range(2)
                ]
                gram = dot_tn(halves[0], halves[0]) + dot_tn(halves[1], halves[1])
                poly, inverse = polynomial_of(gram, 512)
                poly = (poly * (inverse * factor)).astype(BF16)
                update[...] = jnp.zeros(update.shape, BF16)
                for h in range(2):
                    step = dot(halves[h], poly).astype(BF16).reshape(OWNERS, ROWS, 512)
                    update[:, :, low + 512 * h : low + 512 * (h + 1)] = step
            else:
                start = low - low % 128
                stop = -(-high // 128) * 128
                values = window[:, :, start:stop].reshape(GROUPED, stop - start)
                lane = iota((GROUPED, stop - start), 1) + start
                values = jnp.where((lane >= low) & (lane < high), values, jnp.zeros((), BF16))
                poly, inverse = polynomial_of(dot_nt(values, values), GROUPED)
                poly = (poly * (inverse * factor)).astype(BF16)
                step = dot(poly, values).astype(BF16).reshape(OWNERS, ROWS, stop - start)
                update[...] = jnp.zeros(update.shape, BF16)
                update[:, :, start:stop] = step


def orthogonalize(window):
    in_vmem = pl.BlockSpec(memory_space=pltpu.VMEM)
    return pl.pallas_call(
        ortho_kernel,
        out_shape=jax.ShapeDtypeStruct(window.shape, BF16),
        in_specs=[in_vmem],
        out_specs=in_vmem,
        compiler_params=pltpu.CompilerParams(vmem_limit_bytes=48 << 20),
        name="orthogonalize",
    )(window)


def slot_of(k, q):
    return sum(1 for j, s, other in ROUTES if other == q and j < k)


def spread_kernel(window, update, parts, send, recv, gather_send, gather_recv):
    base, piece, own = place()
    barrier = greet([(base + flip(piece, bit), own) for bit in (1, 2, 4)])
    greet_owners(barrier, base, piece, own)
    pl.semaphore_wait(barrier, 3 + owner_greetings(piece, own))

    def outgoing(s, q, slot, i):
        src = window.at[i, :, window_lanes(s)]
        return remote(src, parts.at[slot], send.at[OWNERS * s + i], recv.at[slot], (base + q, i))

    for k, s, q in ROUTES:
        matrix = MATRICES[k]
        slot = slot_of(k, q)

        @pl.when(is_at(piece, own, matrix))
        def _(matrix=matrix, s=s, q=q, slot=slot):
            for i in range(OWNERS):
                if q != matrix["piece"] or i != matrix["own"]:
                    outgoing(s, q, slot, i).start()
                else:
                    parts[slot] = window[i, :, window_lanes(s)]

    for k, s, q in ROUTES:
        matrix = MATRICES[k]
        slot = slot_of(k, q)

        @pl.when((piece == q) & not_at(piece, own, matrix))
        def _(matrix=matrix, slot=slot):
            there = (base + matrix["piece"], matrix["own"])
            remote(window.at[0, :, window_lanes(0)], parts.at[slot], send.at[0], recv.at[slot], there).wait_recv()

    shared = [q for q in range(PIECES) if sum(1 for r in ROUTES if r[2] == q) == 2]
    update[:, columns(piece)] = parts[0]
    for q in shared:

        @pl.when(piece == q)
        def _():
            update[:, columns(piece)] = parts[0] + parts[1]

    def view(q, part):
        return update.at[part_rows(part), columns(q)]

    gather = Gather(view, gather_send, gather_recv, 0)
    gather.first()
    gather.second()
    gather.third()
    gather.last()
    gather.finish()
    for k, s, q in ROUTES:
        matrix = MATRICES[k]

        @pl.when(is_at(piece, own, matrix))
        def _(matrix=matrix, s=s, q=q):
            for i in range(OWNERS):
                if q != matrix["piece"] or i != matrix["own"]:
                    outgoing(s, q, 0, i).wait_send()


def spread_steps(window):
    in_vmem = pl.BlockSpec(memory_space=pltpu.VMEM)

    def dma(n):
        return pltpu.SemaphoreType.DMA((n,))

    return pl.pallas_call(
        spread_kernel,
        out_shape=jax.ShapeDtypeStruct((ROWS, COLS), BF16),
        in_specs=[in_vmem],
        out_specs=in_vmem,
        scratch_shapes=[
            vmem((2, ROWS, PIECE), BF16),
            dma(12), dma(2), dma(Gather.SEMS), dma(Gather.SEMS),
        ],
        compiler_params=pltpu.CompilerParams(
            collective_id=2, has_side_effects=True, vmem_limit_bytes=40 << 20
        ),
        name="spread_steps",
    )(window)


def finish_kernel(
    vector_step, moment, update, conv, w_in, w_out, wide, narrow,
    mom_in, mom_conv, mom_out, mom_wide, mom_narrow,
    new_in, new_conv, new_out, new_wide, new_narrow, low_in, low_conv, low_out,
):
    lanes = slice(CONV_AT, CONV_AT + 3200)
    mom_conv[...] = moment[:SHARD, lanes].astype(F32)
    value = conv[...] - update[:SHARD, lanes].astype(F32)
    new_conv[...] = value
    low_conv[...] = value.astype(BF16)
    for b in range(2):
        lanes = slice(WO_AT[b], WO_AT[b] + D)
        mom_out[b] = moment[:SHARD, lanes].astype(F32)
        value = w_out[b] - update[:SHARD, lanes].astype(F32)
        new_out[b] = value
        low_out[b] = value.astype(BF16)
        for h in range(2):
            lanes = slice(WI_AT[b][h], WI_AT[b][h] + H)
            rows = slice(h * SHARD, (h + 1) * SHARD)
            mom_in[b, rows, :] = moment[:SHARD, lanes].astype(F32)
            value = w_in[b, rows, :] - update[:SHARD, lanes].astype(F32)
            new_in[b, rows, :] = value
            low_in[b, rows, :] = value.astype(BF16)
        lanes = slice(VEC_AT, VEC_AT + SHARD)
        vectors = moment[:, VEC_AT : VEC_AT + 128].astype(F32)
        for k in range(6):
            m = 6 * b + k
            value = vectors[m : m + 1, :SHARD]
            mom_narrow[b, k : k + 1, :] = value
            new_narrow[b, k : k + 1, :] = narrow[b, k : k + 1, :] - vector_step * value
        for k in range(3):
            for h in range(2):
                m = 16 + 16 * h + 3 * b + k
                lanes = slice(h * SHARD, (h + 1) * SHARD)
                value = vectors[m : m + 1, :SHARD]
                mom_wide[b, k : k + 1, lanes] = value
                new_wide[b, k : k + 1, lanes] = wide[b, k : k + 1, lanes] - vector_step * value


def finish(vector_step, moment, update, conv, w_in, w_out, wide, narrow):
    in_vmem = pl.BlockSpec(memory_space=pltpu.VMEM)
    shapes = [w_in.shape, conv.shape, w_out.shape, wide.shape, narrow.shape]
    outs = [jax.ShapeDtypeStruct(s, F32) for s in shapes + shapes]
    outs += [jax.ShapeDtypeStruct(s, BF16) for s in shapes[:3]]
    return pl.pallas_call(
        functools.partial(finish_kernel, vector_step),
        out_shape=tuple(outs),
        in_specs=[in_vmem] * 7,
        out_specs=(in_vmem,) * len(outs),
        compiler_params=pltpu.CompilerParams(vmem_limit_bytes=40 << 20),
        name="finish",
    )(moment, update, conv, w_in, w_out, wide, narrow)


def shards(
    extra, vector_step, tokens, cotangent, lengths, dilation, proj_in, conv_weight, proj_out, vec_wide, vec_narrow,
    mom_in, mom_conv, mom_out, mom_wide, mom_narrow,
):
    full = gather_weights(conv_weight, proj_in, proj_out, vec_wide, vec_narrow)
    moments = (mom_conv, mom_in, mom_out, mom_wide, mom_narrow)
    out, grad_tokens, grads = compute(dilation, lengths, tokens, cotangent, full, moments)
    moment, window = reduce_grads(grads, extra)
    update = spread_steps(orthogonalize(window))
    rest = finish(vector_step, moment, update, conv_weight, proj_in, proj_out, vec_wide, vec_narrow)
    return (out, grad_tokens) + tuple(rest)


def solution(mesh):
    groups, owners = mesh.shape["dp"], mesh.shape["fsdp"]
    assert owners == OWNERS and groups % PIECES == 0
    extra, bit = [], PIECES
    while bit < groups:
        extra.append(bit)
        bit *= 2
    assert bit == groups
    vector_step = VECTOR_RATE / math.sqrt(TOK * groups * owners)
    tok, rep = P(("dp", "fsdp"), None), P()
    mid, first, final = P(None, "fsdp", None), P("fsdp", None), P(None, None, "fsdp")
    params = (mid, first, mid, final, final)
    return jax.shard_map(
        functools.partial(shards, tuple(extra), vector_step),
        mesh=mesh,
        in_specs=(tok, tok, tok, rep) + params + params,
        out_specs=(tok, tok) + params + params + (mid, first, mid),
        check_vma=False,
    )
```

time: 1170 us -> 245 us (0.21); the launches traced: 1150 us -> 240 us
  waiting for transfers between devices: 460 us -> 0 us
  blocking collectives: 249 us -> 0 us
  Pallas kernels: 0 us -> 215 us
  local copies, waits for them, and re-layouts: 223 us -> 24.1 us
  matrix products: 98.6 us -> 0 us
  other arithmetic: 51.9 us -> 0 us
  loops' own time: 41.4 us -> 0 us
  between operations: 23.5 us -> 0.97 us
    unnamed x9 -> x0, waiting for transfers between devices: 427 us -> none
    pallas_call x0 -> x6, Pallas kernels: none -> 215 us  [the longest x1 64 us: reduce_grads(): pl.pallas_call(functools.partial(reduce_kernel, extra), out_shape=(jax.Sh...]
    all_gather x9 -> x0, blocking collectives: 150 us -> none  [the longest x2 50.4 us: fetch_forward(): lax.all_gather(low_out[b], 'fsdp', axis=0, tiled=True)]
    unnamed x1 -> x0, blocking collectives: 98.9 us -> none
    dot_general x48 -> x0, matrix products: 98.6 us -> none  [the longest x10 30.6 us: orthogonalize(): current = COEF_A * current + jnp.dot(polynomial, current, precision=PRECISE)]
    slice x16 -> x0, local copies, waits for them, and re-layouts: 48 us -> none  [the longest x2 17.3 us: block_forward(): narrow_vec[4]]
    another operation x6 -> x0, loops' own time: 41.4 us -> none  [shards(): lax.cond(owner_self == k % owners, orthogonalize, jnp.zeros_like, matrice...]
    unnamed x126 -> x23, local copies, waits for them, and re-layouts: 65 us -> 24.1 us
  transfers between devices with their start and end apart: 6 -> 0, of which waited for: 4 -> 0; matrix products, arithmetic and copies ran while one was open for 17% -> 0% of each run, Pallas kernels for 0% -> 0%
where the time goes in v1:
time: 245 us; the launch traced here: 240 us
  Pallas kernels  215 us (88%)
  local copies, waits for them, and re-layouts  24.1 us (10%)
    pallas_call x1, Pallas kernels, reduce_grads(): pl.pallas_call(functools.partial(reduce_kernel, extra), out_shape=(jax.Sh...  64 us
    pallas_call x1, Pallas kernels, spread_steps(): pl.pallas_call(spread_kernel, out_shape=jax.ShapeDtypeStruct((ROWS, COLS)...  43.6 us
    pallas_call x1, Pallas kernels, compute(): pl.pallas_call(compute_kernel, out_shape=(jax.ShapeDtypeStruct((TOK, D),...  42 us
    pallas_call x1, Pallas kernels, gather_weights(): pl.pallas_call(gather_kernel, out_shape=jax.ShapeDtypeStruct((OWNERS, ROW...  40.9 us
    unnamed x23, local copies, waits for them, and re-layouts  24.1 us
    pallas_call x1, Pallas kernels, orthogonalize(): pl.pallas_call(ortho_kernel, out_shape=jax.ShapeDtypeStruct(window.shape,...  22.4 us

profile of v1, /device:TPU:1, one launch (start us, length us, event | category | flops | bytes accessed | tf_op | source)
XLA Modules:
  0.0 240.4 jit_solution(3511265695516996575)
XLA Ops:
  0.6 0.7 copy.30.wide
  1.3 0.7 copy.31.narrow
  2.0 1.3 copy.35.mom_wide
  3.3 1.3 copy.36.mom_narrow
  4.6 2.0 copy.32.tokens
  6.6 2.0 copy.33.cotangent
  8.6 0.0 copy-start.1
  8.6 0.0 copy-start.2
  8.6 1.3 copy.29.w_out
  9.9 2.0 copy.34.mom_out
  11.9 0.0 copy-done.1
  11.9 0.0 copy-done.2
  11.9 40.9 %gather_weights.1.full = bf16[4,112,7168]{2,1,0:T(8,128)(2,1)S(1)} custom-call(f32[100,3200]{1,0:T(8,128)S(1)} %copy-done.1, f32[2,200,400]{2,1,0:T(8,128)S(1)} %copy-done.2, f32[2,100,800]{2,1,0:T(8,128)S(1)} %copy.29.w_out, f32[2,3,200]{2,1,0:T(4,128)S(1)} %copy.30.wide, f32[2,6,100]{2,1,0:T(8,128)S(1)} %copy.31.narrow), custom_call_target="tpu_custom_call" | custom-call | tf_op jit(solution)/shard_map/gather_weights/pallas_call | solution.py:222
  52.9 0.0 copy-start
  52.9 2.7 %copy-done = bf16[4,112,7168]{2,1,0:T(8,128)(2,1)} copy-done((bf16[4,112,7168]{2,1,0:T(8,128)(2,1)}, bf16[4,112,7168]{2,1,0:T(8,128)(2,1)S(1)}, u32[]{:S(2)}) %copy-start) | copy-done | bytes 6422552
  55.6 42.0 %blocks.1 = (bf16[256,800]{1,0:T(8,128)(2,1)}, f32[256,800]{1,0:T(8,128)}, bf16[4,112,7168]{2,1,0:T(8,128)(2,1)}) custom-call(s32[2]{0:T(128)} %dilation.1, s32[1,8]{1,0:T(1,128)} %lengths.1, bf16[256,800]{1,0:T(8,128)(2,1)} %copy.32.tokens, bf16[256,800]{1,0:T(8,128)(2,1)} %copy.33.cotangent, bf16[4,112,7168]{2,1,0:T(8,128)(2,1)} %copy-done, ...), custom_call_target="tpu_custom_call" | custom-call | tf_op jit(solution)/shard_map/blocks/pallas_call | solution.py:477
  97.5 1.9 copy.40
  99.5 2.3 copy.41
  101.8 64.0 %reduce_grads.1 = (bf16[112,7168]{1,0:T(8,128)(2,1)S(1)}, bf16[4,112,2688]{2,1,0:T(8,128)(2,1)S(1)}) custom-call(bf16[4,112,7168]{2,1,0:T(8,128)(2,1)} %get-tuple-element.35.grads), custom_call_target="tpu_custom_call" | custom-call | tf_op jit(solution)/shard_map/reduce_grads/pallas_call | solution.py:701
  165.8 22.4 %orthogonalize.1.window = bf16[4,112,2688]{2,1,0:T(8,128)(2,1)S(1)} custom-call(bf16[4,112,2688]{2,1,0:T(8,128)(2,1)S(1)} %get-tuple-element.37.window), custom_call_target="tpu_custom_call" | custom-call | tf_op jit(solution)/shard_map/orthogonalize/pallas_call | solution.py:795
  188.2 43.6 %spread_steps.1.update = bf16[112,7168]{1,0:T(8,128)(2,1)S(1)} custom-call(bf16[4,112,2688]{2,1,0:T(8,128)(2,1)S(1)} %orthogonalize.1.window), custom_call_target="tpu_custom_call" | custom-call | tf_op jit(solution)/shard_map/spread_steps/pallas_call | solution.py:873
  231.8 2.5 %finish.1 = (f32[2,200,400]{2,1,0:T(8,128)}, f32[100,3200]{1,0:T(8,128)}, f32[2,100,800]{2,1,0:T(8,128)S(1)}, f32[2,3,200]{2,1,0:T(4,128)S(1)}, f32[2,6,100]{2,1...) custom-call(bf16[112,7168]{1,0:T(8,128)(2,1)S(1)} %get-tuple-element, ...), custom_call_target="tpu_custom_call" | custom-call | tf_op jit(solution)/shard_map/finish/pallas_call | solution.py:933
  234.3 0.6 copy.43
  234.9 0.6 copy.44
  235.5 0.6 copy.46
  236.1 0.6 copy.47
  236.7 1.0 copy.48
  237.7 1.2 copy.42
  238.9 1.2 copy.45
Async XLA Ops:
  8.6 3.3 %copy-start.1 = (f32[100,3200]{1,0:T(8,128)S(1)}, f32[100,3200]{1,0:T(8,128)}, u32[]{:S(2)}) copy-start(f32[100,3200]{1,0:T(8,128)} %conv.3) | copy-start | bytes 3840004
  8.6 3.3 %copy-start.2 = (f32[2,200,400]{2,1,0:T(8,128)S(1)}, f32[2,200,400]{2,1,0:T(8,128)}, u32[]{:S(2)}) copy-start(f32[2,200,400]{2,1,0:T(8,128)} %w_in.3) | copy-start | bytes 1920004
  52.9 2.7 %copy-start = (bf16[4,112,7168]{2,1,0:T(8,128)(2,1)}, bf16[4,112,7168]{2,1,0:T(8,128)(2,1)S(1)}, u32[]{:S(2)}) copy-start(bf16[4,112,7168]{2,1,0:T(8,128)(2,1)S(1)} %gather_weights.1.full) | copy-start | bytes 19267588

commit v2 on v1

--- a/solution.py
+++ b/solution.py
@@ -68,18 +68,18 @@
     slab[...] = jnp.zeros((ROWS, COLS), BF16)
     slab[:SHARD, CONV_AT : CONV_AT + 3200] = conv[...].astype(BF16)
     for b in range(2):
-        slab[:SHARD, WO_AT[b] : WO_AT[b] + D] = w_out[b].astype(BF16)
+        slab[:SHARD, WO_AT[b] : WO_AT[b] + D] = w_out[:, b, :].astype(BF16)
         for h in range(2):
             at = WI_AT[b][h]
             slab[:SHARD, at : at + H] = w_in[b, h * SHARD : (h + 1) * SHARD, :].astype(BF16)
     for b in range(2):
         for k in range(6):
             m = 6 * b + k
-            slab[m : m + 1, VEC_AT : VEC_AT + SHARD] = narrow[b, k : k + 1, :].astype(BF16)
+            slab[m : m + 1, VEC_AT : VEC_AT + SHARD] = narrow[k, b : b + 1, :].astype(BF16)
         for k in range(3):
             for h in range(2):
                 m = 16 + 16 * h + 3 * b + k
-                part = wide[b, k : k + 1, h * SHARD : (h + 1) * SHARD]
+                part = wide[k, b : b + 1, h * SHARD : (h + 1) * SHARD]
                 slab[m : m + 1, VEC_AT : VEC_AT + SHARD] = part.astype(BF16)
 
 
@@ -349,12 +349,11 @@
     def window(at):
         return at - at % 128
 
-    x_one[...] = tokens[...].astype(F32)
+    x_one[...] = tokens[...].astype(F32).T
     for b in range(2):
-        src = tokens if b == 0 else x_one
-        norm_forward(src, D, 16, wide(b, 0), wide(b, 1), act_d.at[b], unit_d.at[b], slope_d.at[b], spread_d.at[b])
+        norm_forward(x_one, D, 128, wide(b, 0), wide(b, 1), act_d.at[b], unit_d.at[b], slope_d.at[b], spread_d.at[b])
         hid[:, :] = dot(act_d[b], w_in[b].astype(BF16)) + narrow(b, 0)
-        norm_forward(hid, H, 32, narrow(b, 1), narrow(b, 2), act_h.at[0], unit_h.at[b, 0], slope_h.at[b, 0], spread_h.at[b, 0])
+        norm_forward(hid, H, 128, narrow(b, 1), narrow(b, 2), act_h.at[0], unit_h.at[b, 0], slope_h.at[b, 0], spread_h.at[b, 0])
         act_g[b, 0] = dot(act_h[0], perm_h[...]).astype(BF16)
         for j, (at, offset) in enumerate(taps(b)):
             moved = dot(mover(offset), act_g[b, 0]).astype(BF16)
@@ -367,23 +366,21 @@
             else:
                 conv_in[...] += product
         conv_in[:, :H] += narrow(b, 3)
-        norm_forward(conv_in, H, 32, narrow(b, 4), narrow(b, 5), act_h.at[1], unit_h.at[b, 1], slope_h.at[b, 1], spread_h.at[b, 1])
+        norm_forward(conv_in, H, 128, narrow(b, 4), narrow(b, 5), act_h.at[1], unit_h.at[b, 1], slope_h.at[b, 1], spread_h.at[b, 1])
         act_g[b, 1] = dot(act_h[1], perm_h[...]).astype(BF16)
         result = (x_one[...] + dot(act_g[b, 1], weight_out(b))) + wide(b, 2)
         if b == 0:
             x_one[...] = result
         else:
-            out[...] = result.astype(BF16)
+            out[...] = result.T.astype(BF16)
 
     grads[:, :, VEC_AT : VEC_AT + 128] = jnp.zeros((OWNERS, ROWS, 128), BF16)
-    upstream = cotangent
     rows_w, rows_n = [None] * 6, [None] * 12
     for b in (1, 0):
         if b == 1:
-            e3 = cotangent[...]
-            rows_w[3 * b + 2] = jnp.sum(cotangent[...].astype(F32), axis=0, keepdims=True)
-        else:
-            e3 = wide_grad[...].astype(BF16)
+            wide_grad[...] = cotangent[...].astype(F32).T
+        rows_w[3 * b + 2] = jnp.sum(wide_grad[...], axis=0, keepdims=True)
+        e3 = wide_grad[...].astype(BF16)
         grads[:, :, WO_AT[b] : WO_AT[b] + D] = dot_tn(act_g[b, 1], e3).astype(BF16).reshape(OWNERS, ROWS, D)
         grads[:, :, WO_AT[b] + D : WO_AT[b] + PIECE] = jnp.zeros((OWNERS, ROWS, PIECE - D), BF16)
         back = dot_nt(e3, weight_out(b)).astype(BF16)
@@ -392,7 +389,7 @@
         def keep_low(rows, dx):
             act_h[0, rows, :] = dx.astype(BF16)
 
-        sums = norm_backward(spare, H, 32, narrow(b, 4), unit_h.at[b, 1], slope_h.at[b, 1], spread_h.at[b, 1], keep_low)
+        sums = norm_backward(spare, H, 128, narrow(b, 4), unit_h.at[b, 1], slope_h.at[b, 1], spread_h.at[b, 1], keep_low)
         rows_n[6 * b + 4], rows_n[6 * b + 5], rows_n[6 * b + 3] = sums
         low_at, high_at = (1920, 3200) if b == 1 else (0, 2048)
         span = high_at - low_at
@@ -413,7 +410,7 @@
             grads[:, :, high - 128 : high] += piece[:, :, span - 128 :]
         back = dot_nt(e_all[:, :span], full[:, :, low:high].reshape(GROUPED, span)).astype(BF16)
         spare[...] = dot_nt(back, perm_h[...])
-        sums = norm_backward(spare, H, 32, narrow(b, 1), unit_h.at[b, 0], slope_h.at[b, 0], spread_h.at[b, 0], keep_low)
+        sums = norm_backward(spare, H, 128, narrow(b, 1), unit_h.at[b, 0], slope_h.at[b, 0], spread_h.at[b, 0], keep_low)
         rows_n[6 * b + 1], rows_n[6 * b + 2], rows_n[6 * b + 0] = sums
         tall[:, :] = dot_tn(act_d[b], act_h[0])
         for i in range(OWNERS):
@@ -426,16 +423,12 @@
         wide_back = dot_nt(act_h[0], w_in[b].astype(BF16))
         x_one[...] = wide_back
 
-        def add_up(rows, dx, b=b):
-            if b == 1:
-                wide_grad[rows, :] = cotangent[rows, :].astype(F32) + dx
-            else:
-                grad_tokens[rows, :] = wide_grad[rows, :] + dx
-
-        sums = norm_backward(x_one, D, 16, wide(b, 0), unit_d.at[b], slope_d.at[b], spread_d.at[b], add_up)
+        def add_up(rows, dx):
+            wide_grad[rows, :] += dx
+
+        sums = norm_backward(x_one, D, 128, wide(b, 0), unit_d.at[b], slope_d.at[b], spread_d.at[b], add_up)
         rows_w[3 * b + 0], rows_w[3 * b + 1] = sums[0], sums[1]
-        if b == 1:
-            rows_w[2] = jnp.sum(wide_grad[...], axis=0, keepdims=True)
+    grad_tokens[...] = wide_grad[...].T
     for m in range(12):
         vec_n[m : m + 1, :] = rows_n[m]
     for m in range(6):
@@ -457,17 +450,17 @@
         full_rows = slice(0, SHARD)
         add(full_rows, slice(CONV_AT, CONV_AT + 3200), mom_conv[...])
         for b in range(2):
-            add(full_rows, slice(WO_AT[b], WO_AT[b] + D), mom_out[b])
+            add(full_rows, slice(WO_AT[b], WO_AT[b] + D), mom_out[:, b, :])
             for h in range(2):
                 at = WI_AT[b][h]
                 add(full_rows, slice(at, at + H), mom_in[b, h * SHARD : (h + 1) * SHARD, :])
             for k in range(6):
                 m = 6 * b + k
-                add(slice(m, m + 1), slice(VEC_AT, VEC_AT + SHARD), mom_narrow[b, k : k + 1, :])
+                add(slice(m, m + 1), slice(VEC_AT, VEC_AT + SHARD), mom_narrow[k, b : b + 1, :])
             for k in range(3):
                 for h in range(2):
                     m = 16 + 16 * h + 3 * b + k
-                    part = mom_wide[b, k : k + 1, h * SHARD : (h + 1) * SHARD]
+                    part = mom_wide[k, b : b + 1, h * SHARD : (h + 1) * SHARD]
                     add(slice(m, m + 1), slice(VEC_AT, VEC_AT + SHARD), part)
 
 
@@ -477,8 +470,8 @@
     return pl.pallas_call(
         compute_kernel,
         out_shape=(
-            jax.ShapeDtypeStruct((TOK, D), BF16),
-            jax.ShapeDtypeStruct((TOK, D), F32),
+            jax.ShapeDtypeStruct((D, TOK), BF16),
+            jax.ShapeDtypeStruct((D, TOK), F32),
             jax.ShapeDtypeStruct((OWNERS, ROWS, COLS), BF16),
         ),
         in_specs=[in_smem] * 2 + [in_vmem] * 8,
@@ -740,7 +733,8 @@
     return dot(a.astype(BF16), b.astype(BF16))
 
 
-def polynomial_of(gram, size):
+def polynomial_of(gram):
+    size = gram.shape[0]
     eye = iota((size, size), 0) == iota((size, size), 1)
     unit = jnp.where(eye, 1.0, 0.0)
     power = jnp.sum(jnp.sum(jnp.where(eye, gram, 0.0), axis=1, keepdims=True), axis=0, keepdims=True)
@@ -758,36 +752,77 @@
     return result, inverse
 
 
-def ortho_kernel(window, update):
+def ortho_kernel(window, update, gram, poly):
     piece, own = lax.axis_index("dp") % PIECES, lax.axis_index("fsdp")
+    owner = {"out": False, "conv": False, "in": False}
+    low, high, factor = jnp.int32(0), jnp.int32(0), jnp.float32(0)
     for matrix in MATRICES:
-
-        @pl.when(is_at(piece, own, matrix))
-        def _(matrix=matrix):
-            low, high = matrix["lanes"]
-            factor = MATRIX_RATE * matrix["scale"]
-            if matrix["kind"] == "in":
-                halves = [
-                    window[:, :, low + 512 * h : low + 512 * (h + 1)].reshape(GROUPED, 512) for h in range(2)
-                ]
-                gram = dot_tn(halves[0], halves[0]) + dot_tn(halves[1], halves[1])
-                poly, inverse = polynomial_of(gram, 512)
-                poly = (poly * (inverse * factor)).astype(BF16)
-                update[...] = jnp.zeros(update.shape, BF16)
-                for h in range(2):
-                    step = dot(halves[h], poly).astype(BF16).reshape(OWNERS, ROWS, 512)
-                    update[:, :, low + 512 * h : low + 512 * (h + 1)] = step
-            else:
-                start = low - low % 128
-                stop = -(-high // 128) * 128
-                values = window[:, :, start:stop].reshape(GROUPED, stop - start)
-                lane = iota((GROUPED, stop - start), 1) + start
-                values = jnp.where((lane >= low) & (lane < high), values, jnp.zeros((), BF16))
-                poly, inverse = polynomial_of(dot_nt(values, values), GROUPED)
-                poly = (poly * (inverse * factor)).astype(BF16)
-                step = dot(poly, values).astype(BF16).reshape(OWNERS, ROWS, stop - start)
-                update[...] = jnp.zeros(update.shape, BF16)
-                update[:, :, start:stop] = step
+        here = is_at(piece, own, matrix)
+        owner[matrix["kind"]] = owner[matrix["kind"]] | here
+        low = jnp.where(here, matrix["lanes"][0], low)
+        high = jnp.where(here, matrix["lanes"][1], high)
+        factor = jnp.where(here, MATRIX_RATE * matrix["scale"], factor)
+
+    def half(h):
+        return pl.ds(pl.multiple_of(low + 512 * h, 128), 512)
+
+    def conv_part(k, width):
+        lanes = pl.ds(pl.multiple_of(k * width, width), width)
+        values = window[:, :, lanes].reshape(GROUPED, width)
+        lane = iota((GROUPED, width), 1) + k * width
+        return lanes, jnp.where((lane >= low) & (lane < high), values, jnp.zeros((), BF16))
+
+    @pl.when(owner["in"])
+    def _():
+        a = window[:, :, half(0)].reshape(GROUPED, 512)
+        b = window[:, :, half(1)].reshape(GROUPED, 512)
+        gram[...] = dot_tn(a, a) + dot_tn(b, b)
+
+    @pl.when(owner["out"])
+    def _():
+        gram[...] = jnp.zeros(gram.shape, F32)
+        a = window[:, :, :PIECE].reshape(GROUPED, PIECE)
+        gram[:GROUPED, :GROUPED] = dot_nt(a, a)
+
+    @pl.when(owner["conv"])
+    def _():
+        gram[...] = jnp.zeros(gram.shape, F32)
+
+        def body(k, carry):
+            values = conv_part(k, 512)[1]
+            gram[:GROUPED, :GROUPED] += dot_nt(values, values)
+            return carry
+
+        lax.fori_loop(0, 4, body, 0)
+
+    @pl.when(owner["in"] | owner["out"] | owner["conv"])
+    def _():
+        result, inverse = polynomial_of(gram[...])
+        poly[...] = (result * (inverse * factor)).astype(BF16)
+
+    @pl.when(owner["in"])
+    def _():
+        update[...] = jnp.zeros(update.shape, BF16)
+        for h in range(2):
+            step = dot(window[:, :, half(h)].reshape(GROUPED, 512), poly[...])
+            update[:, :, half(h)] = step.astype(BF16).reshape(OWNERS, ROWS, 512)
+
+    @pl.when(owner["out"])
+    def _():
+        step = dot(poly[:GROUPED, :GROUPED], window[:, :, :PIECE].reshape(GROUPED, PIECE))
+        update[:, :, :PIECE] = step.astype(BF16).reshape(OWNERS, ROWS, PIECE)
+
+    @pl.when(owner["conv"])
+    def _():
+        update[:, :, 2048:] = jnp.zeros((OWNERS, ROWS, WINDOW - 2048), BF16)
+
+        def body(k, carry):
+            lanes, values = conv_part(k, 512)
+            step = dot(poly[:GROUPED, :GROUPED], values)
+            update[:, :, lanes] = step.astype(BF16).reshape(OWNERS, ROWS, 512)
+            return carry
+
+        lax.fori_loop(0, 4, body, 0)
 
 
 def orthogonalize(window):
@@ -797,6 +832,7 @@
         out_shape=jax.ShapeDtypeStruct(window.shape, BF16),
         in_specs=[in_vmem],
         out_specs=in_vmem,
+        scratch_shapes=[vmem((512, 512), F32), vmem((512, 512), BF16)],
         compiler_params=pltpu.CompilerParams(vmem_limit_bytes=48 << 20),
         name="orthogonalize",
     )(window)
@@ -898,9 +934,9 @@
     low_conv[...] = value.astype(BF16)
     for b in range(2):
         lanes = slice(WO_AT[b], WO_AT[b] + D)
-        mom_out[b] = moment[:SHARD, lanes].astype(F32)
-        value = w_out[b] - update[:SHARD, lanes].astype(F32)
-        new_out[b] = value
+        mom_out[:, b, :] = moment[:SHARD, lanes].astype(F32)
+        value = w_out[:, b, :] - update[:SHARD, lanes].astype(F32)
+        new_out[:, b, :] = value
         low_out[b] = value.astype(BF16)
         for h in range(2):
             lanes = slice(WI_AT[b][h], WI_AT[b][h] + H)
@@ -914,22 +950,22 @@
         for k in range(6):
             m = 6 * b + k
             value = vectors[m : m + 1, :SHARD]
-            mom_narrow[b, k : k + 1, :] = value
-            new_narrow[b, k : k + 1, :] = narrow[b, k : k + 1, :] - vector_step * value
+            mom_narrow[k, b : b + 1, :] = value
+            new_narrow[k, b : b + 1, :] = narrow[k, b : b + 1, :] - vector_step * value
         for k in range(3):
             for h in range(2):
                 m = 16 + 16 * h + 3 * b + k
                 lanes = slice(h * SHARD, (h + 1) * SHARD)
                 value = vectors[m : m + 1, :SHARD]
-                mom_wide[b, k : k + 1, lanes] = value
-                new_wide[b, k : k + 1, lanes] = wide[b, k : k + 1, lanes] - vector_step * value
+                mom_wide[k, b : b + 1, lanes] = value
+                new_wide[k, b : b + 1, lanes] = wide[k, b : b + 1, lanes] - vector_step * value
 
 
 def finish(vector_step, moment, update, conv, w_in, w_out, wide, narrow):
     in_vmem = pl.BlockSpec(memory_space=pltpu.VMEM)
     shapes = [w_in.shape, conv.shape, w_out.shape, wide.shape, narrow.shape]
     outs = [jax.ShapeDtypeStruct(s, F32) for s in shapes + shapes]
-    outs += [jax.ShapeDtypeStruct(s, BF16) for s in shapes[:3]]
+    outs += [jax.ShapeDtypeStruct(s, BF16) for s in shapes[:2] + [(2, SHARD, D)]]
     return pl.pallas_call(
         functools.partial(finish_kernel, vector_step),
         out_shape=tuple(outs),
@@ -944,13 +980,20 @@
     extra, vector_step, tokens, cotangent, lengths, dilation, proj_in, conv_weight, proj_out, vec_wide, vec_narrow,
     mom_in, mom_conv, mom_out, mom_wide, mom_narrow,
 ):
+    proj_out, vec_wide, vec_narrow = swap(proj_out), swap(vec_wide), swap(vec_narrow)
+    moments = (mom_conv, mom_in, swap(mom_out), swap(mom_wide), swap(mom_narrow))
     full = gather_weights(conv_weight, proj_in, proj_out, vec_wide, vec_narrow)
-    moments = (mom_conv, mom_in, mom_out, mom_wide, mom_narrow)
-    out, grad_tokens, grads = compute(dilation, lengths, tokens, cotangent, full, moments)
+    out, grad_tokens, grads = compute(dilation, lengths, tokens.T, cotangent.T, full, moments)
     moment, window = reduce_grads(grads, extra)
     update = spread_steps(orthogonalize(window))
-    rest = finish(vector_step, moment, update, conv_weight, proj_in, proj_out, vec_wide, vec_narrow)
-    return (out, grad_tokens) + tuple(rest)
+    rest = list(finish(vector_step, moment, update, conv_weight, proj_in, proj_out, vec_wide, vec_narrow))
+    for k in (2, 3, 4, 7, 8, 9):
+        rest[k] = swap(rest[k])
+    return (out.T, grad_tokens.T) + tuple(rest)
+
+
+def swap(array):
+    return jnp.transpose(array, (1, 0, 2))
 
 
 def solution(mesh):

time: 245 us -> 195 us (0.80); the launches traced: 240 us -> 193 us
  Pallas kernels: 215 us -> 184 us
  local copies, waits for them, and re-layouts: 24.1 us -> 8.69 us
    pallas_call x1, Pallas kernels: 22.4 us -> 0.32 us  [orthogonalize(): pl.pallas_call(ortho_kernel, out_shape=jax.ShapeDtypeStruct(window.shape,...]
    unnamed x23, local copies, waits for them, and re-layouts: 24.1 us -> 8.69 us
    pallas_call x1, Pallas kernels: 42 us -> 28.7 us  [compute(): pl.pallas_call(compute_kernel, out_shape=(jax.ShapeDtypeStruct((D, TOK),...]
    pallas_call x1, Pallas kernels: 43.6 us -> 46.4 us  [spread_steps(): pl.pallas_call(spread_kernel, out_shape=jax.ShapeDtypeStruct((ROWS, COLS)...]
where the time goes in v2:
time: 195 us; the launch traced here: 193 us
  Pallas kernels  184 us (94%)
  local copies, waits for them, and re-layouts  8.69 us (4%)
    pallas_call x1, Pallas kernels, reduce_grads(): pl.pallas_call(functools.partial(reduce_kernel, extra), out_shape=(jax.Sh...  65 us
    pallas_call x1, Pallas kernels, spread_steps(): pl.pallas_call(spread_kernel, out_shape=jax.ShapeDtypeStruct((ROWS, COLS)...  46.4 us
    pallas_call x1, Pallas kernels, gather_weights(): pl.pallas_call(gather_kernel, out_shape=jax.ShapeDtypeStruct((OWNERS, ROW...  40.7 us
    pallas_call x1, Pallas kernels, compute(): pl.pallas_call(compute_kernel, out_shape=(jax.ShapeDtypeStruct((D, TOK),...  28.7 us
    unnamed x23, local copies, waits for them, and re-layouts  8.69 us

profile of v2, /device:TPU:1, one launch (start us, length us, event | category | flops | bytes accessed | tf_op | source)
XLA Modules:
  0.0 193.4 jit_solution(3332675451358717931)
XLA Ops:
  0.6 0.0 copy-start.1
  0.7 1.3 copy-done.1
  2.0 0.0 copy-start.3
  2.0 1.1 copy-done.3
  3.1 0.0 copy-start.5
  3.1 1.1 copy-done.5
  4.2 0.0 copy-start.7
  4.2 0.7 copy-done.7
  4.9 0.0 copy-start.9
  4.9 0.7 copy-done.9
  5.6 40.7 %gather_weights.1.full = bf16[4,112,7168]{2,1,0:T(8,128)(2,1)S(1)} custom-call(f32[100,3200]{1,0:T(8,128)S(1)} %copy-done.1, f32[2,200,400]{2,1,0:T(8,128)S(1)} %copy-done.3, f32[100,2,800]{2,1,0:T(2,128)S(1)} %bitcast.16, f32[3,2,200]{2,1,0:T(2,128)S(1)} %bitcast.18, f32[6,2,100]{2,1,0:T(2,128)S(1)} %bitcast.20), custom_call_target="tpu_custom_call" | custom-call | tf_op jit(solution)/shard_map/gather_weights/pallas_call | solution.py:222
  46.3 0.0 copy-start
  46.3 2.7 %copy-done = bf16[4,112,7168]{2,1,0:T(8,128)(2,1)} copy-done((bf16[4,112,7168]{2,1,0:T(8,128)(2,1)}, bf16[4,112,7168]{2,1,0:T(8,128)(2,1)S(1)}, u32[]{:S(2)}) %copy-start) | copy-done | bytes 6422552
  49.0 28.7 %blocks.1 = (bf16[800,256]{1,0:T(8,128)(2,1)}, f32[800,256]{1,0:T(8,128)}, bf16[4,112,7168]{2,1,0:T(8,128)(2,1)}) custom-call(s32[2]{0:T(128)} %dilation.1, s32[1,8]{1,0:T(1,128)} %lengths.1, bf16[800,256]{1,0:T(8,128)(2,1)} %bitcast.23, bf16[800,256]{1,0:T(8,128)(2,1)} %bitcast.24, bf16[4,112,7168]{2,1,0:T(8,128)(2,1)} %copy-done, f32[100,3200]{1,0:T(8,128)} %mom_conv.1, ...), custom_call_target="tpu_custom_call" | custom-call | tf_op jit(solution)/shard_map/blocks/pallas_call | solution.py:470
  77.7 65.0 %reduce_grads.1 = (bf16[112,7168]{1,0:T(8,128)(2,1)S(1)}, bf16[4,112,2688]{2,1,0:T(8,128)(2,1)S(1)}) custom-call(bf16[4,112,7168]{2,1,0:T(8,128)(2,1)} %get-tuple-element.35.grads), custom_call_target="tpu_custom_call" | custom-call | tf_op jit(solution)/shard_map/reduce_grads/pallas_call | solution.py:694
  142.6 0.3 orthogonalize.1.window
  142.9 0.0 copy-start.2
  143.0 0.0 copy-start.4
  143.0 0.0 copy-start.6
  143.0 0.0 copy-start.8
  143.0 0.0 copy-start.10
  143.0 46.4 %spread_steps.1.update = bf16[112,7168]{1,0:T(8,128)(2,1)S(1)} custom-call(bf16[4,112,2688]{2,1,0:T(8,128)(2,1)S(1)} %orthogonalize.1.window), custom_call_target="tpu_custom_call" | custom-call | tf_op jit(solution)/shard_map/spread_steps/pallas_call | solution.py:909
  189.4 0.0 copy-done.2
  189.4 0.0 copy-done.4
  189.4 0.0 copy-done.6
  189.4 0.0 copy-done.8
  189.4 0.0 copy-done.10
  189.4 2.9 %finish.1 = (f32[2,200,400]{2,1,0:T(8,128)}, f32[100,3200]{1,0:T(8,128)}, f32[100,2,800]{2,1,0:T(2,128)}, f32[3,2,200]{2,1,0:T(2,128)}, f32[6,2,100]{2,1,0:T(2,1...) custom-call(bf16[112,7168]{1,0:T(8,128)(2,1)S(1)} %get-tuple-element, ...), custom_call_target="tpu_custom_call" | custom-call | tf_op jit(solution)/shard_map/finish/pallas_call | solution.py:969
  192.4 1.0 copy.29
Async XLA Ops:
  0.6 1.3 copy-start.1
  2.0 1.1 copy-start.3
  3.1 1.1 copy-start.5
  4.2 0.7 copy-start.7
  4.9 0.7 copy-start.9
  46.3 2.7 %copy-start = (bf16[4,112,7168]{2,1,0:T(8,128)(2,1)}, bf16[4,112,7168]{2,1,0:T(8,128)(2,1)S(1)}, u32[]{:S(2)}) copy-start(bf16[4,112,7168]{2,1,0:T(8,128)(2,1)S(1)} %gather_weights.1.full) | copy-start | bytes 19267588
  142.9 46.5 %copy-start.2 = (f32[100,3200]{1,0:T(8,128)S(1)}, f32[100,3200]{1,0:T(8,128)}, u32[]{:S(2)}) copy-start(f32[100,3200]{1,0:T(8,128)} %conv.3) | copy-start | bytes 3840004
  143.0 46.5 %copy-start.4 = (f32[2,200,400]{2,1,0:T(8,128)S(1)}, f32[2,200,400]{2,1,0:T(8,128)}, u32[]{:S(2)}) copy-start(f32[2,200,400]{2,1,0:T(8,128)} %w_in.3) | copy-start | bytes 1920004
  143.0 46.5 %copy-start.6 = (f32[2,100,800]{2,0,1:T(2,128)S(1)}, f32[2,100,800]{2,0,1:T(2,128)}, u32[]{:S(2)}) copy-start(f32[2,100,800]{2,0,1:T(2,128)} %param.20) | copy-start | bytes 1920004
  143.0 46.5 %copy-start.8 = (f32[2,3,200]{2,0,1:T(2,128)S(1)}, f32[2,3,200]{2,0,1:T(2,128)}, u32[]{:S(2)}) copy-start(f32[2,3,200]{2,0,1:T(2,128)} %param.21) | copy-start | bytes 14404
  143.0 46.5 %copy-start.10 = (f32[2,6,100]{2,0,1:T(2,128)S(1)}, f32[2,6,100]{2,0,1:T(2,128)}, u32[]{:S(2)}) copy-start(f32[2,6,100]{2,0,1:T(2,128)} %param.22) | copy-start | bytes 14404

commit v3 on v2

--- a/solution.py
+++ b/solution.py
@@ -216,27 +216,6 @@
         copy.wait_send()
 
 
-def gather_weights(conv, w_in, w_out, wide, narrow):
-    in_vmem = pl.BlockSpec(memory_space=pltpu.VMEM)
-    count = 3 * Gather.SEMS
-    return pl.pallas_call(
-        gather_kernel,
-        out_shape=jax.ShapeDtypeStruct((OWNERS, ROWS, COLS), BF16),
-        in_specs=[in_vmem] * 5,
-        out_specs=in_vmem,
-        scratch_shapes=[
-            pltpu.SemaphoreType.DMA((3,)),
-            pltpu.SemaphoreType.DMA((3,)),
-            pltpu.SemaphoreType.DMA((count,)),
-            pltpu.SemaphoreType.DMA((count,)),
-        ],
-        compiler_params=pltpu.CompilerParams(
-            collective_id=0, has_side_effects=True, vmem_limit_bytes=40 << 20
-        ),
-        name="gather_weights",
-    )(conv, w_in, w_out, wide, narrow)
-
-
 def norm_forward(src, width, chunk, gain, shift, act, unit, slope, spread):
     def body(k, carry):
         rows = pl.ds(pl.multiple_of(k * chunk, chunk), chunk)
@@ -287,12 +266,16 @@
 
 
 def compute_kernel(
-    dilation, lengths, tokens, cotangent, full, mom_conv, mom_in, mom_out, mom_wide, mom_narrow,
+    dilation, lengths, tokens, cotangent, conv, in_shard, out_shard, wide_shard, narrow_shard,
+    mom_conv, mom_in, mom_out, mom_wide, mom_narrow,
     out, grad_tokens, grads,
-    far, perm_h, vec_w, vec_n, w_in, x_one, wide_grad, tall,
+    full, z_send, z_recv, send, recv, far, perm_h, vec_w, vec_n, w_in, x_one, wide_grad, tall,
     act_d, act_h, act_g, hid, conv_in, spare, e_all,
     unit_d, slope_d, spread_d, unit_h, slope_h, spread_h,
 ):
+    gather_kernel(
+        conv, in_shard, out_shard, wide_shard, narrow_shard, full, z_send, z_recv, send, recv
+    )
     own = lax.axis_index("fsdp")
     row, col = iota((TOK, TOK), 0), iota((TOK, TOK), 1)
     seg_row, seg_col = jnp.zeros((TOK, TOK), jnp.int32), jnp.zeros((TOK, TOK), jnp.int32)
@@ -464,7 +447,7 @@
                     add(slice(m, m + 1), slice(VEC_AT, VEC_AT + SHARD), part)
 
 
-def compute(dilation, lengths, tokens, cotangent, full, moments):
+def compute(dilation, lengths, tokens, cotangent, params, moments):
     in_vmem = pl.BlockSpec(memory_space=pltpu.VMEM)
     in_smem = pl.BlockSpec(memory_space=pltpu.SMEM)
     return pl.pallas_call(
@@ -474,9 +457,14 @@
             jax.ShapeDtypeStruct((D, TOK), F32),
             jax.ShapeDtypeStruct((OWNERS, ROWS, COLS), BF16),
         ),
-        in_specs=[in_smem] * 2 + [in_vmem] * 8,
+        in_specs=[in_smem] * 2 + [in_vmem] * 12,
         out_specs=(in_vmem,) * 3,
         scratch_shapes=[
+            vmem((OWNERS, ROWS, COLS), BF16),
+            pltpu.SemaphoreType.DMA((3,)),
+            pltpu.SemaphoreType.DMA((3,)),
+            pltpu.SemaphoreType.DMA((3 * Gather.SEMS,)),
+            pltpu.SemaphoreType.DMA((3 * Gather.SEMS,)),
             vmem((TOK, TOK), jnp.int32),
             vmem((H, GROUPED), BF16),
             vmem((16, D), F32),
@@ -499,9 +487,11 @@
             vmem((2, 2, TOK, H), F32),
             vmem((2, 2, TOK, 128), F32),
         ],
-        compiler_params=pltpu.CompilerParams(vmem_limit_bytes=58 << 20),
+        compiler_params=pltpu.CompilerParams(
+            collective_id=0, has_side_effects=True, vmem_limit_bytes=58 << 20
+        ),
         name="blocks",
-    )(dilation, lengths, tokens, cotangent, full, *moments)
+    )(dilation, lengths, tokens, cotangent, *params, *moments)
 
 
 MATRICES = (
@@ -982,8 +972,8 @@
 ):
     proj_out, vec_wide, vec_narrow = swap(proj_out), swap(vec_wide), swap(vec_narrow)
     moments = (mom_conv, mom_in, swap(mom_out), swap(mom_wide), swap(mom_narrow))
-    full = gather_weights(conv_weight, proj_in, proj_out, vec_wide, vec_narrow)
-    out, grad_tokens, grads = compute(dilation, lengths, tokens.T, cotangent.T, full, moments)
+    params = (conv_weight, proj_in, proj_out, vec_wide, vec_narrow)
+    out, grad_tokens, grads = compute(dilation, lengths, tokens.T, cotangent.T, params, moments)
     moment, window = reduce_grads(grads, extra)
     update = spread_steps(orthogonalize(window))
     rest = list(finish(vector_step, moment, update, conv_weight, proj_in, proj_out, vec_wide, vec_narrow))

time: 195 us -> 187 us (0.959)
  local copies, waits for them, and re-layouts: 8.69 us -> 2.69 us
  Pallas kernels: 184 us -> 180 us
    pallas_call x1 -> x0, Pallas kernels: 40.7 us -> none  [gather_weights(): pl.pallas_call(gather_kernel, out_shape=jax.ShapeDtypeStruct((OWNERS, ROW...]
    pallas_call x1, Pallas kernels: 28.7 us -> 68.5 us  [compute(): pl.pallas_call(compute_kernel, out_shape=(jax.ShapeDtypeStruct((D, TOK),...]
    unnamed x23 -> x17, local copies, waits for them, and re-layouts: 8.69 us -> 2.69 us
    pallas_call x1, Pallas kernels: 46.4 us -> 43.8 us  [spread_steps(): pl.pallas_call(spread_kernel, out_shape=jax.ShapeDtypeStruct((ROWS, COLS)...]
where the time goes in v3:
time: 187 us; the launch traced here: 184 us
  Pallas kernels  180 us (96%)
  local copies, waits for them, and re-layouts  2.69 us (1%)
    pallas_call x1, Pallas kernels, compute(): pl.pallas_call(compute_kernel, out_shape=(jax.ShapeDtypeStruct((D, TOK),...  68.5 us
    pallas_call x1, Pallas kernels, reduce_grads(): pl.pallas_call(functools.partial(reduce_kernel, extra), out_shape=(jax.Sh...  65 us
    pallas_call x1, Pallas kernels, spread_steps(): pl.pallas_call(spread_kernel, out_shape=jax.ShapeDtypeStruct((ROWS, COLS)...  43.8 us

profile of v3, /device:TPU:1, one launch (start us, length us, event | category | flops | bytes accessed | tf_op | source)
XLA Modules:
  0.0 183.9 jit_solution(17392580570390477945)
XLA Ops:
  0.6 68.5 %blocks.1 = (bf16[800,256]{1,0:T(8,128)(2,1)}, f32[800,256]{1,0:T(8,128)}, bf16[4,112,7168]{2,1,0:T(8,128)(2,1)}) custom-call(s32[2]{0:T(128)} %dilation.1, s32[1,8]{1,0:T(1,128)} %lengths.1, bf16[800,256]{1,0:T(8,128)(2,1)} %bitcast.25, bf16[800,256]{1,0:T(8,128)(2,1)} %bitcast.26, f32[100,3200]{1,0:T(8,128)} %conv.3, f32[2,200,400]{2,1,0:T(8,128)} %w_in.1, ...), custom_call_target="tpu_custom_call" | custom-call | tf_op jit(solution)/shard_map/blocks/pallas_call | solution.py:453
  69.1 65.0 %reduce_grads.1 = (bf16[112,7168]{1,0:T(8,128)(2,1)S(1)}, bf16[4,112,2688]{2,1,0:T(8,128)(2,1)S(1)}) custom-call(bf16[4,112,7168]{2,1,0:T(8,128)(2,1)} %get-tuple-element.35.grads), custom_call_target="tpu_custom_call" | custom-call | tf_op jit(solution)/shard_map/reduce_grads/pallas_call | solution.py:684
  134.1 0.3 orthogonalize.1.window
  134.4 0.0 copy-start
  134.4 0.0 copy-start.1
  134.4 0.0 copy-start.2
  134.4 0.0 copy-start.3
  134.5 0.0 copy-start.4
  134.5 43.8 %spread_steps.1.update = bf16[112,7168]{1,0:T(8,128)(2,1)S(1)} custom-call(bf16[4,112,2688]{2,1,0:T(8,128)(2,1)S(1)} %orthogonalize.1.window), custom_call_target="tpu_custom_call" | custom-call | tf_op jit(solution)/shard_map/spread_steps/pallas_call | solution.py:899
  178.3 0.0 copy-done
  178.3 0.0 copy-done.1
  178.3 0.0 copy-done.2
  178.3 0.0 copy-done.3
  178.3 0.0 copy-done.4
  178.4 0.0 copy-start.6
  178.4 2.9 %finish.1 = (f32[2,200,400]{2,1,0:T(8,128)}, f32[100,3200]{1,0:T(8,128)}, f32[100,2,800]{2,1,0:T(2,128)}, f32[3,2,200]{2,1,0:T(2,128)}, f32[6,2,100]{2,1,0:T(2,1...) custom-call(bf16[112,7168]{1,0:T(8,128)(2,1)S(1)} %get-tuple-element, ...), custom_call_target="tpu_custom_call" | custom-call | tf_op jit(solution)/shard_map/finish/pallas_call | solution.py:959
  181.3 0.0 copy-start.5
  181.3 1.0 copy.29
  182.3 0.0 copy-done.6
  182.3 0.8 copy.32
  183.0 0.0 copy-done.5
  183.0 0.9 copy.33
Async XLA Ops:
  134.4 43.9 %copy-start = (f32[100,3200]{1,0:T(8,128)S(1)}, f32[100,3200]{1,0:T(8,128)}, u32[]{:S(2)}) copy-start(f32[100,3200]{1,0:T(8,128)} %conv.3) | copy-start | bytes 3840004
  134.4 43.9 %copy-start.1 = (f32[2,200,400]{2,1,0:T(8,128)S(1)}, f32[2,200,400]{2,1,0:T(8,128)}, u32[]{:S(2)}) copy-start(f32[2,200,400]{2,1,0:T(8,128)} %w_in.1) | copy-start | bytes 1920004
  134.4 43.9 %copy-start.2 = (f32[2,100,800]{2,0,1:T(2,128)S(1)}, f32[2,100,800]{2,0,1:T(2,128)}, u32[]{:S(2)}) copy-start(f32[2,100,800]{2,0,1:T(2,128)} %param.20) | copy-start | bytes 1920004
  134.4 43.9 %copy-start.3 = (f32[2,3,200]{2,0,1:T(2,128)S(1)}, f32[2,3,200]{2,0,1:T(2,128)}, u32[]{:S(2)}) copy-start(f32[2,3,200]{2,0,1:T(2,128)} %param.21) | copy-start | bytes 14404
  134.5 43.9 %copy-start.4 = (f32[2,6,100]{2,0,1:T(2,128)S(1)}, f32[2,6,100]{2,0,1:T(2,128)}, u32[]{:S(2)}) copy-start(f32[2,6,100]{2,0,1:T(2,128)} %param.22) | copy-start | bytes 14404
  178.4 3.9 %copy-start.6 = (bf16[800,256]{1,0:T(8,128)(2,1)S(1)}, bf16[800,256]{1,0:T(8,128)(2,1)}, u32[]{:S(2)}) copy-start(bf16[800,256]{1,0:T(8,128)(2,1)} %get-tuple-element.33) | copy-start | bytes 1228804
  181.3 1.8 copy-start.5

commit v4 on v0

v4 whole, which is shorter than its diff:
```python
import functools
import math

import jax
import jax.numpy as jnp
from jax import lax
from jax.experimental import pallas as pl
from jax.experimental.pallas import tpu as pltpu
from jax.sharding import PartitionSpec as P

D = 800
H = 400
K_ENC = 5
K_DEC = 3
NS_STEPS = 5
EPSILON = 1e-05
NORM_FLOOR = 1e-07
COEF_A = 3.4445
COEF_B = -4.775
COEF_C = 2.0315
MOMENT_DECAY = 0.5
MATRIX_RATE = 0.5
VECTOR_RATE = 0.1

F32 = jnp.float32
BF16 = jnp.bfloat16
MESH = pl.DeviceIdType.MESH

OWNERS = 4
PIECES = 8
SHARD = 100
ROWS = 112
MIX, ENC, DEC = 0, 1, 2
WIDTH = (256, 256, 384)
IN_AT = ((MIX, 0), (DEC, 1280))
OUT_AT = ((MIX, 896), (DEC, 2176))
CONV_AT = ((ENC, 0), (DEC, 0))
CONV_LANES = ((0, 2048), (1920, 3200))
VEC_AT = 1792
SPLIT = K_ENC * H
TOK = 256
GROUPED = OWNERS * ROWS
WINDOW = 2048

GELU_K = math.sqrt(2.0 / math.pi)
GELU_C = 0.044715


def vmem(shape, dtype):
    return pltpu.VMEM(shape, dtype)


def dot(a, b):
    return lax.dot_general(a, b, (((1,), (0,)), ((), ())), preferred_element_type=F32)


def dot_nt(a, b):
    return lax.dot_general(a, b, (((1,), (1,)), ((), ())), preferred_element_type=F32)


def dot_tn(a, b):
    return lax.dot_general(a, b, (((0,), (0,)), ((), ())), preferred_element_type=F32)


def one_hot(mask):
    return jnp.where(mask, 1.0, 0.0).astype(BF16)


def iota(shape, dim):
    return lax.broadcasted_iota(jnp.int32, shape, dim)


def add_low(*parts):
    total = parts[0].astype(F32)
    for part in parts[1:]:
        total = total + part.astype(F32)
    return total.astype(BF16)


def spans(chunk, low, high):
    width = WIDTH[chunk]
    for q in range(low // width, -(-high // width)):
        yield q, max(low - q * width, 0), min(high - q * width, width)


def load(ref, chunk, low, high, lead=(), rows=slice(None)):
    parts = []
    for q, start, stop in spans(chunk, low, high):
        parts.append(ref[lead + (q // 4, q // 2 % 2, q % 2, rows, slice(start, stop))])
    return parts[0] if len(parts) == 1 else jnp.concatenate(parts, axis=-1)


def store(ref, chunk, low, value, lead=(), rows=slice(None), add=False):
    at = 0
    for q, start, stop in spans(chunk, low, low + value.shape[-1]):
        index = lead + (q // 4, q // 2 % 2, q % 2, rows, slice(start, stop))
        part = value[..., at : at + stop - start]
        ref[index] = add_low(ref[index], part) if add else part
        at += stop - start


def lay_out(conv, w_in, w_out, wide, narrow, put):
    for b in range(2):
        chunk, at = CONV_AT[b]
        lanes = CONV_LANES[b]
        put(chunk, at, slice(0, SHARD), conv[:, lanes[0] : lanes[1]])
        chunk, at = OUT_AT[b]
        put(chunk, at, slice(0, SHARD), w_out[:, b, :])
        chunk, at = IN_AT[b]
        first, second = w_in[b, :SHARD, :], w_in[b, SHARD:, :]
        zeros = jnp.zeros((SHARD, 512 - H), F32)
        low = jnp.concatenate([first, zeros], axis=1)
        high = pltpu.roll(jnp.concatenate([second, zeros], axis=1), H % 128, 1)
        put(chunk, at, slice(0, SHARD), low[:, :384])
        put(chunk, at + 384, slice(0, SHARD), low[:, 384:] + high[:, :128])
        put(chunk, at + 512, slice(0, SHARD), high[:, 128:])
    for b in range(2):
        for k in range(6):
            m = 6 * b + k
            put(MIX, VEC_AT, slice(m, m + 1), narrow[k, b : b + 1, :])
        for k in range(3):
            for h in range(2):
                m = 16 + 16 * h + 3 * b + k
                put(MIX, VEC_AT, slice(m, m + 1), wide[k, b : b + 1, h * SHARD : (h + 1) * SHARD])


def flip(value, bit):
    return value + bit - 2 * bit * ((value // bit) % 2)


def other_owner(own, step):
    if step == 0:
        return own
    if step == 3:
        return 3 - own
    return flip(own, step)


def remote(src, dst, send, recv, device):
    return pltpu.make_async_remote_copy(
        src_ref=src,
        dst_ref=dst,
        send_sem=send,
        recv_sem=recv,
        device_id=device,
        device_id_type=MESH,
    )


class Place:
    def __init__(self, send, recv, extra):
        at = lax.axis_index("dp")
        self.piece = at % PIECES
        self.base = at - self.piece
        self.me = at
        self.own = lax.axis_index("fsdp")
        self.y, self.x, self.c = self.piece // 4, self.piece // 2 % 2, self.piece % 2
        self.core, self.near_x, self.near_y = [
            (self.base + flip(self.piece, bit), self.own) for bit in (1, 2, 4)
        ]
        self.column = [(at, other_owner(self.own, step)) for step in (1, 2, 3)]
        self.far = [(flip(at, bit), self.own) for bit in extra]
        self.send, self.recv, self.used = send, recv, 0
        self.started = []

    def take(self, count):
        first = self.used
        self.used += count
        return first

    def start(self, src, dst, device):
        k = self.take(1)
        copy = remote(src, dst, self.send.at[k], self.recv.at[k], device)
        copy.start()
        self.started.append(copy)
        return copy

    def finish(self):
        for copy in self.started:
            copy.wait_send()


class Gather:
    LOW, HIGH, ALL = pl.ds(0, 64), pl.ds(64, 48), slice(None)

    def __init__(self, place, view):
        self.place, self.view = place, view

    def move(self, device, *index):
        ref = self.view(*index)
        return self.place.start(ref, ref, device)

    def first(self):
        p = self.place
        self.a = self.move(p.near_y, p.y, p.x, p.c, self.LOW)
        self.b = self.move(p.near_x, p.y, p.x, p.c, self.HIGH)

    def second(self):
        p = self.place
        self.a.wait_recv()
        self.a = self.move(p.near_x, self.ALL, p.x, p.c, self.LOW)
        self.b.wait_recv()
        self.b = self.move(p.near_y, p.y, self.ALL, p.c, self.HIGH)

    def third(self):
        p = self.place
        self.a.wait_recv()
        self.b.wait_recv()
        self.a = self.move(p.core, self.ALL, self.ALL, p.c, self.ALL)

    def last(self):
        self.a.wait_recv()


class WeightGather(Gather):
    def __init__(self, place, ref):
        def view(y, x, c, rows):
            return ref.at[pl.ds(1, 3), y, x, c, rows]

        super().__init__(place, view)
        self.ref = ref

    def cross(self):
        p = self.place
        mine = self.ref.at[0, p.y, p.x, p.c]
        self.crossing = [
            p.start(mine, self.ref.at[step, p.y, p.x, p.c], p.column[step - 1]) for step in (1, 2, 3)
        ]

    def first(self):
        for copy in self.crossing:
            copy.wait_recv()
        super().first()


class Reduce:
    def __init__(self, place, grads, moment, room):
        self.place, self.grads, self.moment = place, grads, moment
        self.from_core, self.sums, self.from_x, self.from_y = room[:4]
        self.last_x, self.last_y, self.from_z, self.from_far = room[4:]

    def core(self):
        p = self.place
        self.halves = []
        for y in (1 - p.y, p.y):
            src = self.grads.at[:, y, :, 1 - p.c]
            self.halves.append((y, p.start(src, self.from_core.at[:, y], p.core)))

    def plane(self):
        p = self.place
        self.a = []
        for k, (y, copy) in enumerate(self.halves):
            copy.wait_recv()
            self.sums[:, y] = add_low(self.grads[:, y, :, p.c], self.from_core[:, y])
            self.a.append(
                p.start(self.sums.at[0:2, y, 1 - p.x], self.from_x.at[:, y], p.near_x)
            )
            if k == 0:
                self.b = p.start(self.sums.at[2:4, y], self.from_y, p.near_y)

    def turn(self):
        p = self.place
        y, x = 1 - p.y, 1 - p.x
        self.a[0].wait_recv()
        self.sums[0:2, y, p.x] = add_low(self.sums[0:2, y, p.x], self.from_x[:, y])
        self.y_last = p.start(self.sums.at[0:2, y, p.x], self.last_y, p.near_y)
        self.b.wait_recv()
        self.sums[2:4, p.y, x] = add_low(self.sums[2:4, p.y, x], self.from_y[:, x])
        self.x_last = p.start(self.sums.at[2:4, p.y, x], self.last_x, p.near_x)

    def cross(self):
        p = self.place
        y, x = p.y, p.x
        self.a[1].wait_recv()
        self.y_last.wait_recv()
        self.sums[0:2, y, x] = add_low(self.sums[0:2, y, x], self.from_x[:, y], self.last_y[...])
        self.x_last.wait_recv()
        self.sums[2:4, y, x] = add_low(self.sums[2:4, y, x], self.from_y[:, x], self.last_x[...])
        for k, device in enumerate(p.far):
            p.start(self.sums.at[:, y, x], self.from_far.at[k], device).wait_recv()
            p.started.pop().wait_send()
            self.sums[:, y, x] = add_low(self.sums[:, y, x], self.from_far[k])
        self.crossing = [
            p.start(self.sums.at[step, y, x], self.from_z.at[step - 1], p.column[step - 1])
            for step in (1, 2, 3)
        ]

    def finish(self):
        p = self.place
        for copy in self.crossing:
            copy.wait_recv()
        parts = [self.sums[0, p.y, p.x]] + [self.from_z[k] for k in range(3)]
        self.moment[p.y, p.x, p.c] = add_low(*parts)


def reduce_room(chunk, extra):
    width = WIDTH[chunk]
    shapes = (
        (OWNERS, 2, 2), (OWNERS, 2, 2), (2, 2), (2, 2), (2,), (2,), (3,), (max(len(extra), 1), OWNERS),
    )
    return [vmem(shape + (ROWS, width), BF16) for shape in shapes]


MATRICES = (
    dict(kind="row", chunk=DEC, first=0, last=3, piece=2, own=2, lanes=(80, 1280), slot=0, scale=1.0),
    dict(kind="in", chunk=DEC, first=3, last=5, piece=4, own=2, lanes=(128, 928), slot=1, scale=1.0),
    dict(kind="row", chunk=DEC, first=5, last=7, piece=6, own=1, lanes=(256, 1056), slot=0, scale=math.sqrt(D / H)),
    dict(kind="row", chunk=ENC, first=0, last=7, piece=0, own=1, lanes=(0, 2000), slot=0, scale=1.0),
    dict(kind="in", chunk=MIX, first=0, last=3, piece=5, own=1, lanes=(0, 800), slot=0, scale=1.0),
    dict(kind="row", chunk=MIX, first=3, last=6, piece=3, own=1, lanes=(128, 928), slot=1, scale=math.sqrt(D / H)),
)


class Owner:
    def __init__(self, place, matrix):
        self.place, self.matrix = place, matrix
        self.width = WIDTH[matrix["chunk"]]
        self.count = OWNERS * (matrix["last"] - matrix["first"] + 1)
        p = place
        self.here = (p.piece == matrix["piece"]) & (p.own == matrix["own"])
        self.away = (p.piece != matrix["piece"]) | (p.own != matrix["own"])
        self.holds = (p.piece >= matrix["first"]) & (p.piece <= matrix["last"])
        self.device = (p.base + matrix["piece"], matrix["own"])
        inside = matrix["first"] <= matrix["piece"] <= matrix["last"]
        self.self_at = OWNERS * (matrix["piece"] - matrix["first"]) + matrix["own"] if inside else -1

    def holder(self, r):
        return (self.place.base + self.matrix["first"] + r // OWNERS, r % OWNERS)

    def each_holder(self, act):
        def body(r, carry):
            @pl.when(r != self.self_at)
            def _():
                act(r)

            return carry

        lax.fori_loop(0, self.count, body, 0)

    def lanes(self, k):
        return pl.ds(pl.multiple_of(k * self.width, 128), self.width)

    def greet(self, barrier):
        @pl.when(self.holds & self.away)
        def _():
            pl.semaphore_signal(barrier, inc=1, device_id=self.device, device_id_type=MESH)

        @pl.when(self.here)
        def _():
            def signal(r):
                pl.semaphore_signal(barrier, inc=1, device_id=self.holder(r), device_id_type=MESH)

            self.each_holder(signal)

    def greetings(self):
        others = self.count - (1 if self.self_at >= 0 else 0)
        return jnp.where(self.holds & self.away, 1, 0) + jnp.where(self.here, others, 0)

    def to_owner(self, moment, window, send, recv, k):
        p = self.place
        at = p.piece - self.matrix["first"]
        src = moment.at[p.y, p.x, p.c]
        dst = window.at[p.own, :, self.lanes(at)]
        return remote(src, dst, send.at[k], recv.at[OWNERS * at + p.own], self.device)

    def gather(self, moment, window, send, recv, k):
        @pl.when(self.holds & self.away)
        def _():
            self.to_owner(moment, window, send, recv, k).start()

        if self.self_at >= 0:

            @pl.when(self.here)
            def _():
                p = self.place
                at = p.piece - self.matrix["first"]
                window[p.own, :, self.lanes(at)] = moment[p.y, p.x, p.c]

    def gather_sent(self, moment, window, send, recv, k):
        @pl.when(self.holds & self.away)
        def _():
            self.to_owner(moment, window, send, recv, k).wait_send()

    def gathered(self, moment, window, send, recv, k):
        def wait(r):
            dst = window.at[r % OWNERS, :, self.lanes(r // OWNERS)]
            p = self.place
            src = moment.at[p.y, p.x, p.c]
            remote(src, dst, send.at[k], recv.at[r], self.holder(r)).wait_recv()

        self.each_holder(wait)

    def outgoing(self, window, parts, send, recv, r):
        src = window.at[r % OWNERS, :, self.lanes(r // OWNERS)]
        dst = parts.at[self.matrix["slot"]]
        return remote(src, dst, send.at[r], recv.at[2 * self.matrix["chunk"] + self.matrix["slot"]], self.holder(r))

    def spread(self, window, parts, send, recv):
        self.each_holder(lambda r: self.outgoing(window, parts, send, recv, r).start())
        if self.self_at >= 0:
            p = self.place
            at = p.piece - self.matrix["first"]
            parts[self.matrix["slot"]] = window[p.own, :, self.lanes(at)]

    def spread_sent(self, window, parts, send, recv):
        @pl.when(self.here)
        def _():
            self.each_holder(lambda r: self.outgoing(window, parts, send, recv, r).wait_send())

    def arrived(self, window, parts, send, recv):
        @pl.when(self.holds & self.away)
        def _():
            src = window.at[0, :, self.lanes(0)]
            dst = parts.at[self.matrix["slot"]]
            sems = (send.at[0], recv.at[2 * self.matrix["chunk"] + self.matrix["slot"]])
            remote(src, dst, sems[0], sems[1], self.device).wait_recv()


def split(a):
    high = a.astype(BF16)
    return high, (a - high.astype(F32)).astype(BF16)


def dot_fine(a, b):
    a_high, a_low = split(a)
    b_high, b_low = split(b)
    return dot(a_high, b_high) + (dot(a_high, b_low) + dot(a_low, b_high))


def dot_low(a, b):
    return dot(a.astype(BF16), b.astype(BF16))


def polynomial_of(gram):
    size = gram.shape[0]
    eye = iota((size, size), 0) == iota((size, size), 1)
    unit = jnp.where(eye, 1.0, 0.0)
    power = jnp.sum(jnp.sum(jnp.where(eye, gram, 0.0), axis=1, keepdims=True), axis=0, keepdims=True)
    inverse = 1.0 / (jnp.sqrt(power) + NORM_FLOOR)
    current = gram * inverse * inverse
    result = None
    for step in range(NS_STEPS):
        square = dot_fine if step > 2 else dot_low
        poly = COEF_A * unit + COEF_B * current + COEF_C * square(current, current)
        result = poly if result is None else dot_low(poly, result)
        if step < NS_STEPS - 1:
            first = dot_fine if step < 2 else dot_low
            second = dot_fine if step < 1 else dot_low
            current = second(first(poly, current), poly)
    return result, inverse


def orthogonalize(owners, window, gram, poly, halves):
    is_in, is_row = False, False
    low, high, factor, parts = jnp.int32(0), jnp.int32(0), jnp.float32(0), jnp.int32(0)
    for owner in owners:
        matrix, here = owner.matrix, owner.here
        if matrix["kind"] == "in":
            is_in = is_in | here
        else:
            is_row = is_row | here
        low = jnp.where(here, matrix["lanes"][0], low)
        high = jnp.where(here, matrix["lanes"][1], high)
        parts = jnp.where(here, -(-matrix["lanes"][1] // 512), parts)
        factor = jnp.where(here, MATRIX_RATE * matrix["scale"], factor)

    def part(k):
        lanes = pl.ds(pl.multiple_of(k * 512, 512), 512)
        values = window[:, :, lanes].reshape(GROUPED, 512)
        lane = iota((GROUPED, 512), 1) + k * 512
        return lanes, jnp.where((lane >= low) & (lane < high), values, jnp.zeros((), BF16))

    def half(h):
        return pl.ds(pl.multiple_of(low + 384 * h, 128), 512)

    @pl.when(is_in)
    def _():
        valid = iota((GROUPED, 512), 1) < H
        for h in range(2):
            values = window[:, :, half(h)].reshape(GROUPED, 512).astype(F32)
            if h:
                values = pltpu.roll(values, 512 - H % 128, 1)
            halves[h] = jnp.where(valid, values, 0.0).astype(BF16)
        gram[...] = dot_tn(halves[0], halves[0]) + dot_tn(halves[1], halves[1])

    @pl.when(is_row)
    def _():
        gram[...] = jnp.zeros(gram.shape, F32)

        def body(k, carry):
            values = part(k)[1]
            gram[:GROUPED, :GROUPED] += dot_nt(values, values)
            return carry

        lax.fori_loop(0, parts, body, 0)

    @pl.when(is_in | is_row)
    def _():
        result, inverse = polynomial_of(gram[...])
        poly[...] = (result * (inverse * factor)).astype(BF16)

    @pl.when(is_in)
    def _():
        window[:, :, :1152] = jnp.zeros((OWNERS, ROWS, 1152), BF16)
        window[:, :, half(0)] = dot(halves[0], poly[...]).astype(BF16).reshape(OWNERS, ROWS, 512)
        step = pltpu.roll(dot(halves[1], poly[...]), H % 128, 1).reshape(OWNERS, ROWS, 512)
        window[:, :, half(1)] = add_low(window[:, :, half(1)], step)

    @pl.when(is_row)
    def _():
        def body(k, carry):
            lanes, values = part(k)
            step = dot(poly[:GROUPED, :GROUPED], values)
            window[:, :, lanes] = step.astype(BF16).reshape(OWNERS, ROWS, 512)
            return carry

        lax.fori_loop(0, parts, body, 0)


def norm_forward(src, width, gain, shift, act, unit, slope, spread, chunk=128):
    def body(k, carry):
        rows = pl.ds(pl.multiple_of(k * chunk, chunk), chunk)
        x = src[rows, :width].astype(F32)
        center = x - jnp.mean(x, axis=1, keepdims=True)
        scale = lax.rsqrt(jnp.mean(center * center, axis=1, keepdims=True) + EPSILON)
        xhat = center * scale
        a = xhat * gain + shift
        square = a * a
        half = 0.5 + 0.5 * jnp.tanh(a * (GELU_K + (GELU_K * GELU_C) * square))
        act[rows, :width] = (a * half).astype(BF16)
        unit[rows, :width] = xhat.astype(BF16)
        inner = GELU_K + (3.0 * GELU_K * GELU_C) * square
        slope[rows, :width] = (half + (2.0 * a * inner) * (half * (1.0 - half))).astype(BF16)
        spread[rows, :] = jnp.broadcast_to(scale, (chunk, 128))
        return carry

    lax.fori_loop(0, TOK // chunk, body, 0)


def fold_rows(values):
    total = values[0:8]
    for k in range(1, values.shape[0] // 8):
        total = total + values[8 * k : 8 * k + 8]
    return total


def norm_backward(grad, width, gain, unit, slope, spread, finish, chunk=128):
    def body(k, sums):
        rows = pl.ds(pl.multiple_of(k * chunk, chunk), chunk)
        da = grad[rows, :width] * slope[rows, :width].astype(F32)
        xhat = unit[rows, :width].astype(F32)
        product = da * xhat
        dxhat = da * gain
        mean_one = jnp.mean(dxhat, axis=1, keepdims=True)
        mean_two = jnp.mean(dxhat * xhat, axis=1, keepdims=True)
        dx = spread[rows, 0:1] * (dxhat - mean_one - xhat * mean_two)
        finish(rows, dx)
        return (sums[0] + fold_rows(product), sums[1] + fold_rows(da), sums[2] + fold_rows(dx))

    zero = jnp.zeros((8, width), F32)
    sums = lax.fori_loop(0, TOK // chunk, body, (zero, zero, zero))
    return tuple(jnp.sum(s, axis=0, keepdims=True) for s in sums)


def step_kernel(
    extra,
    dilation, lengths, tokens_hbm, cotangent_hbm,
    conv_hbm, in_hbm, out_hbm, wide_hbm, narrow_hbm,
    mom_conv_hbm, mom_in_hbm, mom_out_hbm, mom_wide_hbm, mom_narrow_hbm,
    out, grad_tokens, moment_mix, moment_enc, moment_dec, update_mix, update_enc, update_dec,
    send, recv, own_send, own_recv, back_send, back_recv, local,
    full_mix, full_enc, full_dec, grads_mix, grads_enc, grads_dec, parts_mix, parts_enc, parts_dec, window,
    tokens, cotangent, conv, in_shard, out_shard, wide_shard, narrow_shard,
    far, perm_h, vec_w, vec_n, w_in, x_one, wide_grad, tall,
    act_d, act_h, act_g, act_t, e_all,
    unit_d, slope_d, spread_d, unit_h, slope_h, spread_h,
    gram, poly, halves, *rooms,
):
    place = Place(send, recv, extra)
    own = place.own
    full = (full_mix, full_enc, full_dec)
    grads = (grads_mix, grads_enc, grads_dec)
    moments = (moment_mix, moment_enc, moment_dec)
    updates = (update_mix, update_enc, update_dec)
    parts = (parts_mix, parts_enc, parts_dec)
    owners = [Owner(place, matrix) for matrix in MATRICES]
    conv_in, spare = gram.at[:TOK], gram.at[TOK:]
    hid = spare

    sources = (conv_hbm, in_hbm, out_hbm, wide_hbm, narrow_hbm, tokens_hbm, cotangent_hbm)
    shard = (conv, in_shard, out_shard, wide_shard, narrow_shard)
    targets = shard + (tokens, cotangent)
    fetches = [pltpu.make_async_copy(s, t, local.at[k]) for k, (s, t) in enumerate(zip(sources, targets))]
    for fetch in fetches:
        fetch.start()
    for ref in parts:
        ref[...] = jnp.zeros(ref.shape, BF16)
    barrier = pltpu.get_barrier_semaphore()
    for device in [place.core, place.near_x, place.near_y] + place.column + place.far:
        pl.semaphore_signal(barrier, inc=1, device_id=device, device_id_type=MESH)
    for owner in owners:
        owner.greet(barrier)
    for ref in full:
        ref[0] = jnp.zeros(ref.shape[1:], BF16)

    def put_weights(chunk, low, rows, values):
        store(full[chunk], chunk, low, values.astype(BF16), lead=(0,), rows=rows)

    for fetch in fetches[:5]:
        fetch.wait()
    lay_out(*shard, put_weights)
    sources = (mom_conv_hbm, mom_in_hbm, mom_out_hbm, mom_wide_hbm, mom_narrow_hbm)
    moment_fetches = [pltpu.make_async_copy(s, t, local.at[7 + k]) for k, (s, t) in enumerate(zip(sources, shard))]
    for fetch in moment_fetches:
        fetch.start()
    greetings = 6 + len(extra)
    for owner in owners:
        greetings = greetings + owner.greetings()
    pl.semaphore_wait(barrier, greetings)

    gathers = [WeightGather(place, ref) for ref in full]
    for gather in gathers:
        gather.cross()

    row, col = iota((TOK, TOK), 0), iota((TOK, TOK), 1)
    seg_row, seg_col = jnp.zeros((TOK, TOK), jnp.int32), jnp.zeros((TOK, TOK), jnp.int32)
    end = jnp.int32(0)
    for k in range(8):
        end = end + lengths[0, k]
        seg_row = seg_row + jnp.where(row >= end, 1, 0)
        seg_col = seg_col + jnp.where(col >= end, 1, 0)
    far[...] = jnp.where(seg_row == seg_col, col - row, 4 * TOK)

    def mover(offset):
        return one_hot(far[...] == offset)

    gathers[MIX].first()
    row, col = iota((H, GROUPED), 0), iota((H, GROUPED), 1)
    used = jnp.zeros((H, GROUPED), jnp.int32)
    for s in range(OWNERS):
        r = col - ROWS * s
        inside = (r >= 0) & (r < SHARD) & (row == r + SHARD * other_owner(own, s))
        used = used + jnp.where(inside, 1, 0)
    perm_h[...] = used.astype(F32).astype(BF16)
    gathers[MIX].second()
    gathers[ENC].first()
    fetches[5].wait()
    x_one[...] = tokens[...].astype(F32).T
    gathers[MIX].third()
    gathers[ENC].second()
    gathers[DEC].first()
    fetches[6].wait()
    wide_grad[...] = cotangent[...].astype(F32).T
    gathers[MIX].last()

    row_n, col_n = iota((128, H), 0), iota((128, H), 1)
    row_w, col_w = iota((128, D), 0), iota((128, D), 1)

    def put_narrow(s):
        return one_hot((col_n == row_n + SHARD * other_owner(own, s)) & (row_n < SHARD))

    def put_wide(s, h):
        return one_hot((col_w == row_w + SHARD * (2 * other_owner(own, s) + h)) & (row_w < SHARD))

    total_n, total_w = jnp.zeros((16, H), F32), jnp.zeros((16, D), F32)
    for s in range(OWNERS):
        vectors = load(full[MIX], MIX, VEC_AT, VEC_AT + 128, lead=(s,))
        total_n = total_n + dot(vectors[0:16], put_narrow(s))
        for h in range(2):
            total_w = total_w + dot(vectors[16 + 16 * h : 32 + 16 * h], put_wide(s, h))
    vec_n[...] = total_n
    vec_w[...] = total_w

    def narrow(b, k):
        return vec_n[6 * b + k : 6 * b + k + 1, :]

    def wide(b, k):
        return vec_w[3 * b + k : 3 * b + k + 1, :]

    def weights(chunk, low, high):
        return load(full[chunk], chunk, low, high, lead=(slice(None),)).reshape(GROUPED, high - low)

    def weight_out(b):
        chunk, at = OUT_AT[b]
        return weights(chunk, at, at + 896)[:, :D]

    def place_in(b):
        chunk, at = IN_AT[b]
        for i in range(OWNERS):
            slot = other_owner(own, i)
            values = load(full[chunk], chunk, at, at + 896, lead=(slot,)).astype(F32)[:SHARD]
            tall[2 * SHARD * i : 2 * SHARD * i + SHARD, :] = values[:, :H]
            high = pltpu.roll(values[:, 384:], 512 - H % 128, 1)
            tall[2 * SHARD * i + SHARD : 2 * SHARD * (i + 1), :] = high[:, :H]
        w_in[b] = tall[...].astype(BF16)

    def taps(b):
        if b == 0:
            return [(H * j, (j - K_ENC // 2) * dilation[0]) for j in range(K_ENC)]
        return [(SPLIT - CONV_LANES[1][0] + H * j, -j * dilation[1]) for j in range(K_DEC)]

    def forward_in(b):
        norm_forward(x_one, D, wide(b, 0), wide(b, 1), act_d.at[b], unit_d.at[b], slope_d.at[b], spread_d.at[b])
        place_in(b)
        hid[:, :H] = dot(act_d[b], w_in[b]) + narrow(b, 0)
        norm_forward(
            hid, H, narrow(b, 1), narrow(b, 2), act_h.at[0], unit_h.at[b, 0], slope_h.at[b, 0], spread_h.at[b, 0]
        )
        act_g[b, 0] = dot(act_h[0], perm_h[...]).astype(BF16)

    def forward_conv(b):
        for j, (at, offset) in enumerate(taps(b)):
            moved = dot(mover(offset), act_g[b, 0]).astype(BF16)
            low = at - at % 128
            product = dot(moved, weights(CONV_AT[b][0], low, low + 512))
            if at % 128:
                product = pltpu.roll(product, 512 - at % 128, 1)
            if j == 0:
                conv_in[...] = product
            else:
                conv_in[...] += product
        conv_in[:, :H] += narrow(b, 3)

    def forward_out(b):
        norm_forward(
            conv_in, H, narrow(b, 4), narrow(b, 5), act_h.at[1], unit_h.at[b, 1], slope_h.at[b, 1], spread_h.at[b, 1]
        )
        act_g[b, 1] = dot(act_h[1], perm_h[...]).astype(BF16)
        return (x_one[...] + dot(act_g[b, 1], weight_out(b))) + wide(b, 2)

    forward_in(0)
    gathers[ENC].third()
    gathers[DEC].second()
    gathers[ENC].last()
    forward_conv(0)
    gathers[DEC].third()
    x_one[...] = forward_out(0)
    gathers[DEC].last()
    forward_in(1)
    forward_conv(1)
    out[...] = forward_out(1).T.astype(BF16)

    reduces = [
        Reduce(place, grads[k], moments[k], rooms[8 * k : 8 * k + 8]) for k in range(3)
    ]
    once = lax.axis_index("dp") == 0
    grouped = (slice(None),)

    def put_grads(chunk, low, values, add=False):
        store(grads[chunk], chunk, low, values.reshape(OWNERS, ROWS, values.shape[-1]), lead=grouped, add=add)

    def fold_moment(chosen):
        @pl.when(once)
        def _():
            def put(chunk, low, rows, values):
                if chunk == chosen:
                    half = (MOMENT_DECAY * values).astype(F32)
                    store(grads[chunk], chunk, low, half, lead=(0,), rows=rows, add=True)

            lay_out(*shard, put)

    rows_w, rows_n = [None] * 6, [None] * 12

    def keep_low(rows, dx):
        act_h[0, rows, :] = dx.astype(BF16)

    def backward_out(b):
        rows_w[3 * b + 2] = jnp.sum(wide_grad[...], axis=0, keepdims=True)
        e3 = wide_grad[...].astype(BF16)
        chunk, at = OUT_AT[b]
        product = dot_tn(act_g[b, 1], e3).astype(BF16)
        put_grads(chunk, at, jnp.concatenate([product, jnp.zeros((GROUPED, 896 - D), BF16)], axis=1))
        back = dot_nt(e3, weight_out(b)).astype(BF16)
        spare[:, :H] = dot_nt(back, perm_h[...])
        sums = norm_backward(
            spare, H, narrow(b, 4), unit_h.at[b, 1], slope_h.at[b, 1], spread_h.at[b, 1], keep_low
        )
        rows_n[6 * b + 4], rows_n[6 * b + 5], rows_n[6 * b + 3] = sums

    def backward_conv(b):
        span = CONV_LANES[b][1] - CONV_LANES[b][0]
        e_all[:, :span] = jnp.zeros((TOK, span), BF16)
        for at, offset in taps(b):
            moved = dot(mover(-offset), act_h[0])
            moved = jnp.concatenate([moved, jnp.zeros((TOK, 512 - H), F32)], axis=1)
            if at % 128:
                moved = pltpu.roll(moved, at % 128, 1)
            low = at - at % 128
            e_all[:, low : low + 512] += moved.astype(BF16)
        chunk = CONV_AT[b][0]
        width = WIDTH[chunk]
        act_t[...] = act_g[b, 0].T

        def piece(q):
            lanes = pl.ds(pl.multiple_of(q * width, 128), width)
            return (q // 4, q // 2 % 2, q % 2), lanes

        def body(q, carry):
            at, lanes = piece(q)
            product = dot(act_t[...], e_all[:, lanes]).astype(BF16)
            grads[chunk][(slice(None),) + at] = product.reshape(OWNERS, ROWS, width)
            return carry

        lax.fori_loop(0, span // width, body, 0)
        rest = span // width * width
        if rest < span:
            put_grads(chunk, rest, dot(act_t[...], e_all[:, rest:span]).astype(BF16))

    def backward_hidden(b):
        span = CONV_LANES[b][1] - CONV_LANES[b][0]
        chunk = CONV_AT[b][0]
        width = WIDTH[chunk]

        def body(q, total):
            lanes = pl.ds(pl.multiple_of(q * width, 128), width)
            values = full[chunk][:, q // 4, q // 2 % 2, q % 2].reshape(GROUPED, width)
            return total + dot_nt(e_all[:, lanes], values)

        back = lax.fori_loop(0, span // width, body, jnp.zeros((TOK, GROUPED), F32))
        rest = span // width * width
        if rest < span:
            back = back + dot_nt(e_all[:, rest:span], weights(chunk, rest, span))
        spare[:, :H] = dot_nt(back.astype(BF16), perm_h[...])
        sums = norm_backward(
            spare, H, narrow(b, 1), unit_h.at[b, 0], slope_h.at[b, 0], spread_h.at[b, 0], keep_low
        )
        rows_n[6 * b + 1], rows_n[6 * b + 2], rows_n[6 * b + 0] = sums

    def backward_weight_in(b):
        chunk, at = IN_AT[b]
        tall[...] = dot_tn(act_d[b], act_h[0])
        zeros = jnp.zeros((SHARD, 512 - H), F32)
        for i in range(OWNERS):
            slot = other_owner(own, i)
            first = tall[2 * SHARD * i : 2 * SHARD * i + SHARD, :]
            second = tall[2 * SHARD * i + SHARD : 2 * SHARD * (i + 1), :]
            low = jnp.concatenate([first, zeros], axis=1)
            high = pltpu.roll(jnp.concatenate([second, zeros], axis=1), H % 128, 1)
            whole = jnp.concatenate([low[:, :384], low[:, 384:] + high[:, :128], high[:, 128:]], axis=1)
            store(grads[chunk], chunk, at, whole.astype(BF16), lead=(slot,), rows=slice(0, SHARD))
        store(
            grads[chunk], chunk, at, jnp.zeros((OWNERS, ROWS - SHARD, 896), BF16), lead=grouped, rows=slice(SHARD, ROWS)
        )

    def backward_in(b):
        x_one[...] = dot_nt(act_h[0], w_in[b])

        def add_up(rows, dx):
            wide_grad[rows, :] += dx

        sums = norm_backward(
            x_one, D, wide(b, 0), unit_d.at[b], slope_d.at[b], spread_d.at[b], add_up
        )
        rows_w[3 * b + 0], rows_w[3 * b + 1] = sums[0], sums[1]

    for fetch in moment_fetches:
        fetch.wait()
    backward_out(1)
    backward_conv(1)
    backward_hidden(1)
    backward_weight_in(1)
    fold_moment(DEC)
    reduces[DEC].core()
    backward_in(1)
    backward_out(0)
    reduces[DEC].plane()
    backward_conv(0)
    fold_moment(ENC)
    reduces[ENC].core()
    reduces[DEC].turn()
    backward_hidden(0)
    reduces[ENC].plane()
    backward_weight_in(0)
    reduces[DEC].cross()
    backward_in(0)
    for m in range(12):
        vec_n[m : m + 1, :] = rows_n[m]
    for m in range(6):
        vec_w[m : m + 1, :] = rows_w[m]
    low_n, low_w = vec_n[...].astype(BF16), vec_w[...].astype(BF16)
    for s in range(OWNERS):
        three = [dot_nt(low_n, put_narrow(s))] + [dot_nt(low_w, put_wide(s, h)) for h in range(2)]
        three.append(jnp.zeros((ROWS - 48, 128), F32))
        store(grads[MIX], MIX, VEC_AT, jnp.concatenate(three, axis=0).astype(BF16), lead=(s,))
        store(grads[MIX], MIX, VEC_AT + 128, jnp.zeros((ROWS, 128), BF16), lead=(s,))
    fold_moment(MIX)
    reduces[MIX].core()
    grad_tokens[...] = wide_grad[...].T
    reduces[ENC].turn()
    reduces[MIX].plane()

    spread_moments = []

    def to_owners(chunk):
        reduces[chunk].finish()
        for k, owner in enumerate(owners):
            if owner.matrix["chunk"] == chunk:
                owner.gather(moments[chunk], window, own_send, own_recv, k)

        def view(y, x, c, rows):
            return moments[chunk].at[y, x, c, rows]

        spread_moments.append(Gather(place, view))
        spread_moments[-1].first()

    to_owners(DEC)
    reduces[ENC].cross()
    reduces[MIX].turn()
    to_owners(ENC)
    reduces[MIX].cross()
    to_owners(MIX)
    for k, owner in enumerate(owners):

        @pl.when(owner.here)
        def _(owner=owner, k=k):
            owner.gathered(moments[owner.matrix["chunk"]], window, own_send, own_recv, k)

    orthogonalize(owners, window, gram, poly, halves)
    for owner in owners:

        @pl.when(owner.here)
        def _(owner=owner):
            owner.spread(window, parts[owner.matrix["chunk"]], back_send, back_recv)

    for gather in spread_moments:
        gather.second()
    for gather in spread_moments:
        gather.third()
    spread_updates = []
    for chunk in (DEC, MIX, ENC):
        for owner in owners:
            if owner.matrix["chunk"] == chunk:
                owner.arrived(window, parts[chunk], back_send, back_recv)
        updates[chunk][place.y, place.x, place.c] = parts[chunk][0] + parts[chunk][1]

        def view(y, x, c, rows, chunk=chunk):
            return updates[chunk].at[y, x, c, rows]

        spread_updates.append(Gather(place, view))
        spread_updates[-1].first()
    for gather in spread_updates:
        gather.second()
    for gather in spread_updates:
        gather.third()
    for gather in spread_moments + spread_updates:
        gather.last()
    for k, owner in enumerate(owners):
        chunk = owner.matrix["chunk"]
        owner.gather_sent(moments[chunk], window, own_send, own_recv, k)
        owner.spread_sent(window, parts[chunk], back_send, back_recv)
    place.finish()


def run_step(extra, dilation, lengths, params, tokens, cotangent, moments):
    in_vmem = pl.BlockSpec(memory_space=pltpu.VMEM)
    in_smem = pl.BlockSpec(memory_space=pltpu.SMEM)
    anywhere = pl.BlockSpec(memory_space=pl.ANY)

    def dma(n):
        return pltpu.SemaphoreType.DMA((n,))

    def pieces(chunk, lead, dtype=BF16):
        return vmem(lead + (2, 2, 2, ROWS, WIDTH[chunk]), dtype)

    shared = [jax.ShapeDtypeStruct((2, 2, 2, ROWS, w), BF16) for w in WIDTH]
    scratch = [dma(96), dma(96), dma(6), dma(32), dma(32), dma(6), dma(12)]
    scratch += [pieces(k, (OWNERS,)) for k in range(3)] * 2
    scratch += [vmem((2, ROWS, w), BF16) for w in WIDTH]
    scratch += [vmem((OWNERS, ROWS, WINDOW), BF16)]
    scratch += [vmem(a.shape, a.dtype) for a in (tokens, cotangent) + tuple(params)]
    scratch += [
        vmem((TOK, TOK), jnp.int32),
        vmem((H, GROUPED), BF16),
        vmem((16, D), F32),
        vmem((16, H), F32),
        vmem((2, D, H), BF16),
        vmem((TOK, D), F32),
        vmem((TOK, D), F32),
        vmem((D, H), F32),
        vmem((2, TOK, D), BF16),
        vmem((2, TOK, H), BF16),
        vmem((2, 2, TOK, GROUPED), BF16),
        vmem((GROUPED, TOK), BF16),
        vmem((TOK, 2048), BF16),
        vmem((2, TOK, D), BF16),
        vmem((2, TOK, D), BF16),
        vmem((2, TOK, 128), F32),
        vmem((2, 2, TOK, H), BF16),
        vmem((2, 2, TOK, H), BF16),
        vmem((2, 2, TOK, 128), F32),
        vmem((512, 512), F32),
        vmem((512, 512), BF16),
        vmem((2, GROUPED, 512), BF16),
    ]
    for chunk in range(3):
        scratch += reduce_room(chunk, extra)
    return pl.pallas_call(
        functools.partial(step_kernel, extra),
        out_shape=(
            jax.ShapeDtypeStruct((D, TOK), BF16),
            jax.ShapeDtypeStruct((D, TOK), F32),
            *shared,
            *shared,
        ),
        in_specs=[in_smem] * 2 + [anywhere] * 12,
        out_specs=(in_vmem,) * 8,
        scratch_shapes=scratch,
        compiler_params=pltpu.CompilerParams(
            collective_id=0, has_side_effects=True, vmem_limit_bytes=60 << 20
        ),
        name="step",
    )(dilation, lengths, tokens, cotangent, *params, *moments)


def finish_kernel(
    vector_step, moment_mix, moment_enc, moment_dec, update_mix, update_enc, update_dec,
    conv, w_in, w_out, wide, narrow,
    mom_in, mom_conv, mom_out, mom_wide, mom_narrow,
    new_in, new_conv, new_out, new_wide, new_narrow, low_in, low_conv, low_out,
):
    moments = (moment_mix, moment_enc, moment_dec)
    updates = (update_mix, update_enc, update_dec)

    def conv_lanes(refs, low, high):
        if high <= 1920:
            return load(refs[ENC], ENC, low, high, rows=slice(0, SHARD)).astype(F32)
        if low >= 2048:
            return load(refs[DEC], DEC, low - 1920, high - 1920, rows=slice(0, SHARD)).astype(F32)
        enc = load(refs[ENC], ENC, 1920, 2048, rows=slice(0, SHARD)).astype(F32)
        dec = load(refs[DEC], DEC, 0, 128, rows=slice(0, SHARD)).astype(F32)
        return jnp.where(iota((SHARD, 128), 1) < SPLIT - 1920, enc, dec)

    for low, high in ((0, 1920), (1920, 2048), (2048, 3200)):
        lanes = slice(low, high)
        mom_conv[:, lanes] = conv_lanes(moments, low, high)
        value = conv[:, lanes] - conv_lanes(updates, low, high)
        new_conv[:, lanes] = value
        low_conv[:, lanes] = value.astype(BF16)
    vectors = load(moment_mix, MIX, VEC_AT, VEC_AT + 128).astype(F32)
    for b in range(2):
        chunk, at = OUT_AT[b]

        def out_lanes(refs):
            return load(refs[chunk], chunk, at, at + 896, rows=slice(0, SHARD)).astype(F32)[:, :D]

        mom_out[:, b, :] = out_lanes(moments)
        value = w_out[:, b, :] - out_lanes(updates)
        new_out[:, b, :] = value
        low_out[b] = value.astype(BF16)
        chunk, at = IN_AT[b]

        def in_lanes(refs, h):
            values = load(refs[chunk], chunk, at + 384 * h, at + 384 * h + 512, rows=slice(0, SHARD)).astype(F32)
            if h:
                values = pltpu.roll(values, 512 - H % 128, 1)
            return values[:, :H]

        for h in range(2):
            rows = slice(h * SHARD, (h + 1) * SHARD)
            mom_in[b, rows, :] = in_lanes(moments, h)
            value = w_in[b, rows, :] - in_lanes(updates, h)
            new_in[b, rows, :] = value
            low_in[b, rows, :] = value.astype(BF16)
        for k in range(6):
            m = 6 * b + k
            value = vectors[m : m + 1, :SHARD]
            mom_narrow[k, b : b + 1, :] = value
            new_narrow[k, b : b + 1, :] = narrow[k, b : b + 1, :] - vector_step * value
        for k in range(3):
            for h in range(2):
                m = 16 + 16 * h + 3 * b + k
                lanes = slice(h * SHARD, (h + 1) * SHARD)
                value = vectors[m : m + 1, :SHARD]
                mom_wide[k, b : b + 1, lanes] = value
                new_wide[k, b : b + 1, lanes] = wide[k, b : b + 1, lanes] - vector_step * value


def finish(vector_step, shared, params):
    in_vmem = pl.BlockSpec(memory_space=pltpu.VMEM)
    conv, w_in, w_out, wide, narrow = params
    shapes = [w_in.shape, conv.shape, w_out.shape, wide.shape, narrow.shape]
    outs = [jax.ShapeDtypeStruct(s, F32) for s in shapes + shapes]
    outs += [jax.ShapeDtypeStruct(s, BF16) for s in shapes[:2] + [(2, SHARD, D)]]
    return pl.pallas_call(
        functools.partial(finish_kernel, vector_step),
        out_shape=tuple(outs),
        in_specs=[in_vmem] * 11,
        out_specs=(in_vmem,) * len(outs),
        compiler_params=pltpu.CompilerParams(vmem_limit_bytes=40 << 20),
        name="finish",
    )(*shared, *params)


def swap(array):
    return jnp.transpose(array, (1, 0, 2))


def shards(
    extra, vector_step, tokens, cotangent, lengths, dilation, proj_in, conv_weight, proj_out, vec_wide, vec_narrow,
    mom_in, mom_conv, mom_out, mom_wide, mom_narrow,
):
    params = (conv_weight, proj_in, swap(proj_out), swap(vec_wide), swap(vec_narrow))
    moments = (mom_conv, mom_in, swap(mom_out), swap(mom_wide), swap(mom_narrow))
    out, grad_tokens, *shared = run_step(extra, dilation, lengths, params, tokens.T, cotangent.T, moments)
    rest = list(finish(vector_step, shared, params))
    for k in (2, 3, 4, 7, 8, 9):
        rest[k] = swap(rest[k])
    return (out.T, grad_tokens.T) + tuple(rest)


def solution(mesh):
    groups, owners = mesh.shape["dp"], mesh.shape["fsdp"]
    assert owners == OWNERS and groups % PIECES == 0
    extra, bit = [], PIECES
    while bit < groups:
        extra.append(bit)
        bit *= 2
    assert bit == groups
    vector_step = VECTOR_RATE / math.sqrt(TOK * groups * owners)
    tok, rep = P(("dp", "fsdp"), None), P()
    mid, first, final = P(None, "fsdp", None), P("fsdp", None), P(None, None, "fsdp")
    params = (mid, first, mid, final, final)
    return jax.shard_map(
        functools.partial(shards, tuple(extra), vector_step),
        mesh=mesh,
        in_specs=(tok, tok, tok, rep) + params + params,
        out_specs=(tok, tok) + params + params + (mid, first, mid),
        check_vma=False,
    )
```

time: 1170 us -> 155 us (0.13); the launches traced: 1150 us -> 155 us
  waiting for transfers between devices: 460 us -> 0 us
  blocking collectives: 249 us -> 0 us
  local copies, waits for them, and re-layouts: 223 us -> 8.94 us
  Pallas kernels: 0 us -> 145 us
  matrix products: 98.6 us -> 0 us
  other arithmetic: 51.9 us -> 0 us
  loops' own time: 41.4 us -> 0 us
  between operations: 23.5 us -> 0.76 us
    unnamed x9 -> x0, waiting for transfers between devices: 427 us -> none
    all_gather x9 -> x0, blocking collectives: 150 us -> none  [the longest x2 50.4 us: fetch_forward(): lax.all_gather(low_out[b], 'fsdp', axis=0, tiled=True)]
    pallas_call x0 -> x2, Pallas kernels: none -> 145 us  [the longest x1 142 us: run_step(): pl.pallas_call(functools.partial(step_kernel, extra), out_shape=(jax.Shap...]
    unnamed x1 -> x0, blocking collectives: 98.9 us -> none
    dot_general x48 -> x0, matrix products: 98.6 us -> none  [the longest x10 30.6 us: orthogonalize(): current = COEF_A * current + jnp.dot(polynomial, current, precision=PRECISE)]
    unnamed x126 -> x29, local copies, waits for them, and re-layouts: 65 us -> 8.94 us
    slice x16 -> x0, local copies, waits for them, and re-layouts: 48 us -> none  [the longest x2 17.3 us: block_forward(): narrow_vec[4]]
    another operation x6 -> x0, loops' own time: 41.4 us -> none  [shards(): lax.cond(owner_self == k % owners, orthogonalize, jnp.zeros_like, matrice...]
  transfers between devices with their start and end apart: 6 -> 0, of which waited for: 4 -> 0; matrix products, arithmetic and copies ran while one was open for 17% -> 0% of each run, Pallas kernels for 0% -> 0%
where the time goes in v4:
time: 155 us
  Pallas kernels  145 us (94%)
  local copies, waits for them, and re-layouts  8.94 us (6%)
    pallas_call x1, Pallas kernels, run_step(): pl.pallas_call(functools.partial(step_kernel, extra), out_shape=(jax.Shap...  142 us
    unnamed x29, local copies, waits for them, and re-layouts  8.94 us
    pallas_call x1, Pallas kernels, finish(): pl.pallas_call(functools.partial(finish_kernel, vector_step), out_shape=t...  3.15 us

profile of v4, /device:TPU:1, one launch (start us, length us, event | category | flops | bytes accessed | tf_op | source)
XLA Modules:
  0.0 154.6 jit_solution(4044898888539325103)
XLA Ops:
  0.7 0.0 copy-start
  0.7 0.0 copy-start.1
  0.7 0.0 copy-start.2
  0.7 0.0 copy-start.9
  0.7 0.0 copy-start.10
  0.7 141.8 %step.1 = (bf16[800,256]{1,0:T(8,128)(2,1)}, f32[800,256]{1,0:T(8,128)}, bf16[2,2,2,112,256]{4,3,2,1,0:T(8,128)(2,1)}, bf16[2,2,2,112,256]{4,3,2,1,0:T(8,128)(2,...) custom-call(s32[2]{0:T(128)} %dilation.1, ...), custom_call_target="tpu_custom_call" | custom-call | tf_op jit(solution)/shard_map/step/pallas_call | solution.py:997
  142.5 0.0 copy-done
  142.5 0.0 copy-done.1
  142.5 0.0 copy-done.2
  142.5 0.0 copy-done.9
  142.5 0.0 copy-done.10
  142.5 0.0 copy-start.3
  142.5 1.1 copy-done.3
  143.6 0.0 copy-start.4
  143.6 1.1 copy-done.4
  144.7 0.0 copy-start.5
  144.7 1.0 copy-done.5
  145.8 0.0 copy-start.6
  145.8 1.0 copy-done.6
  146.8 0.0 copy-start.7
  146.8 1.0 copy-done.7
  147.8 0.0 copy-start.8
  147.8 1.0 copy-done.8
  148.8 0.0 copy-start.12
  148.8 3.1 %finish.1 = (f32[2,200,400]{2,1,0:T(8,128)}, f32[100,3200]{1,0:T(8,128)}, f32[100,2,800]{2,1,0:T(2,128)}, f32[3,2,200]{2,1,0:T(2,128)}, f32[6,2,100]{2,1,0:T(2,1...) custom-call(bf16[2,2,2,112,256]{4,3,2,1,0:T(8,128)(2,1)S(1)} %copy-d, ...), custom_call_target="tpu_custom_call" | custom-call | tf_op jit(solution)/shard_map/finish/pallas_call | solution.py:1084
  152.0 0.0 copy-start.11
  152.0 1.0 copy.29
  153.0 0.0 copy-done.12
  153.0 0.8 copy.32
  153.7 0.0 copy-done.11
  153.7 0.9 copy.33
Async XLA Ops:
  0.7 141.8 %copy-start = (f32[100,3200]{1,0:T(8,128)S(1)}, f32[100,3200]{1,0:T(8,128)}, u32[]{:S(2)}) copy-start(f32[100,3200]{1,0:T(8,128)} %conv.1) | copy-start | bytes 3840004
  0.7 141.8 %copy-start.1 = (f32[2,200,400]{2,1,0:T(8,128)S(1)}, f32[2,200,400]{2,1,0:T(8,128)}, u32[]{:S(2)}) copy-start(f32[2,200,400]{2,1,0:T(8,128)} %w_in.1) | copy-start | bytes 1920004
  0.7 141.8 %copy-start.2 = (f32[2,100,800]{2,0,1:T(2,128)S(1)}, f32[2,100,800]{2,0,1:T(2,128)}, u32[]{:S(2)}) copy-start(f32[2,100,800]{2,0,1:T(2,128)} %param.20) | copy-start | bytes 1920004
  0.7 141.8 %copy-start.9 = (f32[2,3,200]{2,0,1:T(2,128)S(1)}, f32[2,3,200]{2,0,1:T(2,128)}, u32[]{:S(2)}) copy-start(f32[2,3,200]{2,0,1:T(2,128)} %param.21) | copy-start | bytes 14404
  0.7 141.8 %copy-start.10 = (f32[2,6,100]{2,0,1:T(2,128)S(1)}, f32[2,6,100]{2,0,1:T(2,128)}, u32[]{:S(2)}) copy-start(f32[2,6,100]{2,0,1:T(2,128)} %param.22) | copy-start | bytes 14404
  142.5 1.1 copy-start.3
  143.6 1.1 copy-start.4
  144.7 1.0 copy-start.5
  145.8 1.0 copy-start.6
  146.8 1.0 copy-start.7
  147.8 1.0 copy-start.8
  148.8 4.2 %copy-start.12 = (bf16[800,256]{1,0:T(8,128)(2,1)S(1)}, bf16[800,256]{1,0:T(8,128)(2,1)}, u32[]{:S(2)}) copy-start(bf16[800,256]{1,0:T(8,128)(2,1)} %get-tuple-element.36) | copy-start | bytes 1228804
  152.0 1.8 %copy-start.11 = (f32[800,256]{1,0:T(8,128)S(1)}, f32[800,256]{1,0:T(8,128)}, u32[]{:S(2)}) copy-start(f32[800,256]{1,0:T(8,128)} %get-tuple-element.37) | copy-start | bytes 2457604

commit v5 on v4

v5 whole, which is shorter than its diff:
```python
import functools
import math

import jax
import jax.numpy as jnp
from jax import lax
from jax.experimental import pallas as pl
from jax.experimental.pallas import tpu as pltpu
from jax.sharding import PartitionSpec as P

D = 800
H = 400
K_ENC = 5
K_DEC = 3
NS_STEPS = 5
EPSILON = 1e-05
NORM_FLOOR = 1e-07
COEF_A = 3.4445
COEF_B = -4.775
COEF_C = 2.0315
MOMENT_DECAY = 0.5
MATRIX_RATE = 0.5
VECTOR_RATE = 0.1

F32 = jnp.float32
BF16 = jnp.bfloat16
MESH = pl.DeviceIdType.MESH

OWNERS = 4
PIECES = 8
SHARD = 100
ROWS = 112
IN0, CONV0, OUT0, MID1, OUT1 = range(5)
WIDTH = (128, 256, 128, 256, 128)
UNITS = range(len(WIDTH))
IN_AT = ((IN0, 0), (MID1, 1200))
OUT_AT = ((OUT0, 0), (OUT1, 0))
CONV_AT = ((CONV0, 0), (MID1, 0))
CONV_SPAN = (2048, 1280)
VEC_AT = 896
SPLIT = K_ENC * H
TOK = 256
GROUPED = OWNERS * ROWS
WINDOW = 2048

GELU_K = math.sqrt(2.0 / math.pi)
GELU_C = 0.044715


def vmem(shape, dtype):
    return pltpu.VMEM(shape, dtype)


def dot(a, b):
    return lax.dot_general(a, b, (((1,), (0,)), ((), ())), preferred_element_type=F32)


def dot_nt(a, b):
    return lax.dot_general(a, b, (((1,), (1,)), ((), ())), preferred_element_type=F32)


def dot_tn(a, b):
    return lax.dot_general(a, b, (((0,), (0,)), ((), ())), preferred_element_type=F32)


def one_hot(mask):
    return jnp.where(mask, 1.0, 0.0).astype(BF16)


def iota(shape, dim):
    return lax.broadcasted_iota(jnp.int32, shape, dim)


def add_low(*parts):
    total = parts[0].astype(F32)
    for part in parts[1:]:
        total = total + part.astype(F32)
    return total.astype(BF16)


def spans(chunk, low, high):
    width = WIDTH[chunk]
    for q in range(low // width, -(-high // width)):
        yield q, max(low - q * width, 0), min(high - q * width, width)


def load(ref, chunk, low, high, lead=(), rows=slice(None)):
    parts = []
    for q, start, stop in spans(chunk, low, high):
        parts.append(ref[lead + (q // 4, q // 2 % 2, q % 2, rows, slice(start, stop))])
    return parts[0] if len(parts) == 1 else jnp.concatenate(parts, axis=-1)


def store(ref, chunk, low, value, lead=(), rows=slice(None), add=False):
    at = 0
    for q, start, stop in spans(chunk, low, low + value.shape[-1]):
        index = lead + (q // 4, q // 2 % 2, q % 2, rows, slice(start, stop))
        part = value[..., at : at + stop - start]
        ref[index] = add_low(ref[index], part) if add else part
        at += stop - start


def shifted(values, at, low, high):
    rows, count = values.shape
    base = at - at % 128
    width = -(-(at % 128 + count) // 128) * 128
    parts = []
    if base > low:
        parts.append(jnp.zeros((rows, base - low), F32))
    if width > count:
        values = jnp.concatenate([values, jnp.zeros((rows, width - count), F32)], axis=1)
    parts.append(pltpu.roll(values, at % 128, 1) if at % 128 else values)
    if high > base + width:
        parts.append(jnp.zeros((rows, high - base - width), F32))
    return parts[0] if len(parts) == 1 else jnp.concatenate(parts, axis=1)


def lane_window(at, count):
    return at - at % 128, -(-(at + count) // 128) * 128


def unshifted(values, at, count):
    if at % 128:
        values = pltpu.roll(values, values.shape[1] - at % 128, 1)
    return values[:, :count]


def lay_out(unit, conv, w_in, w_out, wide, narrow, put):
    rows = slice(0, SHARD)
    for b in range(2):
        if unit == CONV_AT[b][0]:
            low, high = (0, SPLIT) if b == 0 else (SPLIT, SPLIT + K_DEC * H)
            start, stop = lane_window(low, high - low)
            stop = min(stop, 3200)
            values = unshifted(conv[:, start:stop], low, high - low)
            put(0, rows, values, False)
        if unit == OUT_AT[b][0]:
            put(0, rows, w_out[:, b, :], False)
        if unit == IN_AT[b][0]:
            at = IN_AT[b][1]
            low, high = lane_window(at, 2 * H)
            values = shifted(w_in[b, :SHARD, :], at, low, high) + shifted(w_in[b, SHARD:, :], at + H, low, high)
            put(low, rows, values, True)
    if unit == IN0:
        for b in range(2):
            for k in range(6):
                m = 6 * b + k
                put(VEC_AT, slice(m, m + 1), narrow[k, b : b + 1, :], False)
            for k in range(3):
                for h in range(2):
                    m = 16 + 16 * h + 3 * b + k
                    put(VEC_AT, slice(m, m + 1), wide[k, b : b + 1, h * SHARD : (h + 1) * SHARD], False)


def flip(value, bit):
    return value + bit - 2 * bit * ((value // bit) % 2)


def other_owner(own, step):
    if step == 0:
        return own
    if step == 3:
        return 3 - own
    return flip(own, step)


def remote(src, dst, send, recv, device):
    return pltpu.make_async_remote_copy(
        src_ref=src,
        dst_ref=dst,
        send_sem=send,
        recv_sem=recv,
        device_id=device,
        device_id_type=MESH,
    )


class Place:
    def __init__(self, send, recv, extra):
        at = lax.axis_index("dp")
        self.piece = at % PIECES
        self.base = at - self.piece
        self.me = at
        self.own = lax.axis_index("fsdp")
        self.y, self.x, self.c = self.piece // 4, self.piece // 2 % 2, self.piece % 2
        self.core, self.near_x, self.near_y = [
            (self.base + flip(self.piece, bit), self.own) for bit in (1, 2, 4)
        ]
        self.near_xy = (self.base + flip(flip(self.piece, 2), 4), self.own)
        self.column = [(at, other_owner(self.own, step)) for step in (1, 2, 3)]
        self.far = [(flip(at, bit), self.own) for bit in extra]
        self.inner = (self.own == 1) | (self.own == 2)
        self.send, self.recv, self.used = send, recv, 0
        self.started = []

    def take(self, count):
        first = self.used
        self.used += count
        return first

    def start(self, src, dst, device):
        k = self.take(1)
        copy = remote(src, dst, self.send.at[k], self.recv.at[k], device)
        copy.start()
        self.started.append(copy)
        return copy

    def sent(self):
        for copy in self.started:
            copy.wait_send()
        self.started = []


class Direct:
    ALL = slice(None)

    def __init__(self, place, ref):
        self.place, self.ref = place, ref

    def first(self):
        p = self.place
        mine = self.ref.at[p.y, p.x, p.c]
        self.copies = [p.start(mine, mine, device) for device in (p.near_x, p.near_y, p.near_xy)]

    def second(self):
        p = self.place
        for copy in self.copies:
            copy.wait_recv()
        pieces = self.ref.at[self.ALL, self.ALL, p.c]
        self.copies = [p.start(pieces, pieces, p.core)]

    def last(self):
        self.copies[0].wait_recv()


class Gather:
    LOW, HIGH, ALL = pl.ds(0, 64), pl.ds(64, 48), slice(None)

    def __init__(self, place, view):
        self.place, self.view = place, view

    def move(self, device, *index):
        ref = self.view(*index)
        return self.place.start(ref, ref, device)

    def first(self):
        p = self.place
        self.a = self.move(p.near_y, p.y, p.x, p.c, self.LOW)
        self.b = self.move(p.near_x, p.y, p.x, p.c, self.HIGH)

    def second(self):
        p = self.place
        self.a.wait_recv()
        self.a = self.move(p.near_x, self.ALL, p.x, p.c, self.LOW)
        self.b.wait_recv()
        self.b = self.move(p.near_y, p.y, self.ALL, p.c, self.HIGH)

    def third(self):
        p = self.place
        self.a.wait_recv()
        self.b.wait_recv()
        self.a = self.move(p.core, self.ALL, self.ALL, p.c, self.ALL)

    def last(self):
        self.a.wait_recv()


class WeightGather(Gather):
    def __init__(self, place, ref, low, width):
        lanes = pl.ds(low, width)

        def view(y, x, c, rows):
            return ref.at[pl.ds(1, 3), y, x, c, rows, lanes]

        super().__init__(place, view)
        self.ref, self.lanes = ref, lanes

    def slot(self, step):
        p = self.place
        return self.ref.at[step, p.y, p.x, p.c, :, self.lanes]

    def cross(self):
        p = self.place
        self.crossing = [p.start(self.slot(0), self.slot(step), p.column[step - 1]) for step in (1, 2)]
        k = p.take(1)
        self.direct = remote(self.slot(0), self.slot(3), p.send.at[k], p.recv.at[k], p.column[2])
        relay = p.take(1)
        self.relay = remote(self.slot(2), self.slot(3), p.send.at[relay], p.recv.at[k], p.column[0])

        @pl.when(p.inner)
        def _():
            self.direct.start()

    def first(self, followers=()):
        p = self.place
        self.crossing[1].wait_recv()

        @pl.when(p.inner)
        def _():
            self.relay.start()

        self.crossing[0].wait_recv()
        self.direct.wait_recv()
        for follower in followers:
            follower.cross()
        super().first()

    def finish(self):
        @pl.when(self.place.inner)
        def _():
            self.direct.wait_send()
            self.relay.wait_send()


class Reduce:
    def __init__(self, place, grads, moment, room):
        self.place, self.grads, self.moment = place, grads, moment
        self.from_core, self.sums, self.from_x, self.from_y = room[:4]
        self.last_x, self.last_y, self.from_z, self.from_far = room[4:]

    def core(self):
        p = self.place
        self.halves = []
        for y in (1 - p.y, p.y):
            src = self.grads.at[:, y, :, 1 - p.c]
            self.halves.append((y, p.start(src, self.from_core.at[:, y], p.core)))

    def plane(self):
        p = self.place
        self.a = []
        for k, (y, copy) in enumerate(self.halves):
            copy.wait_recv()
            self.sums[:, y] = add_low(self.grads[:, y, :, p.c], self.from_core[:, y])
            self.a.append(
                p.start(self.sums.at[0:2, y, 1 - p.x], self.from_x.at[:, y], p.near_x)
            )
            if k == 0:
                self.b = p.start(self.sums.at[2:4, y], self.from_y, p.near_y)

    def turn(self):
        p = self.place
        y, x = 1 - p.y, 1 - p.x
        self.a[0].wait_recv()
        self.sums[0:2, y, p.x] = add_low(self.sums[0:2, y, p.x], self.from_x[:, y])
        self.y_last = p.start(self.sums.at[0:2, y, p.x], self.last_y, p.near_y)
        self.b.wait_recv()
        self.sums[2:4, p.y, x] = add_low(self.sums[2:4, p.y, x], self.from_y[:, x])
        self.x_last = p.start(self.sums.at[2:4, p.y, x], self.last_x, p.near_x)

    def cross(self):
        p = self.place
        y, x = p.y, p.x
        self.a[1].wait_recv()
        self.y_last.wait_recv()
        self.sums[0:2, y, x] = add_low(self.sums[0:2, y, x], self.from_x[:, y], self.last_y[...])
        self.x_last.wait_recv()
        self.sums[2:4, y, x] = add_low(self.sums[2:4, y, x], self.from_y[:, x], self.last_x[...])
        for k, device in enumerate(p.far):
            p.start(self.sums.at[:, y, x], self.from_far.at[k], device).wait_recv()
            p.started.pop().wait_send()
            self.sums[:, y, x] = add_low(self.sums[:, y, x], self.from_far[k])
        self.crossing = [
            p.start(self.sums.at[step, y, x], self.from_z.at[step - 1], p.column[step - 1])
            for step in (1, 2, 3)
        ]

    def finish(self):
        p = self.place
        for copy in self.crossing:
            copy.wait_recv()
        parts = [self.sums[0, p.y, p.x]] + [self.from_z[k] for k in range(3)]
        self.moment[p.y, p.x, p.c] = add_low(self.moment[p.y, p.x, p.c], *parts)


def reduce_room(chunk, extra):
    width = WIDTH[chunk]
    shapes = (
        (OWNERS, 2, 2), (OWNERS, 2, 2), (2, 2), (2, 2), (2,), (2,), (3,), (max(len(extra), 1), OWNERS),
    )
    return [vmem(shape + (ROWS, width), BF16) for shape in shapes]


MATRICES = (
    dict(kind="row", unit=OUT1, first=0, last=6, piece=6, lanes=(0, D), slot=0, scale=math.sqrt(D / H)),
    dict(kind="row", unit=MID1, first=0, last=4, piece=2, lanes=(0, K_DEC * H), slot=0, scale=1.0),
    dict(kind="in", unit=MID1, first=4, last=7, piece=4, lanes=(176, 976), slot=1, scale=1.0),
    dict(kind="row", unit=OUT0, first=0, last=6, piece=3, lanes=(0, D), slot=0, scale=math.sqrt(D / H)),
    dict(kind="row", unit=CONV0, first=0, last=7, piece=0, lanes=(0, SPLIT), slot=0, scale=1.0),
    dict(kind="in", unit=IN0, first=0, last=6, piece=5, lanes=(0, D), slot=0, scale=1.0),
)
OWNED_AT = (1, 2)


class Owner:
    def __init__(self, place, matrix, half):
        self.place, self.matrix, self.half = place, matrix, half
        at = self.at = OWNED_AT[half]
        self.width = WIDTH[matrix["unit"]]
        self.count = OWNERS * (matrix["last"] - matrix["first"] + 1)
        p = place
        self.here = (p.piece == matrix["piece"]) & (p.own == at)
        self.away = (p.piece != matrix["piece"]) | (p.own != at)
        self.holds = (p.piece >= matrix["first"]) & (p.piece <= matrix["last"])
        self.served = p.own // 2 == half
        self.device = (p.base + matrix["piece"], at)
    def each_served(self, act):
        def body(k, carry):
            piece, own = self.matrix["first"] + k // 2, 2 * self.half + k % 2

            @pl.when((piece != self.matrix["piece"]) | (own != self.at))
            def _():
                act(k // 2, own, (self.place.base + piece, own))

            return carry

        lax.fori_loop(0, self.count // 2, body, 0)

    def lanes(self, k):
        return pl.ds(pl.multiple_of(k * self.width, 128), self.width)

    def to_owner(self, moment, window, send, recv, k):
        p = self.place
        at = p.piece - self.matrix["first"]
        src = moment.at[p.y, p.x, p.c]
        dst = window.at[p.own, :, self.lanes(at)]
        return remote(src, dst, send.at[k], recv.at[0], self.device)

    def gather(self, moment, window, send, recv, k):
        @pl.when(self.holds & self.away)
        def _():
            self.to_owner(moment, window, send, recv, k).start()

        @pl.when(self.here)
        def _():
            p = self.place
            at = p.piece - self.matrix["first"]
            pltpu.make_async_copy(
                moment.at[p.y, p.x, p.c], window.at[p.own, :, self.lanes(at)], recv.at[0]
            ).start()

    def gather_sent(self, moment, window, send, recv, k):
        @pl.when(self.holds & self.away)
        def _():
            self.to_owner(moment, window, send, recv, k).wait_send()

    def whole(self, window, slots, sem):
        values = window.at[slots, :, pl.ds(0, self.count // OWNERS * self.width)]
        return pltpu.make_async_copy(values, values, sem.at[0])

    def gathered(self, window, recv):
        self.whole(window, pl.ds(0, OWNERS), recv).wait()

    def spread(self, window, parts, send, recv, k):
        p = self.place
        slot = parts.at[self.matrix["slot"]]

        def act(at, own, device):
            remote(window.at[own, :, self.lanes(at)], slot, send.at[0], recv.at[k], device).start()

        self.each_served(act)
        at = p.piece - self.matrix["first"]
        pltpu.make_async_copy(window.at[p.own, :, self.lanes(at)], slot, send.at[0]).start()

    def arrived(self, window, parts, send, recv, k):
        @pl.when(self.here)
        def _():
            self.whole(window, pl.ds(2 * self.half, 2), send).wait()

        @pl.when(self.holds & self.served & self.away)
        def _():
            src = window.at[0, :, self.lanes(0)]
            dst = parts.at[self.matrix["slot"]]
            remote(src, dst, send.at[0], recv.at[k], self.device).wait_recv()


def split(a):
    high = a.astype(BF16)
    return high, (a - high.astype(F32)).astype(BF16)


def dot_fine(a, b):
    a_high, a_low = split(a)
    b_high, b_low = split(b)
    return dot(a_high, b_high) + (dot(a_high, b_low) + dot(a_low, b_high))


def dot_low(a, b):
    return dot(a.astype(BF16), b.astype(BF16))


def polynomial_of(gram):
    size = gram.shape[0]
    eye = iota((size, size), 0) == iota((size, size), 1)
    unit = jnp.where(eye, 1.0, 0.0)
    power = jnp.sum(jnp.sum(jnp.where(eye, gram, 0.0), axis=1, keepdims=True), axis=0, keepdims=True)
    inverse = 1.0 / (jnp.sqrt(power) + NORM_FLOOR)
    current = gram * inverse * inverse
    result = None
    for step in range(NS_STEPS):
        square = dot_fine if step > 2 else dot_low
        poly = COEF_A * unit + COEF_B * current + COEF_C * square(current, current)
        result = poly if result is None else dot_low(poly, result)
        if step < NS_STEPS - 1:
            first = dot_fine if step < 2 else dot_low
            second = dot_fine if step < 1 else dot_low
            current = second(first(poly, current), poly)
    return result, inverse


def orthogonalize(owners, window, gram, poly, halves):
    is_row = False
    high, factor, parts = jnp.int32(0), jnp.float32(0), jnp.int32(0)
    half_at = owners[0].place.own // 2
    two = pl.ds(2 * half_at, 2)
    served = pl.ds(pl.multiple_of(2 * ROWS * half_at, 2 * ROWS), 2 * ROWS)
    for owner in owners:
        matrix, here = owner.matrix, owner.here
        if matrix["kind"] == "row":
            is_row = is_row | here
        high = jnp.where(here, matrix["lanes"][1], high)
        parts = jnp.where(here, -(-matrix["lanes"][1] // 512), parts)
        factor = jnp.where(here, MATRIX_RATE * matrix["scale"], factor)
    ins = {}
    for owner in owners:
        if owner.matrix["kind"] == "in":
            at = owner.matrix["lanes"][0]
            ins[at] = ins.get(at, False) | owner.here
    is_in = False
    for here in ins.values():
        is_in = is_in | here

    def part(k):
        lanes = pl.ds(pl.multiple_of(k * 512, 512), 512)
        values = window[:, :, lanes].reshape(GROUPED, 512)
        lane = iota((GROUPED, 512), 1) + k * 512
        return lanes, jnp.where(lane < high, values, jnp.zeros((), BF16))

    for at, here in ins.items():

        @pl.when(here)
        def _(at=at):
            valid = iota((GROUPED, 512), 1) < H
            for h in range(2):
                low = (at + H * h) // 128 * 128
                values = window[:, :, low : low + 512].reshape(GROUPED, 512).astype(F32)
                if (at + H * h) % 128:
                    values = pltpu.roll(values, 512 - (at + H * h) % 128, 1)
                halves[h] = jnp.where(valid, values, 0.0).astype(BF16)

    @pl.when(is_in)
    def _():
        gram[...] = dot_tn(halves[0], halves[0]) + dot_tn(halves[1], halves[1])

    @pl.when(is_row)
    def _():
        gram[...] = jnp.zeros(gram.shape, F32)

        def body(k, carry):
            values = part(k)[1]
            gram[:GROUPED, :GROUPED] += dot_nt(values, values)
            return carry

        lax.fori_loop(0, parts, body, 0)

    @pl.when(is_in | is_row)
    def _():
        result, inverse = polynomial_of(gram[...])
        poly[...] = (result * (inverse * factor)).astype(BF16)

    for at, here in ins.items():

        @pl.when(here)
        def _(at=at):
            window[:, :, :1024] = jnp.zeros((OWNERS, ROWS, 1024), BF16)
            for h in range(2):
                low = (at + H * h) // 128 * 128
                step = dot_nt(halves[h, served], poly[...])
                if (at + H * h) % 128:
                    step = pltpu.roll(step, (at + H * h) % 128, 1)
                lanes = slice(low, low + 512)
                window[two, :, lanes] = add_low(window[two, :, lanes], step.reshape(2, ROWS, 512))

    @pl.when(is_row)
    def _():
        def body(k, carry):
            lanes, values = part(k)
            step = dot(poly[served, :GROUPED], values)
            window[two, :, lanes] = step.astype(BF16).reshape(2, ROWS, 512)
            return carry

        lax.fori_loop(0, parts, body, 0)


def norm_forward(src, width, gain, shift, act, unit, slope, spread, chunk=128):
    def body(k, carry):
        rows = pl.ds(pl.multiple_of(k * chunk, chunk), chunk)
        x = src[rows, :width].astype(F32)
        center = x - jnp.mean(x, axis=1, keepdims=True)
        scale = lax.rsqrt(jnp.mean(center * center, axis=1, keepdims=True) + EPSILON)
        xhat = center * scale
        a = xhat * gain + shift
        square = a * a
        half = 0.5 + 0.5 * jnp.tanh(a * (GELU_K + (GELU_K * GELU_C) * square))
        act[rows, :width] = (a * half).astype(BF16)
        unit[rows, :width] = xhat.astype(BF16)
        inner = GELU_K + (3.0 * GELU_K * GELU_C) * square
        slope[rows, :width] = (half + (2.0 * a * inner) * (half * (1.0 - half))).astype(BF16)
        spread[rows, :] = jnp.broadcast_to(scale, (chunk, 128))
        return carry

    lax.fori_loop(0, TOK // chunk, body, 0)


def fold_rows(values):
    total = values[0:8]
    for k in range(1, values.shape[0] // 8):
        total = total + values[8 * k : 8 * k + 8]
    return total


def norm_backward(grad, width, gain, unit, slope, spread, finish, chunk=128):
    def body(k, sums):
        rows = pl.ds(pl.multiple_of(k * chunk, chunk), chunk)
        da = grad[rows, :width] * slope[rows, :width].astype(F32)
        xhat = unit[rows, :width].astype(F32)
        product = da * xhat
        dxhat = da * gain
        mean_one = jnp.mean(dxhat, axis=1, keepdims=True)
        mean_two = jnp.mean(dxhat * xhat, axis=1, keepdims=True)
        dx = spread[rows, 0:1] * (dxhat - mean_one - xhat * mean_two)
        finish(rows, dx)
        return (sums[0] + fold_rows(product), sums[1] + fold_rows(da), sums[2] + fold_rows(dx))

    zero = jnp.zeros((8, width), F32)
    sums = lax.fori_loop(0, TOK // chunk, body, (zero, zero, zero))
    return tuple(jnp.sum(s, axis=0, keepdims=True) for s in sums)


def step_kernel(
    extra,
    dilation, lengths, tokens_hbm, cotangent_hbm,
    conv_hbm, in_hbm, out_hbm, wide_hbm, narrow_hbm,
    mom_conv_hbm, mom_in_hbm, mom_out_hbm, mom_wide_hbm, mom_narrow_hbm,
    *refs,
):
    results = refs[:12]
    refs = refs[12:]
    out, grad_tokens, moments, updates = refs[0], refs[1], refs[2:7], refs[7:12]
    refs = refs[2:]
    send, recv, own_send, own_recv, back_send, back_recv, local = refs[10:17]
    full, grads, parts = refs[17:22], refs[22:27], refs[27:32]
    rooms = refs[32:72]
    (
        window,
        tokens, cotangent, conv, in_shard, out_shard, wide_shard, narrow_shard,
        far, perm_h, vec_w, vec_n, w_in, x_one, wide_grad, tall,
        masks, act_d, act_h, act_g, act_t, e_all,
        unit_d, slope_d, spread_d, unit_h, slope_h, spread_h,
        gram, poly, halves,
    ) = refs[72:]
    place = Place(send, recv, extra)
    own = place.own
    owners = [Owner(place, matrix, half) for matrix in MATRICES for half in range(2)]
    conv_in, spare = gram.at[:TOK], gram.at[TOK:]
    hid = spare

    results = [
        pltpu.make_async_copy(source, target, local.at[12 + k])
        for k, (source, target) in enumerate(zip((out, grad_tokens) + moments + updates, results))
    ]

    sources = (conv_hbm, in_hbm, out_hbm, wide_hbm, narrow_hbm, tokens_hbm, cotangent_hbm)
    shard = (conv, in_shard, out_shard, wide_shard, narrow_shard)
    targets = shard + (tokens, cotangent)
    fetches = [pltpu.make_async_copy(s, t, local.at[k]) for k, (s, t) in enumerate(zip(sources, targets))]
    for fetch in fetches:
        fetch.start()
    barrier = pltpu.get_barrier_semaphore()
    for device in [place.core, place.near_x, place.near_y] + place.column + place.far:
        pl.semaphore_signal(barrier, inc=1, device_id=device, device_id_type=MESH)

    def pack(unit):
        full[unit][0] = jnp.zeros(full[unit].shape[1:], BF16)

        def put(low, rows, values, add):
            store(full[unit], unit, low, values.astype(BF16), lead=(0,), rows=rows, add=add)

        lay_out(unit, *shard, put)

    in_unit = WeightGather(place, full[IN0], 0, 128)
    conv_unit = WeightGather(place, full[CONV0], 0, 256)
    out_unit = WeightGather(place, full[OUT0], 0, 128)
    mid_unit = WeightGather(place, full[MID1], 0, 256)
    last_unit = WeightGather(place, full[OUT1], 0, 128)

    for k in (1, 3, 4):
        fetches[k].wait()
    pack(IN0)
    pl.semaphore_wait(barrier, 6 + len(extra))
    in_unit.cross()
    fetches[0].wait()
    pack(CONV0)
    conv_unit.cross()
    fetches[2].wait()
    for unit in (OUT0, MID1, OUT1):
        pack(unit)
    sources = (mom_conv_hbm, mom_in_hbm, mom_out_hbm, mom_wide_hbm, mom_narrow_hbm)
    moment_fetches = [pltpu.make_async_copy(s, t, local.at[7 + k]) for k, (s, t) in enumerate(zip(sources, shard))]
    for fetch in moment_fetches:
        fetch.start()

    row, col = iota((TOK, TOK), 0), iota((TOK, TOK), 1)
    seg_row, seg_col = jnp.zeros((TOK, TOK), jnp.int32), jnp.zeros((TOK, TOK), jnp.int32)
    end = jnp.int32(0)
    for k in range(8):
        end = end + lengths[0, k]
        seg_row = seg_row + jnp.where(row >= end, 1, 0)
        seg_col = seg_col + jnp.where(col >= end, 1, 0)
    far[...] = jnp.where(seg_row == seg_col, col - row, 4 * TOK)

    enc_shifts = [(j - K_ENC // 2) * dilation[0] for j in range(K_ENC)]
    dec_shifts = [j * dilation[1] for j in range(1 - K_DEC, K_DEC)]
    for k, shift in enumerate(enc_shifts + dec_shifts):
        masks[k] = one_hot(far[...] == shift)
    tap_masks = (
        [(j, K_ENC - 1 - j) for j in range(K_ENC)],
        [(K_ENC + K_DEC - 1 - j, K_ENC + K_DEC - 1 + j) for j in range(K_DEC)],
    )

    in_unit.first([out_unit, mid_unit])
    row, col = iota((H, GROUPED), 0), iota((H, GROUPED), 1)
    used = jnp.zeros((H, GROUPED), jnp.int32)
    for s in range(OWNERS):
        r = col - ROWS * s
        inside = (r >= 0) & (r < SHARD) & (row == r + SHARD * other_owner(own, s))
        used = used + jnp.where(inside, 1, 0)
    perm_h[...] = used.astype(F32).astype(BF16)
    in_unit.second()
    conv_unit.first([last_unit])
    fetches[5].wait()
    x_one[...] = tokens[...].astype(F32).T
    in_unit.third()
    conv_unit.second()
    fetches[6].wait()
    wide_grad[...] = cotangent[...].astype(F32).T
    in_unit.last()

    row_n, col_n = iota((128, H), 0), iota((128, H), 1)
    row_w, col_w = iota((128, D), 0), iota((128, D), 1)

    def put_narrow(s):
        return one_hot((col_n == row_n + SHARD * other_owner(own, s)) & (row_n < SHARD))

    def put_wide(s, h):
        return one_hot((col_w == row_w + SHARD * (2 * other_owner(own, s) + h)) & (row_w < SHARD))

    total_n, total_w = jnp.zeros((16, H), F32), jnp.zeros((16, D), F32)
    for s in range(OWNERS):
        vectors = load(full[IN0], IN0, VEC_AT, VEC_AT + 128, lead=(s,))
        total_n = total_n + dot(vectors[0:16], put_narrow(s))
        for h in range(2):
            total_w = total_w + dot(vectors[16 + 16 * h : 32 + 16 * h], put_wide(s, h))
    vec_n[...] = total_n
    vec_w[...] = total_w

    def narrow(b, k):
        return vec_n[6 * b + k : 6 * b + k + 1, :]

    def wide(b, k):
        return vec_w[3 * b + k : 3 * b + k + 1, :]

    def weights(unit, low, high):
        return load(full[unit], unit, low, high, lead=(slice(None),)).reshape(GROUPED, high - low)

    def weight_out(b):
        return weights(OUT_AT[b][0], 0, 896)[:, :D]

    def place_in(b):
        unit, at = IN_AT[b]
        for i in range(OWNERS):
            slot = other_owner(own, i)
            for h in range(2):
                low, high = lane_window(at + H * h, H)
                values = load(full[unit], unit, low, high, lead=(slot,)).astype(F32)[:SHARD]
                row_at = SHARD * (2 * i + h)
                tall[row_at : row_at + SHARD, :] = unshifted(values, at + H * h, H)
        w_in[b] = tall[...].astype(BF16)

    def taps(b):
        return [(H * j, forward, backward) for j, (forward, backward) in enumerate(tap_masks[b])]

    def forward_in(b):
        norm_forward(x_one, D, wide(b, 0), wide(b, 1), act_d.at[b], unit_d.at[b], slope_d.at[b], spread_d.at[b])
        place_in(b)
        hid[:, :H] = dot(act_d[b], w_in[b]) + narrow(b, 0)
        norm_forward(
            hid, H, narrow(b, 1), narrow(b, 2), act_h.at[0], unit_h.at[b, 0], slope_h.at[b, 0], spread_h.at[b, 0]
        )
        act_g[b, 0] = dot(act_h[0], perm_h[...]).astype(BF16)

    def forward_conv(b):
        for j, (at, mask, unused) in enumerate(taps(b)):
            moved = dot(masks[mask], act_g[b, 0]).astype(BF16)
            low = at - at % 128
            product = dot(moved, weights(CONV_AT[b][0], low, low + 512))
            if at % 128:
                product = pltpu.roll(product, 512 - at % 128, 1)
            if j == 0:
                conv_in[...] = product
            else:
                conv_in[...] += product
        conv_in[:, :H] += narrow(b, 3)

    def forward_out(b):
        norm_forward(
            conv_in, H, narrow(b, 4), narrow(b, 5), act_h.at[1], unit_h.at[b, 1], slope_h.at[b, 1], spread_h.at[b, 1]
        )
        act_g[b, 1] = dot(act_h[1], perm_h[...]).astype(BF16)
        return (x_one[...] + dot(act_g[b, 1], weight_out(b))) + wide(b, 2)

    forward_in(0)
    out_unit.first()
    mid_unit.first()
    conv_unit.third()

    for fetch in moment_fetches:
        fetch.wait()
    for unit in UNITS:
        moments[unit][...] = jnp.zeros(moments[unit].shape, BF16)

        def put_moment(low, rows, values, add, unit=unit):
            store(moments[unit], unit, low, (MOMENT_DECAY * values).astype(BF16), rows=rows, add=add)

        lay_out(unit, *shard, put_moment)
        parts[unit][...] = jnp.zeros(parts[unit].shape, BF16)

    out_unit.second()
    mid_unit.second()
    last_unit.first()
    conv_unit.last()
    forward_conv(0)
    out_unit.third()
    mid_unit.third()
    last_unit.second()
    out_unit.last()
    x_one[...] = forward_out(0)
    last_unit.third()
    mid_unit.last()
    forward_in(1)
    forward_conv(1)
    last_unit.last()
    out[...] = forward_out(1).T.astype(BF16)
    results[0].start()
    for unit in (in_unit, conv_unit, out_unit, mid_unit, last_unit):
        unit.finish()
    place.sent()
    gathers_used = place.used

    reduces = [Reduce(place, grads[k], moments[k], rooms[8 * k : 8 * k + 8]) for k in UNITS]
    grouped = (slice(None),)

    def put_grads(unit, low, values, add=False):
        store(grads[unit], unit, low, values.reshape(OWNERS, ROWS, values.shape[-1]), lead=grouped, add=add)

    rows_w, rows_n = [None] * 6, [None] * 12

    def keep_low(rows, dx):
        act_h[0, rows, :] = dx.astype(BF16)

    def backward_weight_out(b):
        rows_w[3 * b + 2] = jnp.sum(wide_grad[...], axis=0, keepdims=True)
        product = dot_tn(act_g[b, 1], wide_grad[...].astype(BF16)).astype(BF16)
        put_grads(OUT_AT[b][0], 0, jnp.concatenate([product, jnp.zeros((GROUPED, 1024 - D), BF16)], axis=1))

    def backward_out(b):
        back = dot_nt(wide_grad[...].astype(BF16), weight_out(b)).astype(BF16)
        spare[:, :H] = dot_nt(back, perm_h[...])
        sums = norm_backward(
            spare, H, narrow(b, 4), unit_h.at[b, 1], slope_h.at[b, 1], spread_h.at[b, 1], keep_low
        )
        rows_n[6 * b + 4], rows_n[6 * b + 5], rows_n[6 * b + 3] = sums

    def backward_conv(b):
        span = CONV_SPAN[b]
        e_all[:, :span] = jnp.zeros((TOK, span), BF16)
        for at, unused, mask in taps(b):
            moved = dot(masks[mask], act_h[0])
            moved = jnp.concatenate([moved, jnp.zeros((TOK, 512 - H), F32)], axis=1)
            if at % 128:
                moved = pltpu.roll(moved, at % 128, 1)
            low = at - at % 128
            e_all[:, low : low + 512] += moved.astype(BF16)
        act_t[...] = act_g[b, 0].T
        for low in range(0, span, 512):
            high = min(low + 512, span)
            put_grads(CONV_AT[b][0], low, dot(act_t[...], e_all[:, low:high]).astype(BF16))

    def backward_hidden(b):
        span = CONV_SPAN[b]
        back = None
        for low in range(0, span, 512):
            high = min(low + 512, span)
            part = dot_nt(e_all[:, low:high], weights(CONV_AT[b][0], low, high))
            back = part if back is None else back + part
        spare[:, :H] = dot_nt(back.astype(BF16), perm_h[...])
        sums = norm_backward(
            spare, H, narrow(b, 1), unit_h.at[b, 0], slope_h.at[b, 0], spread_h.at[b, 0], keep_low
        )
        rows_n[6 * b + 1], rows_n[6 * b + 2], rows_n[6 * b + 0] = sums

    def backward_weight_in(b):
        unit, at = IN_AT[b]
        tall[...] = dot_tn(act_d[b], act_h[0])
        low, high = lane_window(at, 2 * H)
        spare_rows = slice(SHARD, ROWS)
        if at % 128:
            rest = jnp.zeros((OWNERS, ROWS - SHARD, high - low - 128), BF16)
            store(grads[unit], unit, low + 128, rest, lead=grouped, rows=spare_rows)
        else:
            rest = jnp.zeros((OWNERS, ROWS - SHARD, high - low), BF16)
            store(grads[unit], unit, low, rest, lead=grouped, rows=spare_rows)
        for i in range(OWNERS):
            slot = other_owner(own, i)
            first = tall[2 * SHARD * i : 2 * SHARD * i + SHARD, :]
            second = tall[2 * SHARD * i + SHARD : 2 * SHARD * (i + 1), :]
            whole = shifted(first, at, low, high) + shifted(second, at + H, low, high)
            where = dict(lead=(slot,), rows=slice(0, SHARD))
            if at % 128:
                store(grads[unit], unit, low, whole[:, :128], add=True, **where)
                store(grads[unit], unit, low + 128, whole[:, 128:].astype(BF16), **where)
            else:
                store(grads[unit], unit, low, whole.astype(BF16), **where)

    def backward_in(b):
        x_one[...] = dot_nt(act_h[0], w_in[b])

        def add_up(rows, dx):
            wide_grad[rows, :] += dx

        sums = norm_backward(
            x_one, D, wide(b, 0), unit_d.at[b], slope_d.at[b], spread_d.at[b], add_up
        )
        rows_w[3 * b + 0], rows_w[3 * b + 1] = sums[0], sums[1]

    spread_moments = []

    def to_owners(unit):
        reduces[unit].finish()
        for k, owner in enumerate(owners):
            if owner.matrix["unit"] == unit:
                owner.gather(moments[unit], window, own_send, own_recv, k)
        spread_moments.append(Direct(place, moments[unit]))

    backward_weight_out(1)
    reduces[OUT1].core()
    backward_out(1)
    reduces[OUT1].plane()
    backward_conv(1)
    backward_hidden(1)
    reduces[OUT1].turn()
    backward_weight_in(1)
    reduces[MID1].core()
    backward_in(1)
    reduces[OUT1].cross()
    backward_weight_out(0)
    reduces[OUT0].core()
    reduces[MID1].plane()
    backward_out(0)
    backward_conv(0)
    reduces[CONV0].core()
    reduces[OUT0].plane()
    to_owners(OUT1)
    backward_hidden(0)
    reduces[MID1].turn()
    reduces[CONV0].plane()
    backward_weight_in(0)
    reduces[OUT0].turn()
    backward_in(0)
    for m in range(12):
        vec_n[m : m + 1, :] = rows_n[m]
    for m in range(6):
        vec_w[m : m + 1, :] = rows_w[m]
    low_n, low_w = vec_n[...].astype(BF16), vec_w[...].astype(BF16)
    for s in range(OWNERS):
        three = [dot_nt(low_n, put_narrow(s))] + [dot_nt(low_w, put_wide(s, h)) for h in range(2)]
        three.append(jnp.zeros((ROWS - 48, 128), F32))
        store(grads[IN0], IN0, VEC_AT, jnp.concatenate(three, axis=0).astype(BF16), lead=(s,))
    reduces[IN0].core()
    reduces[MID1].cross()
    grad_tokens[...] = wide_grad[...].T
    results[1].start()
    reduces[CONV0].turn()
    reduces[IN0].plane()
    reduces[OUT0].cross()
    to_owners(MID1)
    reduces[IN0].turn()
    reduces[CONV0].cross()
    to_owners(OUT0)
    reduces[IN0].cross()
    to_owners(CONV0)
    to_owners(IN0)
    reduces_used, place.used = place.used, 0
    for gather in spread_moments:
        gather.first()
    for owner in owners:

        @pl.when(owner.here)
        def _(owner=owner):
            owner.gathered(window, own_recv)

    orthogonalize(owners, window, gram, poly, halves)
    for k, owner in enumerate(owners):

        @pl.when(owner.here)
        def _(owner=owner, k=k):
            owner.spread(window, parts[owner.matrix["unit"]], back_send, back_recv, k // 2)

    for gather in spread_moments:
        gather.second()
    spread_updates = []

    def take_updates(unit):
        for k, owner in enumerate(owners):
            if owner.matrix["unit"] == unit:
                owner.arrived(window, parts[unit], back_send, back_recv, k // 2)
        total = parts[unit][0]
        if unit == MID1:
            total = total + parts[unit][1]
        updates[unit][place.y, place.x, place.c] = total
        spread_updates.append(Direct(place, updates[unit]))
        spread_updates[-1].first()

    for unit in (OUT1, OUT0, IN0, MID1, CONV0):
        take_updates(unit)
    for gather in spread_moments:
        gather.last()
    for copy in results[2:7]:
        copy.start()
    for gather in spread_updates:
        gather.second()
    for k, unit in enumerate((OUT1, OUT0, IN0, MID1, CONV0)):
        spread_updates[k].last()
        results[7 + unit].start()
    assert place.used <= gathers_used
    for k, owner in enumerate(owners):
        owner.gather_sent(moments[owner.matrix["unit"]], window, own_send, own_recv, k)
    place.sent()
    for copy in results:
        copy.wait()


def run_step(extra, dilation, lengths, params, tokens, cotangent, moments):
    in_smem = pl.BlockSpec(memory_space=pltpu.SMEM)
    anywhere = pl.BlockSpec(memory_space=pltpu.HBM)

    def dma(n):
        return pltpu.SemaphoreType.DMA((n,))

    def pieces(chunk, lead, dtype=BF16):
        return vmem(lead + (2, 2, 2, ROWS, WIDTH[chunk]), dtype)

    shared = [jax.ShapeDtypeStruct((2, 2, 2, ROWS, w), BF16) for w in WIDTH]
    results = [jax.ShapeDtypeStruct((D, TOK), BF16), jax.ShapeDtypeStruct((D, TOK), F32)] + shared + shared
    count = 9 * len(WIDTH) + (10 + len(extra)) * len(WIDTH)
    scratch = [vmem(a.shape, a.dtype) for a in results]
    scratch += [dma(count), dma(count), dma(2 * len(MATRICES)), dma(1), dma(1), dma(len(MATRICES)), dma(24)]
    scratch += [pieces(k, (OWNERS,)) for k in UNITS] * 2
    scratch += [vmem((2 if k == MID1 else 1, ROWS, w), BF16) for k, w in enumerate(WIDTH)]
    for unit in UNITS:
        scratch += reduce_room(unit, extra)
    scratch += [vmem((OWNERS, ROWS, WINDOW), BF16)]
    scratch += [vmem(a.shape, a.dtype) for a in (tokens, cotangent) + tuple(params)]
    scratch += [
        vmem((TOK, TOK), jnp.int32),
        vmem((H, GROUPED), BF16),
        vmem((16, D), F32),
        vmem((16, H), F32),
        vmem((2, D, H), BF16),
        vmem((TOK, D), F32),
        vmem((TOK, D), F32),
        vmem((D, H), F32),
        vmem((K_ENC + 2 * K_DEC - 1, TOK, TOK), BF16),
        vmem((2, TOK, D), BF16),
        vmem((2, TOK, H), BF16),
        vmem((2, 2, TOK, GROUPED), BF16),
        vmem((GROUPED, TOK), BF16),
        vmem((TOK, 2048), BF16),
        vmem((2, TOK, D), BF16),
        vmem((2, TOK, D), BF16),
        vmem((2, TOK, 128), F32),
        vmem((2, 2, TOK, H), BF16),
        vmem((2, 2, TOK, H), BF16),
        vmem((2, 2, TOK, 128), F32),
        vmem((512, 512), F32),
        vmem((512, 512), BF16),
        vmem((2, GROUPED, 512), BF16),
    ]
    return pl.pallas_call(
        functools.partial(step_kernel, extra),
        out_shape=tuple(results),
        in_specs=[in_smem] * 2 + [anywhere] * 12,
        out_specs=(anywhere,) * 12,
        scratch_shapes=scratch,
        compiler_params=pltpu.CompilerParams(
            collective_id=0, has_side_effects=True, vmem_limit_bytes=62 << 20
        ),
        name="step",
    )(dilation, lengths, tokens, cotangent, *params, *moments)


def finish_kernel(
    vector_step, *refs,
):
    in_hbm, out_to_hbm, ins, outs = refs[:17], refs[17:32], refs[32:49], refs[49:62]
    in_sems, out_sems = refs[62:]
    moments, updates = ins[2:7], ins[7:12]
    conv, w_in, w_out, wide, narrow = ins[12:]
    (
        mom_in, mom_conv, mom_out, mom_wide, mom_narrow,
        new_in, new_conv, new_out, new_wide, new_narrow, low_in, low_conv, low_out,
    ) = outs
    arrivals = [pltpu.make_async_copy(s, t, in_sems.at[k]) for k, (s, t) in enumerate(zip(in_hbm, ins))]
    sources = outs + ins[:2]
    targets = out_to_hbm[2:] + out_to_hbm[:2]
    departures = [pltpu.make_async_copy(s, t, out_sems.at[k]) for k, (s, t) in enumerate(zip(sources, targets))]
    arrivals = arrivals[2:] + arrivals[:2]
    for copy in arrivals:
        copy.start()
    rows = slice(0, SHARD)

    def conv_parts(refs):
        enc = load(refs[CONV0], CONV0, 0, 2048, rows=rows).astype(F32)
        dec = load(refs[MID1], MID1, 0, 1280, rows=rows).astype(F32)
        dec = pltpu.roll(dec, SPLIT % 128, 1)
        middle = jnp.where(iota((SHARD, 128), 1) < SPLIT % 128, enc[:, 1920:], dec[:, :128])
        return ((0, enc[:, :1920]), (1920, middle), (2048, dec[:, 128:]))

    def out_lanes(refs, b):
        return load(refs[OUT_AT[b][0]], OUT_AT[b][0], 0, 896, rows=rows).astype(F32)[:, :D]

    def in_lanes(refs, b, h):
        unit, at = IN_AT[b]
        low, high = lane_window(at + H * h, H)
        return unshifted(load(refs[unit], unit, low, high, rows=rows).astype(F32), at + H * h, H)

    for copy in arrivals[:5]:
        copy.wait()
    for low, values in conv_parts(moments):
        mom_conv[:, low : low + values.shape[1]] = values
    departures[1].start()
    for b in range(2):
        mom_out[:, b, :] = out_lanes(moments, b)
        for h in range(2):
            mom_in[b, h * SHARD : (h + 1) * SHARD, :] = in_lanes(moments, b, h)
    departures[0].start()
    departures[2].start()
    for copy in arrivals[15:]:
        copy.wait()
    for copy in departures[13:]:
        copy.start()
    for copy in arrivals[5:15]:
        copy.wait()
    for low, values in conv_parts(updates):
        lanes = slice(low, low + values.shape[1])
        value = conv[:, lanes] - values
        new_conv[:, lanes] = value
        low_conv[:, lanes] = value.astype(BF16)
    departures[6].start()
    departures[11].start()
    for b in range(2):
        value = w_out[:, b, :] - out_lanes(updates, b)
        new_out[:, b, :] = value
        for h in range(2):
            here = slice(h * SHARD, (h + 1) * SHARD)
            value = w_in[b, here, :] - in_lanes(updates, b, h)
            new_in[b, here, :] = value
            low_in[b, here, :] = value.astype(BF16)
    low_out[...] = new_out[...].astype(BF16)
    for k in (5, 7, 10, 12):
        departures[k].start()
    vectors = load(moments[IN0], IN0, VEC_AT, VEC_AT + 128).astype(F32)
    for b in range(2):
        for k in range(6):
            m = 6 * b + k
            value = vectors[m : m + 1, :SHARD]
            mom_narrow[k, b : b + 1, :] = value
            new_narrow[k, b : b + 1, :] = narrow[k, b : b + 1, :] - vector_step * value
        for k in range(3):
            for h in range(2):
                m = 16 + 16 * h + 3 * b + k
                lanes = slice(h * SHARD, (h + 1) * SHARD)
                value = vectors[m : m + 1, :SHARD]
                mom_wide[k, b : b + 1, lanes] = value
                new_wide[k, b : b + 1, lanes] = wide[k, b : b + 1, lanes] - vector_step * value
    for k in (3, 4, 8, 9):
        departures[k].start()
    for copy in departures:
        copy.wait()


def finish(vector_step, shared, params):
    in_hbm = pl.BlockSpec(memory_space=pltpu.HBM)
    conv, w_in, w_out, wide, narrow = params
    shapes = [w_in.shape, conv.shape, w_out.shape, wide.shape, narrow.shape]
    outs = [jax.ShapeDtypeStruct(a.shape, a.dtype) for a in shared[:2]]
    outs += [jax.ShapeDtypeStruct(s, F32) for s in shapes + shapes]
    outs += [jax.ShapeDtypeStruct(s, BF16) for s in shapes[:3]]
    ins = tuple(shared) + tuple(params)
    return pl.pallas_call(
        functools.partial(finish_kernel, vector_step),
        out_shape=tuple(outs),
        in_specs=[in_hbm] * len(ins),
        out_specs=(in_hbm,) * len(outs),
        scratch_shapes=[vmem(a.shape, a.dtype) for a in ins + tuple(outs[2:])]
        + [pltpu.SemaphoreType.DMA((17,)), pltpu.SemaphoreType.DMA((15,))],
        compiler_params=pltpu.CompilerParams(vmem_limit_bytes=62 << 20),
        name="finish",
    )(*ins)


def swap(array):
    return jnp.transpose(array, (1, 0, 2))


def shards(
    extra, vector_step, tokens, cotangent, lengths, dilation, proj_in, conv_weight, proj_out, vec_wide, vec_narrow,
    mom_in, mom_conv, mom_out, mom_wide, mom_narrow,
):
    params = (conv_weight, proj_in, swap(proj_out), swap(vec_wide), swap(vec_narrow))
    moments = (mom_conv, mom_in, swap(mom_out), swap(mom_wide), swap(mom_narrow))
    shared = run_step(extra, dilation, lengths, params, tokens.T, cotangent.T, moments)
    outs = list(finish(vector_step, shared, params))
    for k in (0, 1):
        outs[k] = outs[k].T
    for k in (4, 5, 6, 9, 10, 11, 14):
        outs[k] = swap(outs[k])
    return tuple(outs)


def solution(mesh):
    groups, owners = mesh.shape["dp"], mesh.shape["fsdp"]
    assert owners == OWNERS and groups % PIECES == 0
    extra, bit = [], PIECES
    while bit < groups:
        extra.append(bit)
        bit *= 2
    assert bit == groups
    vector_step = VECTOR_RATE / math.sqrt(TOK * groups * owners)
    tok, rep = P(("dp", "fsdp"), None), P()
    mid, first, final = P(None, "fsdp", None), P("fsdp", None), P(None, None, "fsdp")
    params = (mid, first, mid, final, final)
    return jax.shard_map(
        functools.partial(shards, tuple(extra), vector_step),
        mesh=mesh,
        in_specs=(tok, tok, tok, rep) + params + params,
        out_specs=(tok, tok) + params + params + (mid, first, mid),
        check_vma=False,
    )
```

time: 155 us -> 137 us (0.88)
  Pallas kernels: 145 us -> 136 us
  local copies, waits for them, and re-layouts: 8.94 us -> 0 us
    pallas_call x1, Pallas kernels: 142 us -> 129 us  [run_step(): pl.pallas_call(functools.partial(step_kernel, extra), out_shape=tuple(res...]
    unnamed x29 -> x0, local copies, waits for them, and re-layouts: 8.94 us -> none
    pallas_call x1, Pallas kernels: 3.15 us -> 6.98 us  [finish(): pl.pallas_call(functools.partial(finish_kernel, vector_step), out_shape=t...]
where the time goes in v5:
time: 137 us
  Pallas kernels  136 us (99%)
    pallas_call x1, Pallas kernels, run_step(): pl.pallas_call(functools.partial(step_kernel, extra), out_shape=tuple(res...  129 us
    pallas_call x1, Pallas kernels, finish(): pl.pallas_call(functools.partial(finish_kernel, vector_step), out_shape=t...  6.98 us

profile of v5, /device:TPU:1, one launch (start us, length us, event | category | flops | bytes accessed | tf_op | source)
XLA Modules:
  0.0 136.9 jit_solution(14156883294064496286)
XLA Ops:
  0.6 129.1 %step.1 = (bf16[800,256]{1,0:T(8,128)(2,1)}, f32[800,256]{1,0:T(8,128)}, bf16[2,2,2,112,128]{4,3,2,1,0:T(8,128)(2,1)}, bf16[2,2,2,112,256]{4,3,2,1,0:T(8,128)(2,...) custom-call(s32[2]{0:T(128)} %dilation.1, ...), custom_call_target="tpu_custom_call" | custom-call | tf_op jit(solution)/shard_map/step/pallas_call | solution.py:1098
  129.8 7.0 %finish.1 = (bf16[800,256]{1,0:T(8,128)(2,1)}, f32[800,256]{1,0:T(8,128)}, f32[2,200,400]{2,1,0:T(8,128)}, f32[100,3200]{1,0:T(8,128)}, f32[100,2,800]{2,1,0:T(2...) custom-call(bf16[800,256]{1,0:T(8,128)(2,1)} %get-tuple-element.42.r, ...), custom_call_target="tpu_custom_call" | custom-call | tf_op jit(solution)/shard_map/finish/pallas_call | solution.py:1209

commit v6 on v5

--- a/solution.py
+++ b/solution.py
@@ -189,7 +189,6 @@
         self.near_xy = (self.base + flip(flip(self.piece, 2), 4), self.own)
         self.column = [(at, other_owner(self.own, step)) for step in (1, 2, 3)]
         self.far = [(flip(at, bit), self.own) for bit in extra]
-        self.inner = (self.own == 1) | (self.own == 2)
         self.send, self.recv, self.used = send, recv, 0
         self.started = []
 
@@ -275,41 +274,20 @@
         super().__init__(place, view)
         self.ref, self.lanes = ref, lanes
 
-    def slot(self, step):
-        p = self.place
-        return self.ref.at[step, p.y, p.x, p.c, :, self.lanes]
-
     def cross(self):
         p = self.place
-        self.crossing = [p.start(self.slot(0), self.slot(step), p.column[step - 1]) for step in (1, 2)]
-        k = p.take(1)
-        self.direct = remote(self.slot(0), self.slot(3), p.send.at[k], p.recv.at[k], p.column[2])
-        relay = p.take(1)
-        self.relay = remote(self.slot(2), self.slot(3), p.send.at[relay], p.recv.at[k], p.column[0])
-
-        @pl.when(p.inner)
-        def _():
-            self.direct.start()
-
-    def first(self, followers=()):
-        p = self.place
-        self.crossing[1].wait_recv()
-
-        @pl.when(p.inner)
-        def _():
-            self.relay.start()
-
-        self.crossing[0].wait_recv()
-        self.direct.wait_recv()
-        for follower in followers:
+        index = (p.y, p.x, p.c, self.ALL, self.lanes)
+        mine = self.ref.at[(0,) + index]
+        self.crossing = [
+            p.start(mine, self.ref.at[(step,) + index], p.column[step - 1]) for step in (1, 2, 3)
+        ]
+
+    def first(self, follower=None):
+        for copy in self.crossing:
+            copy.wait_recv()
+        if follower is not None:
             follower.cross()
         super().first()
-
-    def finish(self):
-        @pl.when(self.place.inner)
-        def _():
-            self.direct.wait_send()
-            self.relay.wait_send()
 
 
 class Reduce:
@@ -381,39 +359,59 @@
 
 
 MATRICES = (
-    dict(kind="row", unit=OUT1, first=0, last=6, piece=6, lanes=(0, D), slot=0, scale=math.sqrt(D / H)),
-    dict(kind="row", unit=MID1, first=0, last=4, piece=2, lanes=(0, K_DEC * H), slot=0, scale=1.0),
-    dict(kind="in", unit=MID1, first=4, last=7, piece=4, lanes=(176, 976), slot=1, scale=1.0),
-    dict(kind="row", unit=OUT0, first=0, last=6, piece=3, lanes=(0, D), slot=0, scale=math.sqrt(D / H)),
-    dict(kind="row", unit=CONV0, first=0, last=7, piece=0, lanes=(0, SPLIT), slot=0, scale=1.0),
-    dict(kind="in", unit=IN0, first=0, last=6, piece=5, lanes=(0, D), slot=0, scale=1.0),
+    dict(
+        kind="row", unit=OUT1, first=0, last=6, piece=5, lanes=(0, D), slot=0, scale=math.sqrt(D / H),
+        owners=((0, 0, 2), (3, 2, 2)),
+    ),
+    dict(
+        kind="row", unit=MID1, first=0, last=4, piece=2, lanes=(0, K_DEC * H), slot=0, scale=1.0,
+        owners=((0, 0, 2), (3, 2, 2)),
+    ),
+    dict(
+        kind="in", unit=MID1, first=4, last=7, piece=4, lanes=(176, 976), slot=1, scale=1.0,
+        owners=((0, 0, 2), (3, 2, 2)),
+    ),
+    dict(
+        kind="row", unit=OUT0, first=0, last=6, piece=3, lanes=(0, D), slot=0, scale=math.sqrt(D / H),
+        owners=((1, 0, 2), (2, 2, 2)),
+    ),
+    dict(
+        kind="row", unit=CONV0, first=0, last=7, piece=0, lanes=(0, SPLIT), slot=0, scale=1.0,
+        owners=((1, 0, 2), (2, 2, 2)),
+    ),
+    dict(
+        kind="in", unit=IN0, first=0, last=6, piece=6, lanes=(0, D), slot=0, scale=1.0,
+        owners=((1, 0, 2), (2, 2, 2)),
+    ),
 )
-OWNED_AT = (1, 2)
 
 
 class Owner:
-    def __init__(self, place, matrix, half):
-        self.place, self.matrix, self.half = place, matrix, half
-        at = self.at = OWNED_AT[half]
+    def __init__(self, place, k, owner):
+        self.place, self.k = place, k
+        matrix = self.matrix = MATRICES[k]
+        at, self.first, self.shards = owner
+        self.at = at
         self.width = WIDTH[matrix["unit"]]
         self.count = OWNERS * (matrix["last"] - matrix["first"] + 1)
         p = place
         self.here = (p.piece == matrix["piece"]) & (p.own == at)
         self.away = (p.piece != matrix["piece"]) | (p.own != at)
         self.holds = (p.piece >= matrix["first"]) & (p.piece <= matrix["last"])
-        self.served = p.own // 2 == half
+        self.served = (p.own >= self.first) & (p.own < self.first + self.shards)
         self.device = (p.base + matrix["piece"], at)
     def each_served(self, act):
         def body(k, carry):
-            piece, own = self.matrix["first"] + k // 2, 2 * self.half + k % 2
+            piece = self.matrix["first"] + k // self.shards
+            own = self.first + k % self.shards
 
             @pl.when((piece != self.matrix["piece"]) | (own != self.at))
             def _():
-                act(k // 2, own, (self.place.base + piece, own))
+                act(k // self.shards, own, (self.place.base + piece, own))
 
             return carry
 
-        lax.fori_loop(0, self.count // 2, body, 0)
+        lax.fori_loop(0, self.count // OWNERS * self.shards, body, 0)
 
     def lanes(self, k):
         return pl.ds(pl.multiple_of(k * self.width, 128), self.width)
@@ -458,13 +456,14 @@
             remote(window.at[own, :, self.lanes(at)], slot, send.at[0], recv.at[k], device).start()
 
         self.each_served(act)
-        at = p.piece - self.matrix["first"]
-        pltpu.make_async_copy(window.at[p.own, :, self.lanes(at)], slot, send.at[0]).start()
+        if self.first <= self.at < self.first + self.shards:
+            at = p.piece - self.matrix["first"]
+            pltpu.make_async_copy(window.at[p.own, :, self.lanes(at)], slot, send.at[0]).start()
 
     def arrived(self, window, parts, send, recv, k):
         @pl.when(self.here)
         def _():
-            self.whole(window, pl.ds(2 * self.half, 2), send).wait()
+            self.whole(window, pl.ds(self.first, self.shards), send).wait()
 
         @pl.when(self.holds & self.served & self.away)
         def _():
@@ -510,9 +509,7 @@
 def orthogonalize(owners, window, gram, poly, halves):
     is_row = False
     high, factor, parts = jnp.int32(0), jnp.float32(0), jnp.int32(0)
-    half_at = owners[0].place.own // 2
-    two = pl.ds(2 * half_at, 2)
-    served = pl.ds(pl.multiple_of(2 * ROWS * half_at, 2 * ROWS), 2 * ROWS)
+    low_half, high_half = jnp.int32(0), jnp.int32(0)
     for owner in owners:
         matrix, here = owner.matrix, owner.here
         if matrix["kind"] == "row":
@@ -520,6 +517,8 @@
         high = jnp.where(here, matrix["lanes"][1], high)
         parts = jnp.where(here, -(-matrix["lanes"][1] // 512), parts)
         factor = jnp.where(here, MATRIX_RATE * matrix["scale"], factor)
+        low_half = jnp.where(here, owner.first // 2, low_half)
+        high_half = jnp.where(here, (owner.first + owner.shards) // 2, high_half)
     ins = {}
     for owner in owners:
         if owner.matrix["kind"] == "in":
@@ -572,20 +571,32 @@
         @pl.when(here)
         def _(at=at):
             window[:, :, :1024] = jnp.zeros((OWNERS, ROWS, 1024), BF16)
-            for h in range(2):
-                low = (at + H * h) // 128 * 128
-                step = dot_nt(halves[h, served], poly[...])
-                if (at + H * h) % 128:
-                    step = pltpu.roll(step, (at + H * h) % 128, 1)
-                lanes = slice(low, low + 512)
-                window[two, :, lanes] = add_low(window[two, :, lanes], step.reshape(2, ROWS, 512))
+
+            def body(two_at, carry):
+                two, served = pl.ds(2 * two_at, 2), pl.ds(pl.multiple_of(2 * ROWS * two_at, 2 * ROWS), 2 * ROWS)
+                for h in range(2):
+                    low = (at + H * h) // 128 * 128
+                    step = dot_nt(halves[h, served], poly[...])
+                    if (at + H * h) % 128:
+                        step = pltpu.roll(step, (at + H * h) % 128, 1)
+                    lanes = slice(low, low + 512)
+                    window[two, :, lanes] = add_low(window[two, :, lanes], step.reshape(2, ROWS, 512))
+                return carry
+
+            lax.fori_loop(low_half, high_half, body, 0)
 
     @pl.when(is_row)
     def _():
         def body(k, carry):
             lanes, values = part(k)
-            step = dot(poly[served, :GROUPED], values)
-            window[two, :, lanes] = step.astype(BF16).reshape(2, ROWS, 512)
+
+            def half(two_at, carry):
+                two, served = pl.ds(2 * two_at, 2), pl.ds(pl.multiple_of(2 * ROWS * two_at, 2 * ROWS), 2 * ROWS)
+                step = dot(poly[served, :GROUPED], values)
+                window[two, :, lanes] = step.astype(BF16).reshape(2, ROWS, 512)
+                return carry
+
+            lax.fori_loop(low_half, high_half, half, 0)
             return carry
 
         lax.fori_loop(0, parts, body, 0)
@@ -660,7 +671,7 @@
     ) = refs[72:]
     place = Place(send, recv, extra)
     own = place.own
-    owners = [Owner(place, matrix, half) for matrix in MATRICES for half in range(2)]
+    owners = [Owner(place, k, owner) for k, matrix in enumerate(MATRICES) for owner in matrix["owners"]]
     conv_in, spare = gram.at[:TOK], gram.at[TOK:]
     hid = spare
 
@@ -727,7 +738,8 @@
         [(K_ENC + K_DEC - 1 - j, K_ENC + K_DEC - 1 + j) for j in range(K_DEC)],
     )
 
-    in_unit.first([out_unit, mid_unit])
+    in_unit.first(out_unit)
+    conv_unit.first(mid_unit)
     row, col = iota((H, GROUPED), 0), iota((H, GROUPED), 1)
     used = jnp.zeros((H, GROUPED), jnp.int32)
     for s in range(OWNERS):
@@ -736,13 +748,16 @@
         used = used + jnp.where(inside, 1, 0)
     perm_h[...] = used.astype(F32).astype(BF16)
     in_unit.second()
-    conv_unit.first([last_unit])
+    out_unit.first(last_unit)
     fetches[5].wait()
     x_one[...] = tokens[...].astype(F32).T
+    conv_unit.second()
     in_unit.third()
-    conv_unit.second()
     fetches[6].wait()
     wide_grad[...] = cotangent[...].astype(F32).T
+    mid_unit.first()
+    out_unit.second()
+    conv_unit.third()
     in_unit.last()
 
     row_n, col_n = iota((128, H), 0), iota((128, H), 1)
@@ -819,9 +834,16 @@
         return (x_one[...] + dot(act_g[b, 1], weight_out(b))) + wide(b, 2)
 
     forward_in(0)
-    out_unit.first()
-    mid_unit.first()
-    conv_unit.third()
+    last_unit.first()
+    mid_unit.second()
+    out_unit.third()
+    conv_unit.last()
+    forward_conv(0)
+    last_unit.second()
+    mid_unit.third()
+    out_unit.last()
+    x_one[...] = forward_out(0)
+    last_unit.third()
 
     for fetch in moment_fetches:
         fetch.wait()
@@ -834,25 +856,12 @@
         lay_out(unit, *shard, put_moment)
         parts[unit][...] = jnp.zeros(parts[unit].shape, BF16)
 
-    out_unit.second()
-    mid_unit.second()
-    last_unit.first()
-    conv_unit.last()
-    forward_conv(0)
-    out_unit.third()
-    mid_unit.third()
-    last_unit.second()
-    out_unit.last()
-    x_one[...] = forward_out(0)
-    last_unit.third()
     mid_unit.last()
     forward_in(1)
     forward_conv(1)
     last_unit.last()
     out[...] = forward_out(1).T.astype(BF16)
     results[0].start()
-    for unit in (in_unit, conv_unit, out_unit, mid_unit, last_unit):
-        unit.finish()
     place.sent()
     gathers_used = place.used
 
@@ -968,14 +977,13 @@
     backward_out(0)
     backward_conv(0)
     reduces[CONV0].core()
-    reduces[OUT0].plane()
     to_owners(OUT1)
     backward_hidden(0)
     reduces[MID1].turn()
     reduces[CONV0].plane()
     backward_weight_in(0)
-    reduces[OUT0].turn()
     backward_in(0)
+    reduces[OUT0].plane()
     for m in range(12):
         vec_n[m : m + 1, :] = rows_n[m]
     for m in range(6):
@@ -987,18 +995,21 @@
         store(grads[IN0], IN0, VEC_AT, jnp.concatenate(three, axis=0).astype(BF16), lead=(s,))
     reduces[IN0].core()
     reduces[MID1].cross()
+    reduces[CONV0].turn()
+    reduces[IN0].plane()
     grad_tokens[...] = wide_grad[...].T
     results[1].start()
-    reduces[CONV0].turn()
-    reduces[IN0].plane()
+    to_owners(MID1)
+    reduces[CONV0].cross()
+    reduces[OUT0].turn()
+    reduces[IN0].turn()
+    to_owners(CONV0)
     reduces[OUT0].cross()
-    to_owners(MID1)
-    reduces[IN0].turn()
-    reduces[CONV0].cross()
+    reduces[IN0].cross()
     to_owners(OUT0)
-    reduces[IN0].cross()
-    to_owners(CONV0)
     to_owners(IN0)
+    for k, owner in enumerate(owners):
+        owner.gather_sent(moments[owner.matrix["unit"]], window, own_send, own_recv, k)
     reduces_used, place.used = place.used, 0
     for gather in spread_moments:
         gather.first()
@@ -1013,7 +1024,7 @@
 
         @pl.when(owner.here)
         def _(owner=owner, k=k):
-            owner.spread(window, parts[owner.matrix["unit"]], back_send, back_recv, k // 2)
+            owner.spread(window, parts[owner.matrix["unit"]], back_send, back_recv, owner.k)
 
     for gather in spread_moments:
         gather.second()
@@ -1022,7 +1033,7 @@
     def take_updates(unit):
         for k, owner in enumerate(owners):
             if owner.matrix["unit"] == unit:
-                owner.arrived(window, parts[unit], back_send, back_recv, k // 2)
+                owner.arrived(window, parts[unit], back_send, back_recv, owner.k)
         total = parts[unit][0]
         if unit == MID1:
             total = total + parts[unit][1]
@@ -1042,8 +1053,6 @@
         spread_updates[k].last()
         results[7 + unit].start()
     assert place.used <= gathers_used
-    for k, owner in enumerate(owners):
-        owner.gather_sent(moments[owner.matrix["unit"]], window, own_send, own_recv, k)
     place.sent()
     for copy in results:
         copy.wait()
@@ -1061,7 +1070,7 @@
 
     shared = [jax.ShapeDtypeStruct((2, 2, 2, ROWS, w), BF16) for w in WIDTH]
     results = [jax.ShapeDtypeStruct((D, TOK), BF16), jax.ShapeDtypeStruct((D, TOK), F32)] + shared + shared
-    count = 9 * len(WIDTH) + (10 + len(extra)) * len(WIDTH)
+    count = 8 * len(WIDTH) + (10 + len(extra)) * len(WIDTH)
     scratch = [vmem(a.shape, a.dtype) for a in results]
     scratch += [dma(count), dma(count), dma(2 * len(MATRICES)), dma(1), dma(1), dma(len(MATRICES)), dma(24)]
     scratch += [pieces(k, (OWNERS,)) for k in UNITS] * 2

time: 137 us -> 132 us (0.964)
  Pallas kernels: 136 us -> 131 us
    pallas_call x1, Pallas kernels: 129 us -> 124 us  [run_step(): pl.pallas_call(functools.partial(step_kernel, extra), out_shape=tuple(res...]
where the time goes in v6:
time: 132 us; the launch traced here: 131 us
  Pallas kernels  131 us (99%)
    pallas_call x1, Pallas kernels, run_step(): pl.pallas_call(functools.partial(step_kernel, extra), out_shape=tuple(res...  124 us
    pallas_call x1, Pallas kernels, finish(): pl.pallas_call(functools.partial(finish_kernel, vector_step), out_shape=t...  6.98 us

profile of v6, /device:TPU:1, one launch (start us, length us, event | category | flops | bytes accessed | tf_op | source)
XLA Modules:
  0.0 131.4 jit_solution(4314758282188872728)
XLA Ops:
  0.6 123.6 %step.1 = (bf16[800,256]{1,0:T(8,128)(2,1)}, f32[800,256]{1,0:T(8,128)}, bf16[2,2,2,112,128]{4,3,2,1,0:T(8,128)(2,1)}, bf16[2,2,2,112,256]{4,3,2,1,0:T(8,128)(2,...) custom-call(s32[2]{0:T(128)} %dilation.1, ...), custom_call_target="tpu_custom_call" | custom-call | tf_op jit(solution)/shard_map/step/pallas_call | solution.py:1107
  124.3 7.0 %finish.1 = (bf16[800,256]{1,0:T(8,128)(2,1)}, f32[800,256]{1,0:T(8,128)}, f32[2,200,400]{2,1,0:T(8,128)}, f32[100,3200]{1,0:T(8,128)}, f32[100,2,800]{2,1,0:T(2...) custom-call(bf16[800,256]{1,0:T(8,128)(2,1)} %get-tuple-element.42.r, ...), custom_call_target="tpu_custom_call" | custom-call | tf_op jit(solution)/shard_map/finish/pallas_call | solution.py:1218

commit v7 on v6

--- a/solution.py
+++ b/solution.py
@@ -602,7 +602,7 @@
         lax.fori_loop(0, parts, body, 0)
 
 
-def norm_forward(src, width, gain, shift, act, unit, slope, spread, chunk=128):
+def norm_forward(src, width, gain, shift, act, unit, slope, spread, chunk=256):
     def body(k, carry):
         rows = pl.ds(pl.multiple_of(k * chunk, chunk), chunk)
         x = src[rows, :width].astype(F32)
@@ -629,7 +629,7 @@
     return total
 
 
-def norm_backward(grad, width, gain, unit, slope, spread, finish, chunk=128):
+def norm_backward(grad, width, gain, unit, slope, spread, finish, chunk=256):
     def body(k, sums):
         rows = pl.ds(pl.multiple_of(k * chunk, chunk), chunk)
         da = grad[rows, :width] * slope[rows, :width].astype(F32)
@@ -738,6 +738,17 @@
         [(K_ENC + K_DEC - 1 - j, K_ENC + K_DEC - 1 + j) for j in range(K_DEC)],
     )
 
+    for fetch in moment_fetches:
+        fetch.wait()
+    for unit in UNITS:
+        moments[unit][...] = jnp.zeros(moments[unit].shape, BF16)
+
+        def put_moment(low, rows, values, add, unit=unit):
+            store(moments[unit], unit, low, (MOMENT_DECAY * values).astype(BF16), rows=rows, add=add)
+
+        lay_out(unit, *shard, put_moment)
+        parts[unit][...] = jnp.zeros(parts[unit].shape, BF16)
+
     in_unit.first(out_unit)
     conv_unit.first(mid_unit)
     row, col = iota((H, GROUPED), 0), iota((H, GROUPED), 1)
@@ -844,17 +855,6 @@
     out_unit.last()
     x_one[...] = forward_out(0)
     last_unit.third()
-
-    for fetch in moment_fetches:
-        fetch.wait()
-    for unit in UNITS:
-        moments[unit][...] = jnp.zeros(moments[unit].shape, BF16)
-
-        def put_moment(low, rows, values, add, unit=unit):
-            store(moments[unit], unit, low, (MOMENT_DECAY * values).astype(BF16), rows=rows, add=add)
-
-        lay_out(unit, *shard, put_moment)
-        parts[unit][...] = jnp.zeros(parts[unit].shape, BF16)
 
     mid_unit.last()
     forward_in(1)
@@ -977,7 +977,6 @@
     backward_out(0)
     backward_conv(0)
     reduces[CONV0].core()
-    to_owners(OUT1)
     backward_hidden(0)
     reduces[MID1].turn()
     reduces[CONV0].plane()
@@ -994,6 +993,7 @@
         three.append(jnp.zeros((ROWS - 48, 128), F32))
         store(grads[IN0], IN0, VEC_AT, jnp.concatenate(three, axis=0).astype(BF16), lead=(s,))
     reduces[IN0].core()
+    to_owners(OUT1)
     reduces[MID1].cross()
     reduces[CONV0].turn()
     reduces[IN0].plane()
@@ -1003,8 +1003,8 @@
     reduces[CONV0].cross()
     reduces[OUT0].turn()
     reduces[IN0].turn()
+    reduces[OUT0].cross()
     to_owners(CONV0)
-    reduces[OUT0].cross()
     reduces[IN0].cross()
     to_owners(OUT0)
     to_owners(IN0)

time: 132 us -> 130 us (0.985)
  Pallas kernels: 131 us -> 129 us
    pallas_call x1, Pallas kernels: 124 us -> 122 us  [run_step(): pl.pallas_call(functools.partial(step_kernel, extra), out_shape=tuple(res...]
where the time goes in v7:
time: 130 us
  Pallas kernels  129 us (99%)
    pallas_call x1, Pallas kernels, run_step(): pl.pallas_call(functools.partial(step_kernel, extra), out_shape=tuple(res...  122 us
    pallas_call x1, Pallas kernels, finish(): pl.pallas_call(functools.partial(finish_kernel, vector_step), out_shape=t...  6.98 us

profile of v7, /device:TPU:1, one launch (start us, length us, event | category | flops | bytes accessed | tf_op | source)
XLA Modules:
  0.0 129.6 jit_solution(15675510256070284206)
XLA Ops:
  0.6 121.8 %step.1 = (bf16[800,256]{1,0:T(8,128)(2,1)}, f32[800,256]{1,0:T(8,128)}, bf16[2,2,2,112,128]{4,3,2,1,0:T(8,128)(2,1)}, bf16[2,2,2,112,256]{4,3,2,1,0:T(8,128)(2,...) custom-call(s32[2]{0:T(128)} %dilation.1, ...), custom_call_target="tpu_custom_call" | custom-call | tf_op jit(solution)/shard_map/step/pallas_call | solution.py:1107
  122.5 7.0 %finish.1 = (bf16[800,256]{1,0:T(8,128)(2,1)}, f32[800,256]{1,0:T(8,128)}, f32[2,200,400]{2,1,0:T(8,128)}, f32[100,3200]{1,0:T(8,128)}, f32[100,2,800]{2,1,0:T(2...) custom-call(bf16[800,256]{1,0:T(8,128)(2,1)} %get-tuple-element.42.r, ...), custom_call_target="tpu_custom_call" | custom-call | tf_op jit(solution)/shard_map/finish/pallas_call | solution.py:1218

commit v8 on v7

--- a/solution.py
+++ b/solution.py
@@ -496,7 +496,7 @@
     current = gram * inverse * inverse
     result = None
     for step in range(NS_STEPS):
-        square = dot_fine if step > 2 else dot_low
+        square = dot_fine if step == 3 else dot_low
         poly = COEF_A * unit + COEF_B * current + COEF_C * square(current, current)
         result = poly if result is None else dot_low(poly, result)
         if step < NS_STEPS - 1:

time: 130 us -> 129 us (level)
  no operation moved by 1% of the time
where the time goes in v8:
time: 129 us
  Pallas kernels  128 us (99%)
    pallas_call x1, Pallas kernels, run_step(): pl.pallas_call(functools.partial(step_kernel, extra), out_shape=tuple(res...  121 us
    pallas_call x1, Pallas kernels, finish(): pl.pallas_call(functools.partial(finish_kernel, vector_step), out_shape=t...  6.98 us

profile of v8, /device:TPU:1, one launch (start us, length us, event | category | flops | bytes accessed | tf_op | source)
XLA Modules:
  0.0 129.1 jit_solution(8702623071342573295)
XLA Ops:
  0.6 121.3 %step.1 = (bf16[800,256]{1,0:T(8,128)(2,1)}, f32[800,256]{1,0:T(8,128)}, bf16[2,2,2,112,128]{4,3,2,1,0:T(8,128)(2,1)}, bf16[2,2,2,112,256]{4,3,2,1,0:T(8,128)(2,...) custom-call(s32[2]{0:T(128)} %dilation.1, ...), custom_call_target="tpu_custom_call" | custom-call | tf_op jit(solution)/shard_map/step/pallas_call | solution.py:1107
  121.9 7.0 %finish.1 = (bf16[800,256]{1,0:T(8,128)(2,1)}, f32[800,256]{1,0:T(8,128)}, f32[2,200,400]{2,1,0:T(8,128)}, f32[100,3200]{1,0:T(8,128)}, f32[100,2,800]{2,1,0:T(2...) custom-call(bf16[800,256]{1,0:T(8,128)(2,1)} %get-tuple-element.42.r, ...), custom_call_target="tpu_custom_call" | custom-call | tf_op jit(solution)/shard_map/finish/pallas_call | solution.py:1218
